TPU v7x, 128 devices: a whole 4x4x4 slice. The times are simulated.
128 devices in a mesh: batch: 32 (over y, x, core), chan: 4 (over z).
Axes of the slice: x: 4, y: 4, z: 4, core: 2. Of those that a mesh axis runs over, the one named last changes fastest.
Arguments:
- features: bfloat16 [4, 10436608], P('chan', 'batch'), may hold values from -6 to 6
- lengths: int32 [256], P('batch'), may hold values from 1 to 4, as said below
- labels: int32 [256, 4], P('batch'), may hold values from 0 to 399
- direct: float32 [4, 79872], P('chan'), may hold values from -0.21875 to 0.21875
- squeeze: float32 [4, 39936], P('chan'), may hold values from -0.21875 to 0.21875
- spatial: float32 [4, 497664], P('chan'), may hold values from -0.078125 to 0.078125
- shrink: float32 [4, 9984], P('chan'), may hold values from -0.21875 to 0.21875
- volume: float32 [4, 41472], P('chan'), may hold values from -0.15625 to 0.15625
- pooled: float32 [4, 26624], P('chan'), may hold values from -0.21875 to 0.21875
- readout: float32 [4, 102400], P('chan'), may hold values from -0.9 to 0.9
- affine: float32 [2, 1264], P(None, 'chan'), may hold values from 0.5 to 1.5
- first_direct: float32 [4, 79872], P('chan'), may hold values from -0.013671875 to 0.013671875
- first_squeeze: float32 [4, 39936], P('chan'), may hold values from -0.013671875 to 0.013671875
- first_spatial: float32 [4, 497664], P('chan'), may hold values from -0.0546875 to 0.0546875
- first_shrink: float32 [4, 9984], P('chan'), may hold values from -0.013671875 to 0.013671875
- first_volume: float32 [4, 41472], P('chan'), may hold values from -0.0546875 to 0.0546875
- first_pooled: float32 [4, 26624], P('chan'), may hold values from -0.0546875 to 0.0546875
- first_readout: float32 [4, 102400], P('chan'), may hold values from -0.0546875 to 0.0546875
- first_affine: float32 [2, 1264], P(None, 'chan'), may hold values from -0.0546875 to 0.0546875
- second_direct: float32 [4, 79872], P('chan'), may hold values from 1.9929846e-06 to 7.971938e-06
- second_squeeze: float32 [4, 39936], P('chan'), may hold values from 1.9929846e-06 to 7.971938e-06
- second_spatial: float32 [4, 497664], P('chan'), may hold values from 7.9719386e-05 to 0.00031887754
- second_shrink: float32 [4, 9984], P('chan'), may hold values from 1.9929846e-06 to 7.971938e-06
- second_volume: float32 [4, 41472], P('chan'), may hold values from 7.9719386e-05 to 0.00031887754
- second_pooled: float32 [4, 26624], P('chan'), may hold values from 7.9719386e-05 to 0.00031887754
- second_readout: float32 [4, 102400], P('chan'), may hold values from 7.9719386e-05 to 0.00031887754
- second_affine: float32 [2, 1264], P(None, 'chan'), may hold values from 7.9719386e-05 to 0.00031887754
- running: float32 [2, 1264], P(None, 'chan'), may hold values from 0.002 to 0.02
Outputs:
- moment_direct: float32 [4, 79872], P('chan')
- moment_squeeze: float32 [4, 39936], P('chan')
- moment_spatial: float32 [4, 497664], P('chan')
- moment_shrink: float32 [4, 9984], P('chan')
- moment_volume: float32 [4, 41472], P('chan')
- moment_pooled: float32 [4, 26624], P('chan')
- moment_readout: float32 [4, 102400], P('chan')
- moment_affine: float32 [2, 1264], P(None, 'chan')
- square_direct: float32 [4, 79872], P('chan')
- square_squeeze: float32 [4, 39936], P('chan')
- square_spatial: float32 [4, 497664], P('chan')
- square_shrink: float32 [4, 9984], P('chan')
- square_volume: float32 [4, 41472], P('chan')
- square_pooled: float32 [4, 26624], P('chan')
- square_readout: float32 [4, 102400], P('chan')
- square_affine: float32 [2, 1264], P(None, 'chan')
- master_direct: float32 [4, 79872], P('chan')
- master_squeeze: float32 [4, 39936], P('chan')
- master_spatial: float32 [4, 497664], P('chan')
- master_shrink: float32 [4, 9984], P('chan')
- master_volume: float32 [4, 41472], P('chan')
- master_pooled: float32 [4, 26624], P('chan')
- master_readout: float32 [4, 102400], P('chan')
- master_affine: float32 [2, 1264], P(None, 'chan')
- running_next: float32 [2, 1264], P(None, 'chan')
- loss_sum: float32 [], replicated
- counted: float32 [], replicated
- copies: bfloat16 [4, 797952], P('chan')
Inputs may be any that keep to these rules, and one draw needn't show every extreme that they name: Clip c has lengths[c] valid time steps, the first ones of its 4; some clip has 4.
All inputs are finite; a program needn't handle non-finite values.
Results may differ from a plain program's by a relative error of at most 0.0039.
Values may be sent and summed in bfloat16 or wider, within the bound.
A program may use at most 320 MiB of HBM per device.

v0:
```python
import math

import jax
import jax.numpy as jnp
from jax import lax
from jax.sharding import PartitionSpec as P

CIN = 832
B0 = 384
R1 = 192
O1 = 384
R2 = 48
O2 = 128
B3 = 128
CLASSES = 400
SIDE = 7
STEP = 5


EPS = 1e-05
BETA_ONE = 0.5
BETA_TWO = 0.5
DECAY = 0.01
MOMENTUM = 0.99


def shifted_views(field):
    padded = jnp.pad(field, ((0, 0), (1, 1), (1, 1), (1, 1), (0, 0)))
    frames, height, across = (field.shape[1], field.shape[2], field.shape[3])
    return [
        padded[
            :, shift_t : shift_t + frames, shift_h : shift_h + height, shift_w : shift_w + across, :
        ]
        for shift_t in range(3)
        for shift_h in range(3)
        for shift_w in range(3)
    ]


def patches(field):
    return jnp.concatenate(shifted_views(field), axis=-1)


def box_sum(field):
    return sum(shifted_views(field))


def patches_back(grad_patch, target_shape):
    unused, pullback = jax.vjp(patches, jnp.zeros(target_shape, jnp.float32))
    return pullback(grad_patch)[0]


def step_rates():
    return [
        1.5 / math.sqrt(CIN),
        1.5 / math.sqrt(CIN),
        1.5 / math.sqrt(27 * R1),
        1.5 / math.sqrt(CIN),
        1.5 / math.sqrt(27 * R2),
        1.5 / math.sqrt(CIN),
        0.2,
        0.3,
    ]


def split_columns(packed, widths):
    pieces = []
    offset = 0
    for channels in widths:
        pieces.append(packed[..., offset : offset + channels])
        offset = offset + channels
    return pieces


def local_dot(inputs, weight):
    return jnp.dot(inputs, weight, preferred_element_type=jnp.float32)


def weight_grad(inputs, grads_out):
    flat_in = inputs.reshape(-1, inputs.shape[-1])
    flat_grad = grads_out.reshape(-1, grads_out.shape[-1])
    return lax.dot_general(
        flat_in, flat_grad, (((0,), (0,)), ((), ())), preferred_element_type=jnp.float32
    )


def column_sums(values, voxel_mask):
    return jnp.stack(
        [
            jnp.sum(values * voxel_mask, axis=(0, 1, 2, 3)),
            jnp.sum(values * values * voxel_mask, axis=(0, 1, 2, 3)),
        ]
    )


def apply_norm(conv_out, totals, voxels, params, voxel_mask):
    average = totals[0] / voxels
    variance = totals[1] / voxels - average * average
    inverse = lax.rsqrt(variance + EPS)
    normed = (conv_out - average) * inverse
    before = params[0] * normed + params[1]
    return (voxel_mask * jax.nn.silu(before), (normed, before, inverse), (average, variance))


def norm_back(grad_out, stored, voxel_mask):
    normed, before, inverse = stored
    sigmoid = jax.nn.sigmoid(before)
    grad_before = grad_out * voxel_mask * sigmoid * (1.0 + before * (1.0 - sigmoid))
    return (
        grad_before,
        jnp.stack(
            [
                jnp.sum(grad_before * normed, axis=(0, 1, 2, 3)),
                jnp.sum(grad_before, axis=(0, 1, 2, 3)),
            ]
        ),
    )


def norm_finish(grad_before, stored, params, totals, voxels, voxel_mask):
    normed, before, inverse = stored
    return (
        voxel_mask
        * params[0]
        * inverse
        * (grad_before - totals[1] / voxels - normed * totals[0] / voxels)
    ).astype(jnp.bfloat16)


def adamw(weight, moment_one, moment_two, gradient, step_rate):
    first_new = BETA_ONE * moment_one + (1.0 - BETA_ONE) * gradient
    second_new = BETA_TWO * moment_two + (1.0 - BETA_TWO) * gradient * gradient
    first_hat = first_new / (1.0 - BETA_ONE**STEP)
    second_hat = second_new / (1.0 - BETA_TWO**STEP)
    weight_new = weight - step_rate * (first_hat / (jnp.sqrt(second_hat) + 1e-08) + DECAY * weight)
    return (first_new, second_new, weight_new)


def per_device(
    features,
    lengths,
    labels,
    direct,
    squeeze,
    spatial,
    shrink,
    volume,
    pooled,
    readout,
    affine,
    first_direct,
    first_squeeze,
    first_spatial,
    first_shrink,
    first_volume,
    first_pooled,
    first_readout,
    first_affine,
    second_direct,
    second_squeeze,
    second_spatial,
    second_shrink,
    second_volume,
    second_pooled,
    second_readout,
    second_affine,
    running,
):
    chan_count = lax.axis_size("chan")
    masters = [direct, squeeze, spatial, shrink, volume, pooled, readout, affine]
    shaped = [
        direct.reshape(CIN, -1),
        squeeze.reshape(CIN, -1),
        spatial.reshape(27 * R1, -1),
        shrink.reshape(CIN, -1),
        volume.reshape(27 * R2, -1),
        pooled.reshape(CIN, -1),
        readout.reshape(-1, CLASSES),
    ]
    firsts = [
        first_direct,
        first_squeeze,
        first_spatial,
        first_shrink,
        first_volume,
        first_pooled,
        first_readout,
        first_affine,
    ]
    seconds = [
        second_direct,
        second_squeeze,
        second_spatial,
        second_shrink,
        second_volume,
        second_pooled,
        second_readout,
        second_affine,
    ]
    frames = labels.shape[1]
    local_field = features.reshape(lengths.shape[0], frames, SIDE, SIDE, -1)
    step_mask = (jnp.arange(frames)[None, :] < lengths[:, None]).astype(jnp.float32)
    voxel_mask = jnp.broadcast_to(step_mask[:, :, None, None, None], local_field.shape[:4] + (1,))
    onehot = (labels[:, :, None] == jnp.arange(CLASSES)[None, None, :]).astype(jnp.float32)
    widths = [
        B0 // chan_count,
        R1 // chan_count,
        R2 // chan_count,
        B3 // chan_count,
        O1 // chan_count,
        O2 // chan_count,
    ]
    norm_params = split_columns(affine, widths)
    lowered = [weight.astype(jnp.bfloat16) for weight in shaped]
    complete = lax.all_gather(local_field, "chan", axis=4, tiled=True)
    window = (
        box_sum(complete.astype(jnp.float32) * voxel_mask) / jnp.maximum(box_sum(voxel_mask), 1.0)
    ).astype(jnp.bfloat16)
    first_outs = [
        local_dot(complete, lowered[0]),
        local_dot(complete, lowered[1]),
        local_dot(complete, lowered[3]),
        local_dot(window, lowered[5]),
    ]
    local_stats = jnp.concatenate(
        [column_sums(values, voxel_mask) for values in first_outs], axis=1
    )
    stats_a, counted = lax.psum((local_stats, jnp.sum(step_mask)), "batch")
    plane_size = complete.shape[2] * complete.shape[3]
    voxels = counted * plane_size
    pieces_a = split_columns(stats_a, widths[:4])
    results = [
        apply_norm(first_outs[member], pieces_a[member], voxels, norm_params[member], voxel_mask)
        for member in range(4)
    ]
    gathered = (
        lax.all_gather(results[1][0].astype(jnp.bfloat16), "chan", axis=4, tiled=True),
        lax.all_gather(results[2][0].astype(jnp.bfloat16), "chan", axis=4, tiled=True),
    )
    patch_one = patches(gathered[0])
    patch_two = patches(gathered[1])
    second_outs = [local_dot(patch_one, lowered[2]), local_dot(patch_two, lowered[4])]
    stats_b = lax.psum(
        jnp.concatenate([column_sums(values, voxel_mask) for values in second_outs], axis=1),
        "batch",
    )
    pieces_b = split_columns(stats_b, widths[4:])
    results = results + [
        apply_norm(
            second_outs[member], pieces_b[member], voxels, norm_params[4 + member], voxel_mask
        )
        for member in range(2)
    ]
    head_order = [0, 4, 5, 3]
    feature = jnp.concatenate(
        [jnp.mean(results[member][0], axis=(2, 3)) for member in head_order], axis=-1
    ).astype(jnp.bfloat16)
    logits = lax.psum(local_dot(feature, lowered[6]), "chan")
    logprob = jax.nn.log_softmax(logits, axis=-1)
    loss_local = -jnp.sum(step_mask[:, :, None] * onehot * logprob)
    grad_logits = ((jnp.exp(logprob) - onehot) * step_mask[:, :, None] / counted).astype(
        jnp.bfloat16
    )
    grad_readout = weight_grad(feature, grad_logits)
    grad_feature = lax.dot_general(
        grad_logits, lowered[6], (((2,), (1,)), ((), ())), preferred_element_type=jnp.float32
    )
    grad_heads = split_columns(grad_feature, [widths[member] for member in head_order])
    back_a = []
    for position, member in enumerate(head_order):
        grad_out = jnp.broadcast_to(
            grad_heads[position][:, :, None, None, :] / plane_size, results[member][0].shape
        )
        back_a.append(norm_back(grad_out, results[member][1], voxel_mask))
    sums_a, loss_total = lax.psum(
        (jnp.concatenate([record[1] for record in back_a], axis=1), loss_local), "batch"
    )
    norm_grads = {}
    conv_grads = {}
    pieces = split_columns(sums_a, [widths[member] for member in head_order])
    for position, member in enumerate(head_order):
        norm_grads[member] = pieces[position]
        conv_grads[member] = norm_finish(
            back_a[position][0],
            results[member][1],
            norm_params[member],
            pieces[position],
            voxels,
            voxel_mask,
        )
    grad_direct = weight_grad(complete, conv_grads[0])
    grad_pooled = weight_grad(window, conv_grads[3])
    grad_spatial = weight_grad(patch_one, conv_grads[4])
    grad_volume = weight_grad(patch_two, conv_grads[5])
    grad_patch_one = lax.dot_general(
        conv_grads[4], lowered[2], (((4,), (1,)), ((), ())), preferred_element_type=jnp.float32
    )
    grad_patch_two = lax.dot_general(
        conv_grads[5], lowered[4], (((4,), (1,)), ((), ())), preferred_element_type=jnp.float32
    )
    grad_reduced = (
        lax.psum_scatter(
            patches_back(grad_patch_one, gathered[0].shape), "chan", scatter_dimension=4, tiled=True
        ),
        lax.psum_scatter(
            patches_back(grad_patch_two, gathered[1].shape), "chan", scatter_dimension=4, tiled=True
        ),
    )
    back_b = [
        norm_back(grad_reduced[position], results[1 + position][1], voxel_mask)
        for position in range(2)
    ]
    sums_b = lax.psum(jnp.concatenate([record[1] for record in back_b], axis=1), "batch")
    pieces_c = split_columns(sums_b, widths[1:3])
    norm_grads[1] = pieces_c[0]
    norm_grads[2] = pieces_c[1]
    grad_squeeze = weight_grad(
        complete,
        norm_finish(back_b[0][0], results[1][1], norm_params[1], pieces_c[0], voxels, voxel_mask),
    )
    grad_shrink = weight_grad(
        complete,
        norm_finish(back_b[1][0], results[2][1], norm_params[2], pieces_c[1], voxels, voxel_mask),
    )
    affine_grad = jnp.concatenate([norm_grads[member] for member in range(6)], axis=1)
    rates = step_rates()
    local_grads = [
        grad_direct,
        grad_squeeze,
        grad_spatial,
        grad_shrink,
        grad_volume,
        grad_pooled,
        grad_readout,
    ]
    summed = lax.psum(tuple(local_grads), "batch")
    reduced_grads = list(summed)
    reduced_grads = [gradient.reshape(1, -1) for gradient in reduced_grads]
    reduced_grads.append(affine_grad)
    updated = [
        adamw(
            masters[member], firsts[member], seconds[member], reduced_grads[member], rates[member]
        )
        for member in range(8)
    ]
    fresh = jnp.concatenate(
        [
            jnp.stack([results[member][2][0], results[member][2][1] * voxels / (voxels - 1.0)])
            for member in range(6)
        ],
        axis=1,
    )
    running_next = MOMENTUM * running + (1.0 - MOMENTUM) * fresh
    copies = jnp.concatenate([updated[member][2] for member in range(7)], axis=1).astype(
        jnp.bfloat16
    )
    return (
        updated[0][0],
        updated[1][0],
        updated[2][0],
        updated[3][0],
        updated[4][0],
        updated[5][0],
        updated[6][0],
        updated[7][0],
        updated[0][1],
        updated[1][1],
        updated[2][1],
        updated[3][1],
        updated[4][1],
        updated[5][1],
        updated[6][1],
        updated[7][1],
        updated[0][2],
        updated[1][2],
        updated[2][2],
        updated[3][2],
        updated[4][2],
        updated[5][2],
        updated[6][2],
        updated[7][2],
        running_next,
        loss_total,
        counted,
        copies,
    )


def solution(mesh):
    placed = (
        P("chan", "batch"),
        P("batch"),
        P("batch", None),
        P("chan", None),
        P("chan", None),
        P("chan", None),
        P("chan", None),
        P("chan", None),
        P("chan", None),
        P("chan", None),
        P(None, "chan"),
        P("chan", None),
        P("chan", None),
        P("chan", None),
        P("chan", None),
        P("chan", None),
        P("chan", None),
        P("chan", None),
        P(None, "chan"),
        P("chan", None),
        P("chan", None),
        P("chan", None),
        P("chan", None),
        P("chan", None),
        P("chan", None),
        P("chan", None),
        P(None, "chan"),
        P(None, "chan"),
    )
    return jax.shard_map(
        per_device,
        mesh=mesh,
        in_specs=placed,
        out_specs=(
            P("chan", None),
            P("chan", None),
            P("chan", None),
            P("chan", None),
            P("chan", None),
            P("chan", None),
            P("chan", None),
            P(None, "chan"),
            P("chan", None),
            P("chan", None),
            P("chan", None),
            P("chan", None),
            P("chan", None),
            P("chan", None),
            P("chan", None),
            P(None, "chan"),
            P("chan", None),
            P("chan", None),
            P("chan", None),
            P("chan", None),
            P("chan", None),
            P("chan", None),
            P("chan", None),
            P(None, "chan"),
            P(None, "chan"),
            P(),
            P(),
            P("chan", None),
        ),
        check_vma=False,
    )
```

profile of v0, /device:TPU:0, one launch (start us, length us, event | category | flops | bytes accessed | tf_op | source)
XLA Modules:
  0.0 1315.7 jit_solution(11876085127823185702)
XLA Ops:
  7.2 14.6 %reduce = bf16[326144]{0:T(1024)(128)(2,1)S(1)} reduce(bf16[1,326144]{1,0:T(2,128)(2,1)} %param.28, bf16[]{:T(256)} %constant.268), dimensions={0}, to_apply=%param.28.reduce_sub_computation | reduce | bytes 1304578 | tf_op args[0]
  23.2 10.0 copy.116
  41.8 20.9 %convert_reduce_fusion = bf16[497664]{0:T(1024)(128)(2,1)S(1)} fusion(f32[1,497664]{1,0:T(1,128)S(1)} %copy-done.5), kind=kLoop, calls=%fused_computation.144 | loop fusion | flops 497664 | bytes 2985984 | tf_op jit(solution)/shard_map/convert_element_type | solution.py:214
  62.7 1.8 convert_element_type.118
  69.0 329.1 %all-gather.2.cloned.1.call-done = bf16[8,4,7,7,832]{0,1,3,2,4:T(4,128)(2,1)} async-done(((bf16[8,4,7,7,208]{0,1,3,2,4:T(4,128)(2,1)}), bf16[8,4,7,7,832]{0,1,3,2,4:T(4,128)(2,1)}) %all-gather.2.cloned.1.call-update) | async-done | bytes 2609168 | tf_op jit(solution)/shard_map/all_gather | solution.py:215
  398.1 63.3 %copy.117 = bf16[8,4,7,7,832]{4,0,3,2,1:T(8,128)(2,1)S(1)} copy(bf16[8,4,7,7,832]{0,1,3,2,4:T(4,128)(2,1)} %all-gather.2.cloned.1.call-done) | data formatting | bytes 5218304 | tf_op jit(solution)/shard_map/all_gather | solution.py:215
  461.9 1.9 multiply_reduce_fusion.17
  463.7 1.9 multiply_reduce_fusion.19
  465.7 1.8 multiply_reduce_fusion.21
  467.5 10.4 fusion.29
  477.9 1.5 copy-done.4
  481.2 67.6 %all-reduce.60 = (f32[]{:T(128)}, f32[2,188]{1,0:T(2,128)S(1)}) all-reduce(f32[]{:T(128)} %fusion.137, f32[2,188]{1,0:T(2,128)S(1)} %maximum_maximum_fusion), channel_id=1, replica_groups=mesh['batch'=32,'chan'=4] {'batch'}, use_global_device_ids=true, to_apply=%region_10.11 | all-reduce | flops 377 | bytes 3016 | tf_op jit(solution)/shard_map/psum | solution.py:228
  551.8 2.6 copy.129
  554.4 20.6 %all_gather.11 = bf16[8,4,7,7,48]{0,1,3,2,4:T(4,128)(2,1)S(1)} all-gather(bf16[8,4,7,7,12]{0,1,3,2,4:T(4,128)(2,1)} %copy.129), channel_id=1, replica_groups=mesh['batch'=32,'chan'=4] {'chan'}, dimensions={4}, use_global_device_ids=true | all-gather | bytes 188160 | tf_op jit(solution)/shard_map/all_gather | solution.py:238
  575.0 3.2 copy.130
  578.1 3.6 pad_slice_fusion.53
  581.7 3.4 pad_slice_fusion.52
  586.8 3.5 copy.125
  590.3 76.0 %all_gather.10 = bf16[8,4,7,7,192]{0,1,3,2,4:T(4,128)(2,1)} all-gather(bf16[8,4,7,7,48]{0,1,3,2,4:T(4,128)(2,1)S(1)} %copy.125), channel_id=1, replica_groups=mesh['batch'=32,'chan'=4] {'chan'}, dimensions={4}, use_global_device_ids=true | all-gather | bytes 752640 | tf_op jit(solution)/shard_map/all_gather | solution.py:237
  666.4 15.3 %copy.126 = bf16[8,4,7,7,192]{4,0,3,2,1:T(8,128)(2,1)S(1)} copy(bf16[8,4,7,7,192]{0,1,3,2,4:T(4,128)(2,1)} %all_gather.10) | data formatting | bytes 1204224 | tf_op jit(solution)/shard_map/all_gather | solution.py:237
  681.6 2.6 pad_slice_fusion.27
  684.3 5.6 pad_slice_fusion.26
  690.5 12.4 concatenate.43
  702.9 4.2 multiply_reduce_fusion.10
  707.1 28.3 %concatenate.42 = bf16[8,4,7,7,5184]{4,0,3,2,1:T(8,128)(2,1)} concatenate(bf16[8,4,7,7,192]{4,0,3,2,1:T(8,128)(2,1)} %get-tuple-element.199, bf16[8,4,7,7,192]{4,0,3,2,1:T(8,128)(2,1)} %get-tuple-element.175, bf16[8,4,7,7,192]{4,0,3,2,1:T(8,128)(2,1)} %get-tuple-element.176, bf16[8,4,7,7,192]{4,0,3,2,1:T(8,128)(2,1)} %get-tuple-element.177, ...), dimensions={4} | concatenate | bytes 32514048 | tf_op jit(solution)/shard_map/concatenate | solution.py:41
  735.4 9.3 multiply_reduce_fusion.12
  746.1 67.8 %psum.100 = f32[2,128]{1,0:T(2,128)S(1)} all-reduce(f32[2,128]{1,0:T(2,128)} %maximum_maximum_fusion.2), channel_id=1, replica_groups=mesh['batch'=32,'chan'=4] {'batch'}, use_global_device_ids=true, to_apply=%region_16.17 | all-reduce | flops 256 | bytes 2048 | tf_op jit(solution)/shard_map/psum | solution.py:243
  822.8 17.8 %psum.101 = f32[8,4,400]{2,0,1:T(8,128)} all-reduce(f32[8,4,400]{2,0,1:T(8,128)} %fusion.76), channel_id=1, replica_groups=mesh['batch'=32,'chan'=4] {'chan'}, use_global_device_ids=true, to_apply=%region_20.21 | all-reduce | flops 12800 | bytes 102400 | tf_op jit(solution)/shard_map/psum | solution.py:258
  841.6 1.7 multiply_reduce_fusion.22
  843.3 1.8 fusion.74
  845.3 1.7 multiply_reduce_fusion.3
  847.0 1.7 multiply_reduce_fusion.5
  848.8 62.7 %psum.102 = f32[2,256]{1,0:T(2,128)S(1)} all-reduce(f32[2,256]{1,0:T(2,128)S(1)} %maximum_maximum_fusion.1), channel_id=1, replica_groups=mesh['batch'=32,'chan'=4] {'batch'}, use_global_device_ids=true, to_apply=%region_31.32 | all-reduce | flops 512 | bytes 4096 | tf_op jit(solution)/shard_map/psum | solution.py:275
  912.7 2.2 fusion.69
  915.0 4.2 fusion.154
  919.1 7.3 fusion.153
  926.5 12.7 convolution_bitcast_fusion
  939.1 13.3 %fusion.31 = f32[8,4,7,7,5184]{4,0,3,2,1:T(8,128)} fusion(bf16[5184,96]{1,0:T(8,128)(2,1)S(1)} %copy-done.12, f32[8,4,7,7,96]{4,0,3,2,1:T(8,128)S(1)} %get-tuple-element.259, f32[96]{0:T(128)S(1)} %get-tuple-element.247, f32[96]{0:T(128)S(1)} %get-tuple-element.246, f32[]{:T(128)S(6)} %mul.918, f32[96]{0:T(128)S(1)} %copy-done.95, f32[96]{0:T(128)S(1)} %bitcast.216, ...), kind=kOutput, calls=%fused_computation.151 | convolution fusion | flops 1563835392 | bytes 34126212 | tf_op jit(solution)/shard_map/dot_general | solution.py:295
  952.4 11.6 fusion.152
  964.2 23.7 %fusion.151 = (f32[8,4,7,7,192]{4,0,3,2,1:T(8,128)}, f32[8,4,7,7,192]{4,0,3,2,1:T(8,128)S(1)}, f32[8,4,7,7,192]{4,0,3,2,1:T(8,128)}, f32[8,4,7,7,192]{4,0,3,2,1:...) fusion(f32[8,4,7,7,5184]{4,0,3,2,1:T(8,128)} %fusion.31), kind=kLoop, calls=%fused_computation.434 | loop fusion | bytes 45760512 | tf_op jit(solution)/shard_map/transpose(jvp())/split | solution.py:41
  989.2 4.5 pad_add_fusion.1
  995.0 14.2 %pad_add_fusion = f32[8,6,9,9,192]{4,0,3,2,1:T(8,128)} fusion(f32[8,4,7,7,192]{4,0,3,2,1:T(8,128)} %get-tuple-element.127, f32[8,4,7,7,192]{4,0,3,2,1:T(8,128)} %get-tuple-element.128, f32[8,4,7,7,192]{4,0,3,2,1:T(8,128)} %get-tuple-element.129, f32[8,4,7,7,192]{4,0,3,2,1:T(8,128)} %get-tuple-element.130, f32[8,4,7,7,192]{4,0,3,2,1:T(8,128)} %get-tuple-element.131, ...), kind=kLoop, calls=%fused_computation.136 | loop fusion | flops 14929920 | bytes 28274688 | tf_op jit(solution)/shard_map/transpose(jvp())/add_any | solution.py:31
  1009.1 3.6 pad_add_fusion.2
  1012.7 13.2 %copy.178 = f32[8,4,7,7,192]{0,3,2,1,4:T(8,128)} copy(f32[8,4,7,7,192]{4,0,3,2,1:T(8,128)S(1)} %pad_add_fusion.2) | data formatting | bytes 2408448
  1025.9 13.4 %reshape.652 = f32[192,1568]{1,0:T(8,128)} reshape(f32[192,4,7,7,8]{4,3,2,1,0:T(8,128)} %bitcast.211) | data formatting | bytes 2408448
  1039.6 5.3 convolution_bitcast_fusion.1
  1046.4 4.1 reshape.630
  1051.6 3.6 convolution_bitcast_fusion.3
  1056.2 2.8 convolution_bitcast_fusion.4
  1062.4 1.5 reshape.634
  1064.0 2.8 multiply_reduce_fusion
  1066.8 5.0 reshape.653
  1071.8 5.6 copy.179
  1077.4 2.8 multiply_reduce_fusion.1
  1080.2 62.7 %psum.104 = f32[2,60]{1,0:T(2,128)S(1)} all-reduce(f32[2,60]{1,0:T(2,128)S(1)} %maximum_maximum_fusion.3), channel_id=1, replica_groups=mesh['batch'=32,'chan'=4] {'batch'}, use_global_device_ids=true, to_apply=%region_39.40 | all-reduce | flops 120 | bytes 960 | tf_op jit(solution)/shard_map/psum | solution.py:313
  1142.9 2.0 convolution_bitcast_fusion.5
  1147.3 2.0 convolution_bitcast_fusion.6
  1149.9 124.7 %all-reduce.59 = (f32[1,9984]{1,0:T(1,128)S(1)}, f32[]{:T(128)}) all-reduce(f32[1,9984]{1,0:T(1,128)S(1)} %reshape.631, f32[]{:T(128)S(6)} %neg.37), channel_id=1, replica_groups=mesh['batch'=32,'chan'=4] {'batch'}, use_global_device_ids=true, to_apply=%region_42.43 | all-reduce | flops 9985 | bytes 79880 | tf_op jit(solution)/shard_map/psum | solution.py:336
  1275.4 4.2 convert_dynamic-update-slice_fusion.2
  1279.6 1.9 convert_dynamic-update-slice_fusion.4
  1281.6 17.2 %convert_dynamic-update-slice_fusion = (bf16[1,797952]{1,0:T(2,128)(2,1)S(1)}, f32[1,497664]{1,0:T(1,128)}, f32[1,497664]{1,0:T(1,128)}, f32[1,497664]{1,0:T(1,128)}) fusion(bf16[1,797952]{1,0:T(2,128)(2,1)S(1)} %get-tuple-element.89, f32[1,497664]{1,0:T(1,128)S(1)} %copy-done.6, f32[1,497664]{1,0:T(1,128)} %get-tuple-element.65, f32[1,497664]{1,0:T(1,128)} %param.49, ...), kind=kLoop, calls=%fused_computation.141 | loop fusion | flops 7464960 | bytes 15925248
  1299.8 2.0 convert_dynamic-update-slice_fusion.3
  1303.3 3.8 convert_dynamic-update-slice_fusion.1
  1307.1 1.7 copy-done.88
  (396 shorter events, 47.8 us)
Async XLA Ops:
  7.2 390.9 %all-gather.2.cloned.1.call-start = ((), (), s32[]{:S(2)}) async-start(), calls=%async_computation.1 | async-start | bytes 52183040 | tf_op jit(solution)/shard_map/all_gather | solution.py:215
  33.2 8.0 copy-start.46
  33.2 8.6 copy-start.5
  33.3 1030.7 %all-reduce.65.cloned.1.call-start = ((), (), s32[]{:S(2)}) async-start(), calls=%async_computation.3 | async-start | bytes 1605632
  41.8 22.7 %copy-start.151 = (u32[128]{0:T(128)S(1)}, u32[128]{0:T(128)}, u32[]{:S(2)}) copy-start(u32[128]{0:T(128)} %constant.266) | copy-start | bytes 1540
  41.8 23.2 %copy-start.143 = (s32[8]{0:T(128)S(1)}, s32[8]{0:T(128)}, u32[]{:S(2)}) copy-start(s32[8]{0:T(128)} %param.29) | copy-start | bytes 100
  41.8 23.8 %copy-start.89 = (f32[2,316]{1,0:T(2,128)S(1)}, f32[2,316]{1,0:T(2,128)}, u32[]{:S(2)}) copy-start(f32[2,316]{1,0:T(2,128)} %param.38) | copy-start | bytes 7588
  467.5 11.9 copy-start.42
  479.4 71.8 %copy-start.7 = (f32[8,4,7,7,12]{4,0,3,2,1:T(8,128)S(1)}, f32[8,4,7,7,12]{4,0,3,2,1:T(8,128)}, u32[]{:S(2)}) copy-start(f32[8,4,7,7,12]{4,0,3,2,1:T(8,128)} %get-tuple-element.255) | copy-start | bytes 225796
  479.4 71.8 %copy-start.116 = (f32[12]{0:T(128)S(1)}, f32[12]{0:T(128)}, u32[]{:S(2)}) copy-start(f32[12]{0:T(128)} %get-tuple-element.240) | copy-start | bytes 148
  479.4 71.8 %copy-start.122 = (f32[12]{0:T(128)S(1)}, f32[12]{0:T(128)}, u32[]{:S(2)}) copy-start(f32[12]{0:T(128)} %get-tuple-element.241) | copy-start | bytes 148
  480.4 364.9 %copy-start.9 = (f32[8,4,7,7,32]{4,0,3,2,1:T(8,128)}, f32[8,4,7,7,32]{4,0,3,2,1:T(8,128)S(1)}, u32[]{:S(2)}) copy-start(f32[8,4,7,7,32]{4,0,3,2,1:T(8,128)S(1)} %get-tuple-element.254) | copy-start | bytes 602116
  551.2 23.8 %copy-start.103 = (f32[1,12]{1,0:T(1,128)}, f32[1,12]{1,0:T(1,128)S(1)}, u32[]{:S(2)}) copy-start(f32[1,12]{1,0:T(1,128)S(1)} %get-tuple-element.107) | copy-start | bytes 148
  707.1 205.6 %copy-start.2 = (f32[8,4,7,7,32]{4,0,3,2,1:T(8,128)}, f32[8,4,7,7,32]{4,0,3,2,1:T(8,128)S(1)}, u32[]{:S(2)}) copy-start(f32[8,4,7,7,32]{4,0,3,2,1:T(8,128)S(1)} %get-tuple-element.258) | copy-start | bytes 602116
  707.1 28.3 %copy-start.13 = (f32[8,4,7,7,96]{4,0,3,2,1:T(8,128)S(1)}, f32[8,4,7,7,96]{4,0,3,2,1:T(8,128)}, u32[]{:S(2)}) copy-start(f32[8,4,7,7,96]{4,0,3,2,1:T(8,128)} %get-tuple-element.257) | copy-start | bytes 1806340
  814.5 7.5 copy-start.41
  919.1 7.3 copy-start.91
  919.1 7.3 copy-start.95
  926.5 12.7 copy-start.12
  964.1 23.8 %copy-start.20 = (f32[8,4,7,7,48]{4,0,3,2,1:T(8,128)S(1)}, f32[8,4,7,7,48]{4,0,3,2,1:T(8,128)}, u32[]{:S(2)}) copy-start(f32[8,4,7,7,48]{4,0,3,2,1:T(8,128)} %get-tuple-element.166) | copy-start | bytes 903172
  964.1 23.8 %copy-start.21 = (f32[8,4,7,7,48]{4,0,3,2,1:T(8,128)S(1)}, f32[8,4,7,7,48]{4,0,3,2,1:T(8,128)}, u32[]{:S(2)}) copy-start(f32[8,4,7,7,48]{4,0,3,2,1:T(8,128)} %get-tuple-element.167) | copy-start | bytes 903172
  964.1 23.8 %copy-start.22 = (f32[8,4,7,7,48]{4,0,3,2,1:T(8,128)S(1)}, f32[8,4,7,7,48]{4,0,3,2,1:T(8,128)}, u32[]{:S(2)}) copy-start(f32[8,4,7,7,48]{4,0,3,2,1:T(8,128)} %get-tuple-element.168) | copy-start | bytes 903172
  964.1 23.8 %copy-start.23 = (f32[8,4,7,7,48]{4,0,3,2,1:T(8,128)S(1)}, f32[8,4,7,7,48]{4,0,3,2,1:T(8,128)}, u32[]{:S(2)}) copy-start(f32[8,4,7,7,48]{4,0,3,2,1:T(8,128)} %get-tuple-element.169) | copy-start | bytes 903172
  964.1 23.8 %copy-start.24 = (f32[8,4,7,7,48]{4,0,3,2,1:T(8,128)S(1)}, f32[8,4,7,7,48]{4,0,3,2,1:T(8,128)}, u32[]{:S(2)}) copy-start(f32[8,4,7,7,48]{4,0,3,2,1:T(8,128)} %get-tuple-element.170) | copy-start | bytes 903172
  964.1 23.8 %copy-start.25 = (f32[8,4,7,7,48]{4,0,3,2,1:T(8,128)S(1)}, f32[8,4,7,7,48]{4,0,3,2,1:T(8,128)}, u32[]{:S(2)}) copy-start(f32[8,4,7,7,48]{4,0,3,2,1:T(8,128)} %get-tuple-element.171) | copy-start | bytes 903172
  964.1 23.8 %copy-start.26 = (f32[8,4,7,7,48]{4,0,3,2,1:T(8,128)S(1)}, f32[8,4,7,7,48]{4,0,3,2,1:T(8,128)}, u32[]{:S(2)}) copy-start(f32[8,4,7,7,48]{4,0,3,2,1:T(8,128)} %get-tuple-element.172) | copy-start | bytes 903172
  964.1 23.8 %copy-start.27 = (f32[8,4,7,7,48]{4,0,3,2,1:T(8,128)S(1)}, f32[8,4,7,7,48]{4,0,3,2,1:T(8,128)}, u32[]{:S(2)}) copy-start(f32[8,4,7,7,48]{4,0,3,2,1:T(8,128)} %get-tuple-element.173) | copy-start | bytes 903172
  964.1 23.8 %copy-start.28 = (f32[8,4,7,7,48]{4,0,3,2,1:T(8,128)S(1)}, f32[8,4,7,7,48]{4,0,3,2,1:T(8,128)}, u32[]{:S(2)}) copy-start(f32[8,4,7,7,48]{4,0,3,2,1:T(8,128)} %get-tuple-element.147) | copy-start | bytes 903172
  964.1 23.8 %copy-start.29 = (f32[8,4,7,7,48]{4,0,3,2,1:T(8,128)S(1)}, f32[8,4,7,7,48]{4,0,3,2,1:T(8,128)}, u32[]{:S(2)}) copy-start(f32[8,4,7,7,48]{4,0,3,2,1:T(8,128)} %get-tuple-element.154) | copy-start | bytes 903172
  964.1 24.5 %copy-start.30 = (f32[8,4,7,7,48]{4,0,3,2,1:T(8,128)S(1)}, f32[8,4,7,7,48]{4,0,3,2,1:T(8,128)}, u32[]{:S(2)}) copy-start(f32[8,4,7,7,48]{4,0,3,2,1:T(8,128)} %get-tuple-element.155) | copy-start | bytes 903172
  964.2 24.8 %copy-start.31 = (f32[8,4,7,7,48]{4,0,3,2,1:T(8,128)S(1)}, f32[8,4,7,7,48]{4,0,3,2,1:T(8,128)}, u32[]{:S(2)}) copy-start(f32[8,4,7,7,48]{4,0,3,2,1:T(8,128)} %get-tuple-element.156) | copy-start | bytes 903172
  964.2 25.0 %copy-start.32 = (f32[8,4,7,7,48]{4,0,3,2,1:T(8,128)S(1)}, f32[8,4,7,7,48]{4,0,3,2,1:T(8,128)}, u32[]{:S(2)}) copy-start(f32[8,4,7,7,48]{4,0,3,2,1:T(8,128)} %get-tuple-element.157) | copy-start | bytes 903172
  994.9 71.9 %reduce-scatter.5.cloned.1.call-start = ((), (), s32[]{:S(2)}) async-start(), calls=%async_computation.2 | async-start | bytes 1597440
  1025.9 13.7 %copy-start.3 = (f32[8,4,7,7,32]{4,0,3,2,1:T(8,128)S(1)}, f32[8,4,7,7,32]{4,0,3,2,1:T(8,128)}, u32[]{:S(2)}) copy-start(f32[8,4,7,7,32]{4,0,3,2,1:T(8,128)} %copy-done.2) | copy-start | bytes 602116
  1025.9 13.7 %copy-start.66 = (f32[8,4,32]{2,0,1:T(8,128)S(1)}, f32[8,4,32]{2,0,1:T(8,128)}, u32[]{:S(2)}) copy-start(f32[8,4,32]{2,0,1:T(8,128)} %copy-done.65) | copy-start | bytes 12292
  1025.9 13.7 %copy-start.93 = (f32[1,32]{1,0:T(1,128)S(1)}, f32[1,32]{1,0:T(1,128)}, u32[]{:S(2)}) copy-start(f32[1,32]{1,0:T(1,128)} %copy-done.92) | copy-start | bytes 388
  1025.9 13.7 %copy-start.96 = (f32[32]{0:T(128)S(1)}, f32[32]{0:T(128)}, u32[]{:S(2)}) copy-start(f32[32]{0:T(128)} %get-tuple-element.235) | copy-start | bytes 388
  1025.9 13.7 %copy-start.97 = (f32[32]{0:T(128)S(1)}, f32[32]{0:T(128)}, u32[]{:S(2)}) copy-start(f32[32]{0:T(128)} %get-tuple-element.236) | copy-start | bytes 388
  1025.9 13.7 %copy-start.100 = (f32[32]{0:T(128)S(1)}, f32[32]{0:T(128)}, u32[]{:S(2)}) copy-start(f32[32]{0:T(128)} %copy-done.99) | copy-start | bytes 388
  1025.9 13.7 %copy-start.113 = (f32[32]{0:T(128)S(1)}, f32[32]{0:T(128)}, u32[]{:S(2)}) copy-start(f32[32]{0:T(128)} %copy-done.112) | copy-start | bytes 388
  1025.9 13.7 %copy-start.115 = (f32[32]{0:T(128)S(1)}, f32[32]{0:T(128)}, u32[]{:S(2)}) copy-start(f32[32]{0:T(128)} %copy-done.114) | copy-start | bytes 388
  1039.3 236.0 %all-reduce.67.cloned.1.call-start = ((), (), s32[]{:S(2)}) async-start(), calls=%async_computation.4 | async-start | bytes 6303744 | tf_op jit(solution)/shard_map/psum | solution.py:336
  1147.2 127.4 %slice-start = ((f32[2,256]{1,0:T(2,128)}), f32[2,96]{1,0:T(2,128)S(1)}, s32[]{:S(2)}) async-start(f32[2,256]{1,0:T(2,128)} %copy-done.76), calls=%async_computation.5 | async-start | bytes 2048 | tf_op jit(solution)/shard_map/slice | solution.py:70
  1147.2 127.4 %copy-start.90 = (f32[2,316]{1,0:T(2,128)S(1)}, f32[2,316]{1,0:T(2,128)}, u32[]{:S(2)}) copy-start(f32[2,316]{1,0:T(2,128)} %param.38) | copy-start | bytes 7588
  1147.2 127.4 %copy-start.124 = (f32[2,32]{1,0:T(2,128)S(1)}, f32[2,32]{1,0:T(2,128)}, u32[]{:S(2)}) copy-start(f32[2,32]{1,0:T(2,128)} %slice.674) | copy-start | bytes 772
  1147.2 127.4 %copy-start.126 = (f32[2,316]{1,0:T(2,128)S(1)}, f32[2,316]{1,0:T(2,128)}, u32[]{:S(2)}) copy-start(f32[2,316]{1,0:T(2,128)} %param.54) | copy-start | bytes 7588
  1147.2 127.4 %copy-start.127 = (f32[2,316]{1,0:T(2,128)S(1)}, f32[2,316]{1,0:T(2,128)}, u32[]{:S(2)}) copy-start(f32[2,316]{1,0:T(2,128)} %param.46) | copy-start | bytes 7588
  1147.2 128.1 %copy-start.40 = (f32[1,79872]{1,0:T(1,128)S(1)}, f32[1,79872]{1,0:T(1,128)}, u32[]{:S(2)}) copy-start(f32[1,79872]{1,0:T(1,128)} %param.31) | copy-start | bytes 958468
  1147.3 128.1 %copy-start.56 = (f32[1,79872]{1,0:T(1,128)S(1)}, f32[1,79872]{1,0:T(1,128)}, u32[]{:S(2)}) copy-start(f32[1,79872]{1,0:T(1,128)} %param.47) | copy-start | bytes 958468
  1149.3 130.2 %copy-start.49 = (f32[1,39936]{1,0:T(1,128)S(1)}, f32[1,39936]{1,0:T(1,128)}, u32[]{:S(2)}) copy-start(f32[1,39936]{1,0:T(1,128)} %param.32) | copy-start | bytes 479236
  1149.3 130.2 %copy-start.60 = (f32[1,39936]{1,0:T(1,128)S(1)}, f32[1,39936]{1,0:T(1,128)}, u32[]{:S(2)}) copy-start(f32[1,39936]{1,0:T(1,128)} %param.48) | copy-start | bytes 479236
  1149.3 130.2 %copy-start.61 = (f32[1,39936]{1,0:T(1,128)S(1)}, f32[1,39936]{1,0:T(1,128)}, u32[]{:S(2)}) copy-start(f32[1,39936]{1,0:T(1,128)} %param.40) | copy-start | bytes 479236
  1149.9 131.6 %copy-start.6 = (f32[1,497664]{1,0:T(1,128)S(1)}, f32[1,497664]{1,0:T(1,128)}, u32[]{:S(2)}) copy-start(f32[1,497664]{1,0:T(1,128)} %param.33) | copy-start | bytes 5971972
  1281.5 17.3 %copy-start.64 = (f32[1,9984]{1,0:T(1,128)S(1)}, f32[1,9984]{1,0:T(1,128)}, u32[]{:S(2)}) copy-start(f32[1,9984]{1,0:T(1,128)} %param.34) | copy-start | bytes 119812
  1281.5 17.4 %copy-start.78 = (f32[1,9984]{1,0:T(1,128)S(1)}, f32[1,9984]{1,0:T(1,128)}, u32[]{:S(2)}) copy-start(f32[1,9984]{1,0:T(1,128)} %param.50) | copy-start | bytes 119812
  1281.5 17.4 %copy-start.79 = (f32[1,9984]{1,0:T(1,128)S(1)}, f32[1,9984]{1,0:T(1,128)}, u32[]{:S(2)}) copy-start(f32[1,9984]{1,0:T(1,128)} %param.42) | copy-start | bytes 119812
  1281.5 18.3 %copy-start.47 = (f32[1,41472]{1,0:T(1,128)S(1)}, f32[1,41472]{1,0:T(1,128)}, u32[]{:S(2)}) copy-start(f32[1,41472]{1,0:T(1,128)} %param.35) | copy-start | bytes 497668
  1281.5 18.3 %copy-start.57 = (f32[1,41472]{1,0:T(1,128)S(1)}, f32[1,41472]{1,0:T(1,128)}, u32[]{:S(2)}) copy-start(f32[1,41472]{1,0:T(1,128)} %param.51) | copy-start | bytes 497668
  1281.5 18.3 %copy-start.58 = (f32[1,41472]{1,0:T(1,128)S(1)}, f32[1,41472]{1,0:T(1,128)}, u32[]{:S(2)}) copy-start(f32[1,41472]{1,0:T(1,128)} %param.43) | copy-start | bytes 497668
  1281.5 18.3 %copy-start.59 = (f32[1,41472]{1,0:T(1,128)S(1)}, f32[1,41472]{1,0:T(1,128)}, u32[]{:S(2)}) copy-start(f32[1,41472]{1,0:T(1,128)} %get-tuple-element.66) | copy-start | bytes 497668
  1281.6 20.2 %copy-start.52 = (f32[1,26624]{1,0:T(1,128)S(1)}, f32[1,26624]{1,0:T(1,128)}, u32[]{:S(2)}) copy-start(f32[1,26624]{1,0:T(1,128)} %param.36) | copy-start | bytes 319492
  1281.6 20.2 %copy-start.69 = (f32[1,26624]{1,0:T(1,128)S(1)}, f32[1,26624]{1,0:T(1,128)}, u32[]{:S(2)}) copy-start(f32[1,26624]{1,0:T(1,128)} %param.52) | copy-start | bytes 319492
  1281.6 20.2 %copy-start.70 = (f32[1,26624]{1,0:T(1,128)S(1)}, f32[1,26624]{1,0:T(1,128)}, u32[]{:S(2)}) copy-start(f32[1,26624]{1,0:T(1,128)} %param.44) | copy-start | bytes 319492
  1281.6 20.2 %copy-start.71 = (f32[1,26624]{1,0:T(1,128)S(1)}, f32[1,26624]{1,0:T(1,128)}, u32[]{:S(2)}) copy-start(f32[1,26624]{1,0:T(1,128)} %get-tuple-element.67) | copy-start | bytes 319492
  (95 other events, 363.7 us)
Sparse Core Ops, SparseCore 0:
  33.4 364.6 all-gather.1
  995.0 39.8 all-reduce.64
  1039.4 23.4 reduce-scatter.4
  1146.4 105.2 all-reduce.66
where the time goes:
time: 1330 us; the launch traced here: 1320 us
  blocking collectives  500 us (38%)
  waiting for transfers between devices  329 us (25%)
  local copies, waits for them, and re-layouts  270 us (20%)
  other arithmetic  131 us (10%)
  matrix products  67.6 us (5%)
  between operations  18 us (1%)
    all_gather x1, waiting for transfers between devices, per_device(): complete = lax.all_gather(local_field, 'chan', axis=4, tiled=True)  329 us
    psum x1, blocking collectives, per_device(): summed = lax.psum(tuple(local_grads), 'batch')  125 us
    all_gather x1, blocking collectives, per_device(): lax.all_gather(results[1][0].astype(jnp.bfloat16), 'chan', axis=4, tiled=...  76 us
    psum x1, blocking collectives, per_device(): lax.psum(jnp.concatenate([column_sums(values, voxel_mask) for values in s...  67.8 us
    psum x1, blocking collectives, per_device(): stats_a, counted = lax.psum((local_stats, jnp.sum(step_mask)), 'batch')  67.6 us
    all_gather x1, local copies, waits for them, and re-layouts, per_device(): complete = lax.all_gather(local_field, 'chan', axis=4, tiled=True)  63.3 us
    psum x1, blocking collectives, per_device(): lax.psum((jnp.concatenate([record[1] for record in back_a], axis=1), loss...  62.7 us
    psum x1, blocking collectives, per_device(): lax.psum(jnp.concatenate([record[1] for record in back_b], axis=1), 'batch')  62.7 us
  transfers between devices with their start and end apart: 4, of which 1 were waited for; matrix products, arithmetic and copies ran while one was open for 8% of the time, Pallas kernels for 0%

commit v1 on v0

v1 whole, which is shorter than its diff:
```python
import math
from functools import partial

import jax
import jax.numpy as jnp
from jax import lax
from jax.experimental import pallas as pl
from jax.experimental.pallas import tpu as pltpu
from jax.sharding import PartitionSpec as P

CIN = 832
B0 = 384
R1 = 192
O1 = 384
R2 = 48
O2 = 128
B3 = 128
CLASSES = 400
SIDE = 7
STEP = 5
NC = 4
NB = 32
POS = SIDE * SIDE
ROWS = 32
VOX = POS * ROWS
GROUPS = VOX // 8
GPAD = 208
CB = CIN // NC
GW = 8 * CB
HALF = 25

EPS = 1e-05
BETA_ONE = 0.5
BETA_TWO = 0.5
DECAY = 0.01
MOMENTUM = 0.99

MESH = pl.DeviceIdType.MESH
F32 = jnp.float32
BF16 = jnp.bfloat16


def step_rates():
    return [
        1.5 / math.sqrt(CIN),
        1.5 / math.sqrt(CIN),
        1.5 / math.sqrt(27 * R1),
        1.5 / math.sqrt(CIN),
        1.5 / math.sqrt(27 * R2),
        1.5 / math.sqrt(CIN),
        0.2,
        0.3,
    ]


def adamw(weight, moment_one, moment_two, gradient, step_rate):
    first_new = BETA_ONE * moment_one + (1.0 - BETA_ONE) * gradient
    second_new = BETA_TWO * moment_two + (1.0 - BETA_TWO) * gradient * gradient
    first_hat = first_new / (1.0 - BETA_ONE**STEP)
    second_hat = second_new / (1.0 - BETA_TWO**STEP)
    weight_new = weight - step_rate * (first_hat / (jnp.sqrt(second_hat) + 1e-08) + DECAY * weight)
    return (first_new, second_new, weight_new)


def window_of(r):
    start = CB * r
    tile, offset = divmod(start, 128)
    lanes = 256 if offset + CB <= 256 else 384
    return tile * 128, offset, lanes


def dot(a, b):
    return jnp.dot(a, b, preferred_element_type=F32)


def dot_t(a, b, ca, cb):
    return lax.dot_general(a, b, (((ca,), (cb,)), ((), ())), preferred_element_type=F32)


def send_to(src, dst, send, recv, target):
    return pltpu.make_async_remote_copy(
        src_ref=src, dst_ref=dst, send_sem=send, recv_sem=recv, device_id=target,
        device_id_type=MESH,
    )


def batch_peer(me, d):
    return {"batch": lax.rem(me + d, NB)}


def chan_peer(me, d):
    return {"chan": lax.rem(me + d, NC)}


def share_start(buf, me, send, recv):
    def one(d, carry):
        send_to(buf.at[me], buf.at[me], send.at[d], recv.at[d], batch_peer(me, d)).start()
        return carry

    lax.fori_loop(1, NB, one, 0)


def share_wait(buf, me, send, recv):
    def one(d, carry):
        src = lax.rem(me - d + NB, NB)
        send_to(buf.at[src], buf.at[src], send.at[d], recv.at[d], batch_peer(me, d)).wait_recv()
        return carry

    lax.fori_loop(1, NB, one, 0)

    def two(d, carry):
        send_to(buf.at[me], buf.at[me], send.at[d], recv.at[d], batch_peer(me, d)).wait_send()
        return carry

    lax.fori_loop(1, NB, two, 0)


def total_of(buf, count):
    acc = buf[0]
    for slot in range(1, count):
        acc = acc + buf[slot]
    return acc


def core_kernel(
    x_ref, len_ref, lab_ref, w1_ref, wc_ref, wct_ref, r_ref, aff_ref,
    gwc_ref, gw1_ref, gr_ref, st_ref, sc_ref,
    xf, xg, w1s, ynat, ypos, box, ob, msg, got, apad, acol, at, y2, dpre, dypad, dm, dgot, dnat,
    lbuf, sbuf_a, sbuf_b, sbuf_c, sbuf_d,
    xs, xr, ms, mr, ls, lr, ds_, dr,
    as_, ar, bs, br, cs, cr, es, er,
):
    me_b = lax.axis_index("batch")
    me = lax.axis_index("chan")

    barrier = pltpu.get_barrier_semaphore()

    def greet(d, carry):
        pl.semaphore_signal(barrier, inc=1, device_id=batch_peer(me_b, d), device_id_type=MESH)
        return carry

    lax.fori_loop(1, NB, greet, 0)
    for d in range(1, NC):
        pl.semaphore_signal(barrier, inc=1, device_id=chan_peer(me, d), device_id_type=MESH)

    def flat_rows(i, carry):
        v = x_ref[:, pl.ds(pl.multiple_of(i * 1024, 1024), 1024)].astype(F32)
        xf[pl.ds(pl.multiple_of(i * 8, 8), 8), :] = v.reshape(8, 128)
        return carry

    lax.fori_loop(0, 318, flat_rows, 0, unroll=6)
    xf[pl.ds(2544, 4), :] = x_ref[:, 318 * 1024 : 318 * 1024 + 512].astype(F32).reshape(4, 128)
    xf[pl.ds(2548, 2704 - 2548), :] = jnp.zeros((2704 - 2548, 128), F32)
    for i in range(13):
        xg[me, :, 128 * i : 128 * i + 128] = xf[pl.ds(i, GPAD, stride=13), :].astype(BF16)

    pl.semaphore_wait(barrier, NB - 1 + NC - 1)

    right, left = chan_peer(me, 1), chan_peer(me, NC - 1)
    left_i, right_i = lax.rem(me + NC - 1, NC), lax.rem(me + 1, NC)
    cut = 112

    def part(who, low):
        return xg.at[who, 0:cut] if low else xg.at[who, cut:GPAD]

    hops = []
    for i, (low, to) in enumerate([(True, right), (False, left), (False, right), (True, left)]):
        c = send_to(part(me, low), part(me, low), xs.at[i], xr.at[i], to)
        c.start()
        hops.append(c)

    rowi = lax.broadcasted_iota(jnp.int32, (ROWS, 128), 0)
    lane = lax.broadcasted_iota(jnp.int32, (ROWS, 128), 1)
    clip = rowi // 4
    step = rowi - clip * 4
    lens = jnp.zeros((ROWS, 128), jnp.int32)
    for c in range(8):
        lens = jnp.where(clip == c, len_ref[c], lens)
    mask = (step < lens).astype(F32)
    has_prev = (step > 0).astype(F32)
    has_next = (step < 3).astype(F32)

    def prev_t(v):
        return pltpu.roll(v, 1, 0) * has_prev

    def next_t(v):
        return pltpu.roll(v, ROWS - 1, 0) * has_next

    n_t = mask + prev_t(mask) + next_t(mask)
    is_pool = lane >= 96
    low_half = lane < 64

    def zero_w(i, carry):
        w1s[i] = jnp.zeros((NC, 384, 256), BF16)
        return carry

    lax.fori_loop(0, 8, zero_w, 0)
    for r in range(8):
        _, off, _ = window_of(r)
        for k in range(NC):
            w1s[r, k, off : off + CB, :] = w1_ref[k * CB : (k + 1) * CB, :]

    def zero_pad(i, carry):
        apad[i] = jnp.zeros((ROWS, 256), BF16)
        dypad[i] = jnp.zeros((ROWS, 384), BF16)
        box[i] = jnp.zeros((ROWS, 128), F32)
        return carry

    lax.fori_loop(0, 81, zero_pad, 0)
    dnat[...] = jnp.zeros_like(dnat)

    hops[0].wait_recv()
    f0 = send_to(part(left_i, True), part(left_i, True), xs.at[4], xr.at[4], right)
    f0.start()
    hops[1].wait_recv()
    f1 = send_to(part(right_i, False), part(right_i, False), xs.at[5], xr.at[5], left)
    f1.start()
    hops[2].wait_recv()
    hops[3].wait_recv()
    f0.wait()
    f1.wait()
    for c in hops:
        c.wait_send()

    for r in range(8):
        first, _, lanes = window_of(r)
        acc = jnp.zeros((GPAD, 256), F32)
        for k in range(NC):
            acc = acc + dot(xg[k, :, first : first + lanes], w1s[r, k, 0:lanes, :])
        ynat[0, pl.ds(r, GPAD, stride=8), :] = acc[:, 0:128]
        ynat[1, pl.ds(r, GPAD, stride=8), :] = acc[:, 128:256]

    def padded(p):
        return (p // SIDE + 1) * 9 + lax.rem(p, SIDE) + 1

    def to_pos(p, carry):
        v = ynat[0, pl.ds(p, ROWS, stride=POS), :]
        ypos[p, :, 0:128] = v
        ypos[p, :, 128:256] = ynat[1, pl.ds(p, ROWS, stride=POS), :]
        mz = v * mask
        box[padded(p)] = mz + prev_t(mz) + next_t(mz)
        return carry

    lax.fori_loop(0, POS, to_pos, 0)

    def spread(p):
        h, w = p // SIDE, lax.rem(p, SIDE)
        acc = jnp.zeros((ROWS, 128), F32)
        for dh in range(3):
            for dw in range(3):
                acc = acc + box[(h + dh) * 9 + w + dw]
        n_h = 3 - (h == 0).astype(jnp.int32) - (h == SIDE - 1).astype(jnp.int32)
        n_w = 3 - (w == 0).astype(jnp.int32) - (w == SIDE - 1).astype(jnp.int32)
        return acc, (n_h * n_w).astype(F32)

    def pool(p, carry):
        s1, s2 = carry
        acc, n = spread(p)
        v = ypos[p]
        v0 = jnp.where(is_pool, acc / jnp.maximum(n_t * n, 1.0), v[:, 0:128])
        v1 = v[:, 128:256]
        ypos[p] = jnp.concatenate([v0, v1], axis=1)
        m0, m1 = v0 * mask, v1 * mask
        return (
            s1 + jnp.concatenate([m0, m1], axis=1),
            s2 + jnp.concatenate([m0 * v0, m1 * v1], axis=1),
        )

    zero256 = jnp.zeros((ROWS, 256), F32)
    zero128 = jnp.zeros((ROWS, 128), F32)
    s1, s2 = lax.fori_loop(0, POS, pool, (zero256, zero256))

    def col(v):
        return jnp.sum(v, axis=0, keepdims=True)

    def pack_rows(rows):
        fill = [jnp.zeros((1, 128), F32)] * (8 - len(rows))
        return jnp.concatenate(list(rows) + fill, axis=0)

    sbuf_a[me_b] = pack_rows(
        [col(s1[:, 0:128]), col(s1[:, 128:256]), col(s2[:, 0:128]), col(s2[:, 128:256]), col(mask)]
    )
    share_start(sbuf_a, me_b, as_, ar)
    share_wait(sbuf_a, me_b, as_, ar)
    tot = total_of(sbuf_a, NB)
    counted = tot[4:5, :]
    voxels = counted * float(POS)

    def norm_of(sum1, sum2, tile):
        avg = sum1 / voxels
        var = sum2 / voxels - avg * avg
        inv = lax.rsqrt(var + EPS)
        gain = aff_ref[0:1, 128 * tile : 128 * tile + 128]
        bias = aff_ref[1:2, 128 * tile : 128 * tile + 128]
        return avg, var, inv, gain, bias

    n0 = norm_of(tot[0:1], tot[2:3], 0)
    n1 = norm_of(tot[1:2], tot[3:4], 1)

    def forward(y, n):
        normed = (y - n[0]) * n[2]
        pre = n[3] * normed + n[4]
        sig = jax.nn.sigmoid(pre)
        return normed, pre, sig

    def act1(p, carry):
        _, pre, sig = forward(ypos[p][:, 128:256], n1)
        ob[p] = (mask * (pre * sig))
        return carry

    lax.fori_loop(0, POS, act1, 0)
    ob[POS] = zero128

    def to_msg(p, carry):
        msg[p] = jnp.where(low_half, ob[p], pltpu.roll(ob[p + HALF], 64, 1)).astype(BF16)
        return carry

    lax.fori_loop(0, HALF, to_msg, 0)
    ms_c = []
    for d in range(1, NC):
        c = send_to(msg, got.at[me], ms.at[d], mr.at[d], chan_peer(me, d))
        c.start()
        ms_c.append(c)
    got[me] = msg[...]

    def act0(p, carry):
        _, pre, sig = forward(ypos[p][:, 0:128], n0)
        return carry + mask * (pre * sig)

    feat0 = lax.fori_loop(0, POS, act0, zero128)

    for c in ms_c:
        c.wait_recv()

    def unpack(p, carry):
        g = [got[j, p].astype(F32) for j in range(NC)]
        rl = [pltpu.roll(v, 64, 1) for v in g]
        low = jnp.concatenate(
            [jnp.where(low_half, g[0], rl[1]), jnp.where(low_half, g[2], rl[3])], axis=1
        ).astype(BF16)
        apad[padded(p)] = low
        acol[p] = low
        high = jnp.concatenate(
            [jnp.where(low_half, rl[0], g[1]), jnp.where(low_half, rl[2], g[3])], axis=1
        ).astype(BF16)

        @pl.when(p < POS - HALF)
        def _():
            apad[padded(p + HALF)] = high
            acol[p + HALF] = high

        return carry

    lax.fori_loop(0, HALF, unpack, 0)

    def conv(h, carry):
        s1, s2 = carry
        acc = jnp.zeros((SIDE * ROWS, 384), F32)
        for q in range(9):
            dh, dw = divmod(q, 3)
            lhs = apad[pl.ds((h + dh) * 9 + dw, SIDE)].reshape(SIDE * ROWS, 256)
            acc = acc + dot(lhs, wc_ref[q])
        for w in range(SIDE):
            t = acc[w * ROWS : (w + 1) * ROWS]
            y = t[:, 128:256] + prev_t(t[:, 0:128]) + next_t(t[:, 256:384])
            y2[h * SIDE + w] = y
            m = y * mask
            s1 = s1 + m
            s2 = s2 + m * y
        return s1, s2

    s1, s2 = lax.fori_loop(0, SIDE, conv, (zero128, zero128))
    sbuf_b[me_b] = pack_rows([col(s1), col(s2)])
    share_start(sbuf_b, me_b, bs, br)
    at[...] = jnp.transpose(acol[...].reshape(VOX, 256))
    share_wait(sbuf_b, me_b, bs, br)
    totb = total_of(sbuf_b, NB)
    n2 = norm_of(totb[0:1], totb[1:2], 2)

    def act2(p, carry):
        _, pre, sig = forward(y2[p], n2)
        return carry + mask * (pre * sig)

    feat2 = lax.fori_loop(0, POS, act2, zero128)
    feature = (jnp.concatenate([feat0, feat2], axis=1) / float(POS)).astype(BF16)
    lbuf[me] = dot(feature, r_ref[...])
    ls_c = []
    for d in range(1, NC):
        c = send_to(lbuf.at[me], lbuf.at[me], ls.at[d], lr.at[d], chan_peer(me, d))
        c.start()
        ls_c.append(c)
    for c in ls_c:
        c.wait_recv()
    logits = total_of(lbuf, NC)
    cls = lax.broadcasted_iota(jnp.int32, (ROWS, 512), 1)
    row512 = lax.broadcasted_iota(jnp.int32, (ROWS, 512), 0)
    labs = jnp.zeros((ROWS, 512), jnp.int32)
    for i in range(ROWS):
        labs = jnp.where(row512 == i, lab_ref[i // 4, i % 4], labs)
    real = cls < CLASSES
    logits = jnp.where(real, logits, -1e30)
    peak = jnp.max(logits, axis=1, keepdims=True)
    ex = jnp.exp(logits - peak)
    se = jnp.sum(ex, axis=1, keepdims=True)
    logprob = logits - peak - jnp.log(se)
    mask1 = mask[:, 0:1]
    hit = cls == labs
    loss_rows = -jnp.sum(jnp.where(hit, logprob, 0.0), axis=1, keepdims=True) * mask1
    soft = jnp.where(real, jnp.exp(logprob), 0.0)
    dlog = ((soft - hit.astype(F32)) * mask1 / counted[:, 0:1]).astype(BF16)
    dfeat = dot_t(dlog, r_ref[...], 1, 1) / float(POS)
    df0, df2 = dfeat[:, 0:128], dfeat[:, 128:256]

    def back(y, n, dout):
        normed, pre, sig = forward(y, n)
        return dout * mask * sig * (1.0 + pre * (1.0 - sig)), normed

    def back02(p, carry):
        g0, b0, g2, b2 = carry
        d0, m0 = back(ypos[p][:, 0:128], n0, df0)
        d2, m2 = back(y2[p], n2, df2)
        dpre[p] = jnp.concatenate([d0, d2], axis=1)
        return g0 + d0 * m0, b0 + d0, g2 + d2 * m2, b2 + d2

    g0, b0, g2, b2 = lax.fori_loop(0, POS, back02, (zero128,) * 4)
    loss_row = jnp.broadcast_to(jnp.sum(loss_rows, axis=0, keepdims=True), (1, 128))
    sbuf_c[me_b] = pack_rows([col(g0), col(b0), col(g2), col(b2), loss_row])
    share_start(sbuf_c, me_b, cs, cr)
    gr_ref[...] = dot_t(feature, dlog, 0, 0)
    for c in ls_c:
        c.wait_send()
    for c in ms_c:
        c.wait_send()
    share_wait(sbuf_c, me_b, cs, cr)
    totc = total_of(sbuf_c, NB)

    def finish(y, n, d, gg, gb):
        normed = (y - n[0]) * n[2]
        return mask * n[3] * n[2] * (d - gb / voxels - normed * gg / voxels)

    def dy2_at(p, carry):
        d = dpre[p]
        v = finish(y2[p], n2, d[:, 128:256], totc[2:3], totc[3:4])
        dypad[padded(p)] = jnp.concatenate([next_t(v), v, prev_t(v)], axis=1).astype(BF16)
        return carry

    lax.fori_loop(0, POS, dy2_at, 0)

    def conv_back(h, carry):
        acc = jnp.zeros((SIDE * ROWS, 256), F32)
        for q in range(9):
            dh, dw = divmod(q, 3)
            lhs = dypad[pl.ds((h + 2 - dh) * 9 + 2 - dw, SIDE)].reshape(SIDE * ROWS, 384)
            acc = acc + dot(lhs, wct_ref[q])
        for t in range(2):
            ynat[t, pl.ds(pl.multiple_of(h * SIDE * ROWS, SIDE * ROWS), SIDE * ROWS), :] = acc[
                :, 128 * t : 128 * t + 128
            ]
        return carry

    lax.fori_loop(0, SIDE, conv_back, 0)

    def to_dm(p, carry):
        for j in range(NC):
            a = ynat[j // 2, pl.ds(pl.multiple_of(p * ROWS, ROWS), ROWS), :]
            b = ynat[j // 2, pl.ds(pl.multiple_of((p + HALF) * ROWS, ROWS), ROWS), :]
            if j % 2 == 0:
                dm[j, p] = jnp.where(low_half, a, pltpu.roll(b, 64, 1))
            else:
                dm[j, p] = jnp.where(low_half, pltpu.roll(a, 64, 1), b)
        return carry

    for t in range(2):
        ynat[t, pl.ds(VOX, ROWS), :] = zero128
    lax.fori_loop(0, HALF, to_dm, 0)
    ds_c = []
    for d in range(1, NC):
        to = lax.rem(me + d, NC)
        c = send_to(dm.at[to], dgot.at[me], ds_.at[d], dr.at[d], chan_peer(me, d))
        c.start()
        ds_c.append(c)
    dgot[me] = dm[me]

    def grad_conv(q, carry):
        dh = q // 3
        dw = q - dh * 3
        rhs = jnp.concatenate(
            [
                dypad[pl.ds((h + 2 - dh) * 9 + 2 - dw, SIDE)].reshape(SIDE * ROWS, 384)
                for h in range(SIDE)
            ],
            axis=0,
        )
        gwc_ref[q] = dot(at[...], rhs)
        return carry

    lax.fori_loop(0, 9, grad_conv, 0)

    def dy0_at(p, carry):
        v = finish(ypos[p][:, 0:128], n0, dpre[p][:, 0:128], totc[0:1], totc[1:2])
        v = v.astype(BF16).astype(F32)
        h, w = p // SIDE, lax.rem(p, SIDE)
        n_h = 3 - (h == 0).astype(jnp.int32) - (h == SIDE - 1).astype(jnp.int32)
        n_w = 3 - (w == 0).astype(jnp.int32) - (w == SIDE - 1).astype(jnp.int32)
        share = v / jnp.maximum(n_t * (n_h * n_w).astype(F32), 1.0)
        box[padded(p)] = share + prev_t(share) + next_t(share)
        ypos[p, :, 0:128] = v
        return carry

    lax.fori_loop(0, POS, dy0_at, 0)

    def dy0_nat(p, carry):
        acc, _ = spread(p)
        v = jnp.where(is_pool, acc * mask, ypos[p][:, 0:128])
        lowv = v - v.astype(BF16).astype(F32)
        dnat[0, pl.ds(p, ROWS, stride=POS), :] = v
        dnat[1, pl.ds(p, ROWS, stride=POS), :] = lowv
        return carry

    lax.fori_loop(0, POS, dy0_nat, 0)

    for tile in range(2):
        gw1_ref[:, 128 * tile : 128 * tile + 128] = jnp.zeros((CIN, 128), F32)

    def grad_one(r, width, fold):
        first, off, lanes = window_of(r)
        rhs = jnp.concatenate(
            [dnat[t, pl.ds(r, GPAD, stride=8), :] for t in range(width // 128)], axis=1
        ).astype(BF16)
        for k in range(NC):
            res = dot_t(xg[k, :, first : first + lanes], rhs, 0, 0)[off : off + CB]
            if fold:
                gw1_ref[k * CB : (k + 1) * CB, 0:128] += res[:, 0:128] + res[:, 128:256]
            else:
                gw1_ref[k * CB : (k + 1) * CB, 128:256] += res

    for r in range(8):
        grad_one(r, 256, True)

    for c in ds_c:
        c.wait_recv()

    def back1(p, carry):
        g1, b1 = carry
        s = dgot[0, p] + dgot[1, p] + dgot[2, p] + dgot[3, p]
        d, m = back(ypos[p][:, 128:256], n1, jnp.where(low_half, s, 0.0))
        dpre[p, :, 0:128] = d
        g1, b1 = g1 + d * m, b1 + d
        q = jnp.minimum(p + HALF, POS - 1)
        live = (p < POS - HALF).astype(F32)
        d, m = back(ypos[q][:, 128:256], n1, jnp.where(low_half, pltpu.roll(s, 64, 1), 0.0) * live)

        @pl.when(p < POS - HALF)
        def _():
            dpre[p + HALF, :, 0:128] = d

        return g1 + d * m, b1 + d

    g1, b1 = lax.fori_loop(0, HALF, back1, (zero128, zero128))
    sbuf_d[me_b] = pack_rows([col(g1), col(b1)])
    share_start(sbuf_d, me_b, es, er)
    for c in ds_c:
        c.wait_send()
    share_wait(sbuf_d, me_b, es, er)
    totd = total_of(sbuf_d, NB)

    def dy1_nat(p, carry):
        v = finish(ypos[p][:, 128:256], n1, dpre[p][:, 0:128], totd[0:1], totd[1:2])
        dnat[0, pl.ds(p, ROWS, stride=POS), :] = v
        return carry

    lax.fori_loop(0, POS, dy1_nat, 0)
    for r in range(8):
        grad_one(r, 128, False)

    fix = voxels / (voxels - 1.0)
    for tile, n, gg, gb in (
        (0, n0, totc[0:1], totc[1:2]),
        (1, n1, totd[0:1], totd[1:2]),
        (2, n2, totc[2:3], totc[3:4]),
    ):
        st_ref[:, 128 * tile : 128 * tile + 128] = pack_rows([gg, gb, n[0], n[1] * fix])
    sc_ref[...] = pack_rows([totc[4:5], counted])


def core(x, lengths, labels, w1, wc, wct, r, aff):
    vm = pl.BlockSpec(memory_space=pltpu.VMEM)
    sm = pl.BlockSpec(memory_space=pltpu.SMEM)
    dma = pltpu.SemaphoreType.DMA
    return pl.pallas_call(
        core_kernel,
        out_shape=(
            jax.ShapeDtypeStruct((9, 256, 384), F32),
            jax.ShapeDtypeStruct((CIN, 256), F32),
            jax.ShapeDtypeStruct((256, 512), F32),
            jax.ShapeDtypeStruct((8, 384), F32),
            jax.ShapeDtypeStruct((8, 128), F32),
        ),
        in_specs=[vm, sm, sm, vm, vm, vm, vm, vm],
        out_specs=(vm,) * 5,
        scratch_shapes=[
            pltpu.VMEM((13 * GPAD, 128), F32),
            pltpu.VMEM((NC, GPAD, GW), BF16),
            pltpu.VMEM((8, NC, 384, 256), BF16),
            pltpu.VMEM((2, 8 * GPAD, 128), F32),
            pltpu.VMEM((POS, ROWS, 256), F32),
            pltpu.VMEM((81, ROWS, 128), F32),
            pltpu.VMEM((POS + 1, ROWS, 128), F32),
            pltpu.VMEM((HALF, ROWS, 128), BF16),
            pltpu.VMEM((NC, HALF, ROWS, 128), BF16),
            pltpu.VMEM((81, ROWS, 256), BF16),
            pltpu.VMEM((POS, ROWS, 256), BF16),
            pltpu.VMEM((256, VOX), BF16),
            pltpu.VMEM((POS, ROWS, 128), F32),
            pltpu.VMEM((POS, ROWS, 256), F32),
            pltpu.VMEM((81, ROWS, 384), BF16),
            pltpu.VMEM((NC, HALF, ROWS, 128), F32),
            pltpu.VMEM((NC, HALF, ROWS, 128), F32),
            pltpu.VMEM((2, 8 * GPAD, 128), F32),
            pltpu.VMEM((NC, ROWS, 512), F32),
            pltpu.VMEM((NB, 8, 128), F32),
            pltpu.VMEM((NB, 8, 128), F32),
            pltpu.VMEM((NB, 8, 128), F32),
            pltpu.VMEM((NB, 8, 128), F32),
            dma((6,)), dma((6,)), dma((NC,)), dma((NC,)), dma((NC,)), dma((NC,)), dma((NC,)),
            dma((NC,)),
            dma((NB,)), dma((NB,)), dma((NB,)), dma((NB,)), dma((NB,)), dma((NB,)), dma((NB,)),
            dma((NB,)),
        ],
        compiler_params=pltpu.CompilerParams(
            collective_id=0, has_side_effects=True, vmem_limit_bytes=58 << 20
        ),
        name="block",
    )(x, lengths, labels, w1, wc, wct, r, aff)


def split_columns(packed, widths):
    pieces = []
    offset = 0
    for channels in widths:
        pieces.append(packed[..., offset : offset + channels])
        offset = offset + channels
    return pieces


def conv_weights(spatial, volume):
    sp = spatial.reshape(3, 9, NC, 48, 96)
    vo = volume.reshape(3, 9, NC, 12, 32)
    sp = jnp.pad(sp, ((0, 0), (0, 0), (0, 0), (0, 16), (0, 32)))
    vo = jnp.pad(vo, ((0, 0), (0, 0), (0, 0), (48, 4), (96, 0)))
    both = (sp + vo).astype(BF16)
    return jnp.transpose(both, (1, 2, 3, 0, 4)).reshape(9, 256, 384)


def conv_grads(g):
    g = g.reshape(9, NC, 64, 3, 128)
    sp = jnp.transpose(g[:, :, 0:48, :, 0:96], (3, 0, 1, 2, 4)).reshape(1, -1)
    vo = jnp.transpose(g[:, :, 48:60, :, 96:128], (3, 0, 1, 2, 4)).reshape(1, -1)
    return sp, vo


def per_device(
    features, lengths, labels, direct, squeeze, spatial, shrink, volume, pooled, readout, affine,
    first_direct, first_squeeze, first_spatial, first_shrink, first_volume, first_pooled,
    first_readout, first_affine, second_direct, second_squeeze, second_spatial, second_shrink,
    second_volume, second_pooled, second_readout, second_affine, running,
):
    masters = [direct, squeeze, spatial, shrink, volume, pooled, readout, affine]
    firsts = [
        first_direct, first_squeeze, first_spatial, first_shrink, first_volume, first_pooled,
        first_readout, first_affine,
    ]
    seconds = [
        second_direct, second_squeeze, second_spatial, second_shrink, second_volume,
        second_pooled, second_readout, second_affine,
    ]
    w1 = jnp.concatenate(
        [
            direct.reshape(CIN, 96), pooled.reshape(CIN, 32), squeeze.reshape(CIN, 48),
            shrink.reshape(CIN, 12), jnp.zeros((CIN, 68), F32),
        ],
        axis=1,
    ).astype(BF16)
    wc = conv_weights(spatial, volume)
    wct = jnp.transpose(wc, (0, 2, 1))
    rd = readout.reshape(256, CLASSES)
    rp = jnp.concatenate([rd[0:96], rd[224:256], rd[96:192], rd[192:224]], axis=0)
    rp = jnp.pad(rp, ((0, 0), (0, 112))).astype(BF16)
    a_d, a_s, a_k, a_p, a_sp, a_v = split_columns(affine, [96, 48, 12, 32, 96, 32])
    aff = jnp.concatenate([a_d, a_p, a_s, a_k, jnp.zeros((2, 68), F32), a_sp, a_v], axis=1)
    aff = jnp.pad(aff, ((0, 6), (0, 0)))

    gwc, gw1, gr, stats, scal = core(features, lengths, labels, w1, wc, wct, rp, aff)

    g_sp, g_vo = conv_grads(gwc)
    g_rd = jnp.concatenate([gr[0:96], gr[128:224], gr[224:256], gr[96:128]], axis=0)[:, :CLASSES]
    local = [
        gw1[:, 0:96].reshape(1, -1),
        gw1[:, 128:176].reshape(1, -1),
        g_sp,
        gw1[:, 176:188].reshape(1, -1),
        g_vo,
        gw1[:, 96:128].reshape(1, -1),
        g_rd.reshape(1, -1),
    ]
    grads = list(lax.psum(tuple(local), "batch"))

    def unlanes(rows):
        return jnp.concatenate(
            [rows[:, 0:96], rows[:, 128:188], rows[:, 96:128], rows[:, 256:384]], axis=1
        )

    grads.append(unlanes(stats[0:2]))
    rates = step_rates()
    updated = [
        adamw(masters[i], firsts[i], seconds[i], grads[i], rates[i]) for i in range(8)
    ]
    running_next = MOMENTUM * running + (1.0 - MOMENTUM) * unlanes(stats[2:4])
    copies = jnp.concatenate([updated[i][2] for i in range(7)], axis=1).astype(BF16)
    return (
        *[updated[i][0] for i in range(8)],
        *[updated[i][1] for i in range(8)],
        *[updated[i][2] for i in range(8)],
        running_next,
        scal[0, 0],
        scal[1, 0],
        copies,
    )


def solution(mesh):
    flat = P("chan", None)
    wide = P(None, "chan")
    weights = (flat,) * 7 + (wide,)
    return jax.shard_map(
        per_device,
        mesh=mesh,
        in_specs=(P("chan", "batch"), P("batch"), P("batch", None)) + weights * 3 + (wide,),
        out_specs=weights * 3 + (wide, P(), P(), flat),
        check_vma=False,
    )
```

time: 1330 us -> 398 us (0.30)
  blocking collectives: 500 us -> 126 us
  waiting for transfers between devices: 329 us -> 0.02 us
  local copies, waits for them, and re-layouts: 270 us -> 68.5 us
  Pallas kernels: 0 us -> 126 us
  other arithmetic: 131 us -> 57.4 us
  matrix products: 67.6 us -> 0 us
    all_gather x1 -> x0, waiting for transfers between devices: 329 us -> none  [per_device(): complete = lax.all_gather(local_field, 'chan', axis=4, tiled=True)]
    psum x6 -> x1, blocking collectives: 403 us -> 126 us  [per_device(): grads = list(lax.psum(tuple(local), 'batch'))]
    pallas_call x0 -> x1, Pallas kernels: none -> 126 us  [core(): pl.pallas_call(core_kernel, out_shape=(jax.ShapeDtypeStruct((9, 256, 384)...]
    all_gather x2 -> x0, blocking collectives: 96.6 us -> none  [the longest x1 76 us: per_device(): lax.all_gather(results[1][0].astype(jnp.bfloat16), 'chan', axis=4, tiled=...]
    all_gather x3 -> x0, local copies, waits for them, and re-layouts: 81.7 us -> none  [the longest x1 63.3 us: per_device(): complete = lax.all_gather(local_field, 'chan', axis=4, tiled=True)]
    dot_general x17 -> x0, matrix products: 67.6 us -> none  [the longest x7 29.4 us: weight_grad(): lax.dot_general(flat_in, flat_grad, (((0,), (0,)), ((), ())), preferred_e...]
    split x4 -> x0, local copies, waits for them, and re-layouts: 46.7 us -> none  [patches(): return jnp.concatenate(shifted_views(field), axis=-1)]
    unnamed x313 -> x96, local copies, waits for them, and re-layouts: 46.5 us -> 3.81 us
  transfers between devices with their start and end apart: 4 -> 1, of which waited for: 1 -> 0; matrix products, arithmetic and copies ran while one was open for 8% -> 1% of each run, Pallas kernels for 0% -> 0%
where the time goes in v1:
time: 398 us; the launch traced here: 393 us
  Pallas kernels  126 us (32%)
  blocking collectives  126 us (32%)
  local copies, waits for them, and re-layouts  68.5 us (17%)
  other arithmetic  57.4 us (14%)
  between operations  15 us (4%)
    psum x1, blocking collectives, per_device(): grads = list(lax.psum(tuple(local), 'batch'))  126 us
    pallas_call x1, Pallas kernels, core(): pl.pallas_call(core_kernel, out_shape=(jax.ShapeDtypeStruct((9, 256, 384)...  126 us
    unnamed x8, other arithmetic  45.3 us
  transfers between devices with their start and end apart: 1, of which 0 were waited for; matrix products, arithmetic and copies ran while one was open for 1% of the time, Pallas kernels for 0%

profile of v1, /device:TPU:0, one launch (start us, length us, event | category | flops | bytes accessed | tf_op | source)
XLA Modules:
  0.0 392.8 jit_solution(11935613330513223993)
XLA Ops:
  7.3 0.8 slice.126
  8.1 0.7 slice.125
  8.8 0.7 slice.124
  9.5 0.8 slice.127
  10.2 1.3 convert.59
  11.6 0.3 slice_reduce_fusion.3
  11.8 0.9 slice_reduce_fusion.1
  12.7 1.4 copy.68.lab_ref
  14.2 0.6 pad.20.aff_ref
  14.8 0.9 convert_reduce_fusion.3
  15.7 1.2 convert_reduce_fusion.2
  16.8 1.3 convert_reduce_fusion.1
  18.2 0.9 reshape.204
  19.1 0.8 reshape.203
  19.9 0.8 convert_reduce_fusion
  20.7 0.9 reshape.202
  21.6 1.2 reshape.205
  22.8 0.7 slice.119
  23.5 0.8 slice.117
  24.3 0.7 slice.123
  25.1 0.8 slice.121
  25.9 0.4 reduce.5
  26.3 0.2 reshape.207
  26.6 0.5 broadcast.142
  27.1 16.6 %reduce.20 = f32[497664]{0:T(1024)} reduce(f32[1,497664]{1,0:T(1,128)S(1)} %copy-done.1, f32[]{:T(128)} %broadcast.142), dimensions={0}, to_apply=%param.33.reduce_sub_computation.3 | reduce | bytes 3981316 | tf_op args[5]
  43.7 2.6 reshape.206
  46.2 0.5 fusion.1
  46.8 3.1 copy.66
  49.9 4.7 %reshape.208.wc_ref = bf16[9,256,384]{2,1,0:T(8,128)(2,1)S(1)} reshape(bf16[9,4,64,3,128]{4,3,2,1,0:T(4,128)(2,1)} %copy.66) | data formatting | bytes 3538944 | tf_op jit(solution)/shard_map/reshape | solution.py:652
  54.7 2.3 copy.67
  56.9 0.7 fusion.10.r_ref
  57.8 1.2 concatenate.34.w1_ref
  58.9 125.6 %block.1 = (f32[9,256,384]{2,1,0:T(8,128)}, f32[832,256]{1,0:T(8,128)}, f32[256,512]{1,0:T(8,128)}, f32[8,384]{1,0:T(8,128)}, f32[8,128]{1,0:T(8,128)}) custom-call(bf16[1,326144]{1,0:T(2,128)(2,1)} %x_ref.1, s32[8]{0:T(128)} %len_ref.1, s32[8,4]{1,0:T(8,128)} %copy.68.lab_ref, bf16[832,256]{1,0:T(8,128)(2,1)} %concatenate.34.w1_ref, ...), custom_call_target="tpu_custom_call" | custom-call | tf_op jit(solution)/shard_map/block/pallas_call | solution.py:590
  184.6 1.6 slice.136
  186.2 1.6 slice.134
  187.8 1.7 slice.135
  189.5 2.0 slice.133
  191.5 1.8 slice.129
  193.2 1.8 slice.128
  195.0 3.7 reshape.211
  198.7 2.6 slice_bitcast_fusion.1
  201.4 2.7 slice_bitcast_fusion
  204.1 0.8 pad_maximum_fusion
  204.9 2.6 reshape.216
  207.5 1.9 reshape.215
  209.3 2.1 reshape.210
  211.4 2.2 reshape.209
  213.6 1.8 copy.69
  215.4 5.9 %reshape.212 = f32[1,497664]{1,0:T(1,128)} reshape(f32[3,9,4,48,96]{4,3,2,1,0:T(8,128)} %copy.69) | data formatting | bytes 3981312 | tf_op jit(solution)/shard_map/reshape | solution.py:657
  221.4 0.1 copy.70
  221.5 1.0 reshape.214
  222.7 0.2 slice.131
  222.8 0.3 reshape.213
  223.2 126.2 %psum.52 = f32[1,9984]{1,0:T(1,128)S(1)} all-reduce(f32[1,9984]{1,0:T(1,128)S(1)} %reshape.213), channel_id=1, replica_groups=mesh['batch'=32,'chan'=4] {'batch'}, use_global_device_ids=true, to_apply=%region_3.4 | all-reduce | flops 9984 | bytes 79872 | tf_op jit(solution)/shard_map/psum | solution.py:706
  349.4 1.3 fusion.29
  350.8 0.7 multiply_subtract_fusion.7
  351.5 4.2 %convert_dynamic-update-slice_fusion.2 = (bf16[1,797952]{1,0:T(2,128)(2,1)S(1)}, f32[1,79872]{1,0:T(1,128)}, f32[1,79872]{1,0:T(1,128)}, f32[1,79872]{1,0:T(1,128)}) fusion(f32[1,79872]{1,0:T(1,128)S(1)} %copy-done.9, f32[1,79872]{1,0:T(1,128)} %get-tuple-element.42, f32[1,79872]{1,0:T(1,128)S(1)} %copy-done.25, f32[1,79872]{1,0:T(1,128)S(1)} %copy-done.26), kind=kLoop, calls=%fused_computation.24 | loop fusion | flops 1198079 | bytes 2555904
  355.7 2.8 convert_dynamic-update-slice_fusion.4
  358.7 16.9 %convert_dynamic-update-slice_fusion = (bf16[1,797952]{1,0:T(2,128)(2,1)S(1)}, f32[1,497664]{1,0:T(1,128)}, f32[1,497664]{1,0:T(1,128)}, f32[1,497664]{1,0:T(1,128)}) fusion(bf16[1,797952]{1,0:T(2,128)(2,1)S(1)} %get-tuple-element.68, f32[1,497664]{1,0:T(1,128)S(1)} %copy-done.2, f32[1,497664]{1,0:T(1,128)} %get-tuple-element.44, ...), kind=kLoop, calls=%fused_computation.5 | loop fusion | flops 7464960 | bytes 15925248
  375.7 0.9 convert_dynamic-update-slice_fusion.6
  376.6 1.9 convert_dynamic-update-slice_fusion.3
  378.6 1.5 convert_dynamic-update-slice_fusion.5
  380.1 3.8 convert_dynamic-update-slice_fusion.1
  383.9 1.7 copy-done.41
  (103 shorter events, 0.5 us)
Async XLA Ops:
  7.2 12.7 %copy-start.8 = (f32[1,79872]{1,0:T(1,128)S(1)}, f32[1,79872]{1,0:T(1,128)}, u32[]{:S(2)}) copy-start(f32[1,79872]{1,0:T(1,128)} %param.31) | copy-start | bytes 958468
  7.2 344.3 %all-reduce.7.cloned.1.call-start = ((), (), s32[]{:S(2)}) async-start(), calls=%async_computation | async-start | bytes 6303744 | tf_op jit(solution)/shard_map/psum | solution.py:706
  10.2 15.7 %copy-start.16 = (f32[1,41472]{1,0:T(1,128)S(1)}, f32[1,41472]{1,0:T(1,128)}, u32[]{:S(2)}) copy-start(f32[1,41472]{1,0:T(1,128)} %param.35) | copy-start | bytes 497668
  14.2 12.9 %copy-start.1 = (f32[1,497664]{1,0:T(1,128)S(1)}, f32[1,497664]{1,0:T(1,128)}, u32[]{:S(2)}) copy-start(f32[1,497664]{1,0:T(1,128)} %param.33) | copy-start | bytes 5971972
  54.6 3.1 copy-start
  54.6 2.4 copy-start.23
  54.6 2.3 copy-start.24
  54.6 2.3 copy-start.34
  54.6 2.3 copy-start.35
  54.6 3.1 copy-start.11
  54.6 3.1 copy-start.12
  54.6 3.1 copy-start.13
  54.7 3.1 copy-start.14
  184.6 10.5 %copy-start.4 = (f32[9,256,384]{2,1,0:T(8,128)S(1)}, f32[9,256,384]{2,1,0:T(8,128)}, u32[]{:S(2)}) copy-start(f32[9,256,384]{2,1,0:T(8,128)} %get-tuple-element.34) | copy-start | bytes 10616836
  201.3 2.7 copy-start.10
  201.3 2.7 copy-start.15
  201.4 2.7 copy-start.27
  215.4 5.9 %copy-start.3 = (f32[3,9,4,12,32]{4,0,3,2,1:T(4,128)S(1)}, f32[3,9,4,12,32]{4,0,3,2,1:T(4,128)}, u32[]{:S(2)}) copy-start(f32[3,9,4,12,32]{4,0,3,2,1:T(4,128)} %slice_bitcast_fusion.1) | copy-start | bytes 497668
  221.5 1.2 copy-start.5
  222.5 128.1 %copy-start.43 = (f32[8,384]{1,0:T(8,128)S(1)}, f32[8,384]{1,0:T(8,128)}, u32[]{:S(2)}) copy-start(f32[8,384]{1,0:T(8,128)} %get-tuple-element.36) | copy-start | bytes 36868
  222.5 128.2 %copy-start.42 = (f32[2,316]{1,0:T(2,128)S(1)}, f32[2,316]{1,0:T(2,128)}, u32[]{:S(2)}) copy-start(f32[2,316]{1,0:T(2,128)} %param.38) | copy-start | bytes 7588
  222.5 128.2 %copy-start.44 = (f32[2,316]{1,0:T(2,128)S(1)}, f32[2,316]{1,0:T(2,128)}, u32[]{:S(2)}) copy-start(f32[2,316]{1,0:T(2,128)} %param.54) | copy-start | bytes 7588
  222.5 128.2 %copy-start.45 = (f32[2,316]{1,0:T(2,128)S(1)}, f32[2,316]{1,0:T(2,128)}, u32[]{:S(2)}) copy-start(f32[2,316]{1,0:T(2,128)} %param.46) | copy-start | bytes 7588
  222.5 128.2 %copy-start.46 = (f32[2,316]{1,0:T(2,128)S(1)}, f32[2,316]{1,0:T(2,128)}, u32[]{:S(2)}) copy-start(f32[2,316]{1,0:T(2,128)} %param.55) | copy-start | bytes 7588
  222.5 128.9 %copy-start.9 = (f32[1,79872]{1,0:T(1,128)S(1)}, f32[1,79872]{1,0:T(1,128)}, u32[]{:S(2)}) copy-start(f32[1,79872]{1,0:T(1,128)} %param.31) | copy-start | bytes 958468
  222.6 128.9 %copy-start.25 = (f32[1,79872]{1,0:T(1,128)S(1)}, f32[1,79872]{1,0:T(1,128)}, u32[]{:S(2)}) copy-start(f32[1,79872]{1,0:T(1,128)} %param.47) | copy-start | bytes 958468
  222.6 128.9 %copy-start.26 = (f32[1,79872]{1,0:T(1,128)S(1)}, f32[1,79872]{1,0:T(1,128)}, u32[]{:S(2)}) copy-start(f32[1,79872]{1,0:T(1,128)} %param.39) | copy-start | bytes 958468
  222.6 133.1 %copy-start.18 = (f32[1,39936]{1,0:T(1,128)S(1)}, f32[1,39936]{1,0:T(1,128)}, u32[]{:S(2)}) copy-start(f32[1,39936]{1,0:T(1,128)} %param.32) | copy-start | bytes 479236
  222.6 133.1 %copy-start.31 = (f32[1,39936]{1,0:T(1,128)S(1)}, f32[1,39936]{1,0:T(1,128)}, u32[]{:S(2)}) copy-start(f32[1,39936]{1,0:T(1,128)} %param.48) | copy-start | bytes 479236
  222.6 133.1 %copy-start.32 = (f32[1,39936]{1,0:T(1,128)S(1)}, f32[1,39936]{1,0:T(1,128)}, u32[]{:S(2)}) copy-start(f32[1,39936]{1,0:T(1,128)} %param.40) | copy-start | bytes 479236
  223.2 135.4 %copy-start.2 = (f32[1,497664]{1,0:T(1,128)S(1)}, f32[1,497664]{1,0:T(1,128)}, u32[]{:S(2)}) copy-start(f32[1,497664]{1,0:T(1,128)} %param.33) | copy-start | bytes 5971972
  351.5 7.1 %copy-start.6 = (f32[1,497664]{1,0:T(1,128)S(1)}, f32[1,497664]{1,0:T(1,128)}, u32[]{:S(2)}) copy-start(f32[1,497664]{1,0:T(1,128)} %param.49) | copy-start | bytes 5971972
  358.5 17.1 %copy-start.33 = (f32[1,9984]{1,0:T(1,128)S(1)}, f32[1,9984]{1,0:T(1,128)}, u32[]{:S(2)}) copy-start(f32[1,9984]{1,0:T(1,128)} %param.34) | copy-start | bytes 119812
  358.6 17.1 %copy-start.39 = (f32[1,9984]{1,0:T(1,128)S(1)}, f32[1,9984]{1,0:T(1,128)}, u32[]{:S(2)}) copy-start(f32[1,9984]{1,0:T(1,128)} %param.50) | copy-start | bytes 119812
  358.6 17.1 %copy-start.40 = (f32[1,9984]{1,0:T(1,128)S(1)}, f32[1,9984]{1,0:T(1,128)}, u32[]{:S(2)}) copy-start(f32[1,9984]{1,0:T(1,128)} %param.42) | copy-start | bytes 119812
  358.6 18.0 %copy-start.17 = (f32[1,41472]{1,0:T(1,128)S(1)}, f32[1,41472]{1,0:T(1,128)}, u32[]{:S(2)}) copy-start(f32[1,41472]{1,0:T(1,128)} %param.35) | copy-start | bytes 497668
  358.6 18.0 %copy-start.28 = (f32[1,41472]{1,0:T(1,128)S(1)}, f32[1,41472]{1,0:T(1,128)}, u32[]{:S(2)}) copy-start(f32[1,41472]{1,0:T(1,128)} %param.51) | copy-start | bytes 497668
  358.6 18.0 %copy-start.29 = (f32[1,41472]{1,0:T(1,128)S(1)}, f32[1,41472]{1,0:T(1,128)}, u32[]{:S(2)}) copy-start(f32[1,41472]{1,0:T(1,128)} %param.43) | copy-start | bytes 497668
  358.6 18.0 %copy-start.30 = (f32[1,41472]{1,0:T(1,128)S(1)}, f32[1,41472]{1,0:T(1,128)}, u32[]{:S(2)}) copy-start(f32[1,41472]{1,0:T(1,128)} %get-tuple-element.45) | copy-start | bytes 497668
  358.6 19.9 %copy-start.19 = (f32[1,26624]{1,0:T(1,128)S(1)}, f32[1,26624]{1,0:T(1,128)}, u32[]{:S(2)}) copy-start(f32[1,26624]{1,0:T(1,128)} %param.36) | copy-start | bytes 319492
  358.6 19.9 %copy-start.36 = (f32[1,26624]{1,0:T(1,128)S(1)}, f32[1,26624]{1,0:T(1,128)}, u32[]{:S(2)}) copy-start(f32[1,26624]{1,0:T(1,128)} %param.52) | copy-start | bytes 319492
  358.6 19.9 %copy-start.37 = (f32[1,26624]{1,0:T(1,128)S(1)}, f32[1,26624]{1,0:T(1,128)}, u32[]{:S(2)}) copy-start(f32[1,26624]{1,0:T(1,128)} %param.44) | copy-start | bytes 319492
  358.7 19.9 %copy-start.38 = (f32[1,26624]{1,0:T(1,128)S(1)}, f32[1,26624]{1,0:T(1,128)}, u32[]{:S(2)}) copy-start(f32[1,26624]{1,0:T(1,128)} %get-tuple-element.46) | copy-start | bytes 319492
  375.6 4.4 %copy-start.7 = (f32[1,102400]{1,0:T(1,128)S(1)}, f32[1,102400]{1,0:T(1,128)}, u32[]{:S(2)}) copy-start(f32[1,102400]{1,0:T(1,128)} %param.37) | copy-start | bytes 1228804
  375.6 4.4 %copy-start.20 = (f32[1,102400]{1,0:T(1,128)S(1)}, f32[1,102400]{1,0:T(1,128)}, u32[]{:S(2)}) copy-start(f32[1,102400]{1,0:T(1,128)} %param.53) | copy-start | bytes 1228804
  375.6 4.4 %copy-start.21 = (f32[1,102400]{1,0:T(1,128)S(1)}, f32[1,102400]{1,0:T(1,128)}, u32[]{:S(2)}) copy-start(f32[1,102400]{1,0:T(1,128)} %param.45) | copy-start | bytes 1228804
  375.6 4.4 %copy-start.22 = (f32[1,102400]{1,0:T(1,128)S(1)}, f32[1,102400]{1,0:T(1,128)}, u32[]{:S(2)}) copy-start(f32[1,102400]{1,0:T(1,128)} %get-tuple-element.47) | copy-start | bytes 1228804
  383.9 1.7 copy-start.41
Sparse Core Ops, SparseCore 0:
  222.7 108.3 all-reduce.6

commit v2 on v1

--- a/solution.py
+++ b/solution.py
@@ -28,6 +28,17 @@
 CB = CIN // NC
 GW = 8 * CB
 HALF = 25
+TAPS = 27
+FLAT = {"direct": 624, "squeeze": 312, "spatial": 3888, "shrink": 78, "volume": 324, "pooled": 208,
+        "readout": 800}
+NAMES = ("direct", "squeeze", "spatial", "shrink", "volume", "pooled", "readout")
+BULK = {"spatial": 0, "volume": 3888, "direct": 4224, "pooled": 4848, "readout": 5056}
+LATE = {"squeeze": 0, "shrink": 312}
+CORE_ROWS = 3072
+GROUP_ROWS = 1536
+FIRST_ROWS = 384
+LAST_ROWS = 96
+LATE_ROWS = 16
 
 EPS = 1e-05
 BETA_ONE = 0.5
@@ -115,6 +126,135 @@
     lax.fori_loop(1, NB, two, 0)
 
 
+def digit_of(me, stride, size):
+    return lax.rem(me // stride, size)
+
+
+def digit_peer(me, stride, size, d):
+    digit = digit_of(me, stride, size)
+    return {"batch": me + stride * (lax.rem(digit + d, size) - digit)}
+
+
+def piece(tiles, start, width, dest, lane):
+    tile, off = divmod(start, 128)
+    v = tiles[tile]
+    if off + width > 128:
+        v = jnp.where(lane >= off, v, tiles[tile + 1])
+    shift = (dest - off) % 128
+    return pltpu.roll(v, shift, 1) if shift else v
+
+
+def joined(parts, lane, count):
+    out = []
+    moved = []
+    for value, src, start, width in parts:
+        shift = (start - src) % 128
+        moved.append((pltpu.roll(value, shift, 1) if shift else value, start, width))
+    for i in range(count):
+        acc = None
+        for value, start, width in moved:
+            lo, hi = max(0, start - 128 * i), min(128, start + width - 128 * i)
+            if lo < hi:
+                acc = value if acc is None else jnp.where(lane >= lo, value, acc)
+        out.append(acc)
+    return out
+
+
+def lanes_of(v):
+    return lax.broadcasted_iota(jnp.int32, v, 1)
+
+
+def prepare_w1(flat, wn, wk, w1s):
+    lane = lanes_of((208, 128))
+    tiles = [flat["direct"][pl.ds(i, 208, stride=3), :] for i in range(3)]
+    pool = flat["pooled"][...]
+    for j in range(4):
+        v = jnp.where(
+            lane < 96, piece(tiles, 96 * j, 96, 0, lane), piece([pool], 32 * j, 32, 96, lane)
+        )
+        wn[0, pl.ds(j, 208, stride=4), :] = v
+    lane = lanes_of((104, 128))
+    tiles = [flat["squeeze"][pl.ds(i, 104, stride=3), :] for i in range(3)]
+    for j in range(8):
+        wn[1, pl.ds(j, 104, stride=8), :] = piece(tiles, 48 * j, 48, 0, lane)
+    lane = lanes_of((26, 128))
+    tiles = [flat["shrink"][pl.ds(i, 26, stride=3), :] for i in range(3)]
+    for j in range(32):
+        wk[pl.ds(j, 26, stride=32), :] = piece(tiles, 12 * j, 12, 48, lane)
+    lane = lanes_of((CB, 128))
+    for k in range(NC):
+        rows = slice(k * CB, (k + 1) * CB)
+        second = jnp.where(lane < 48, wn[1, rows, :], jnp.where(lane < 60, wk[rows, :], 0.0))
+        both = jnp.concatenate([wn[0, rows, :], second], axis=1).astype(BF16)
+        for r in range(8):
+            _, off, _ = window_of(r)
+            w1s[r, k, off : off + CB, :] = both
+
+
+def prepare_conv(flat, tb, vn, wc, wct):
+    lane = lanes_of((324, 128))
+    for j in range(4):
+        v = piece([flat["volume"][...]], 32 * j, 32, 96, lane)
+        vn[pl.ds(j, 324, stride=4), :] = jnp.where(lane >= 96, v, 0.0)
+    vn[pl.ds(1296, 8), :] = jnp.zeros((8, 128), F32)
+    lane48 = lanes_of((48, 128))
+    row16 = lax.broadcasted_iota(jnp.int32, (16, 128), 0)
+
+    def one(q, carry):
+        for dt in range(3):
+            tap = dt * 9 + q
+            tiles = [
+                flat["spatial"][pl.ds(tap * 144 + i, 48, stride=3), :] for i in range(3)
+            ]
+            for j in range(4):
+                v = piece(tiles, 96 * j, 96, 0, lane48)
+                tb[pl.ds(j, 48, stride=4), :] = jnp.where(lane48 < 96, v, 0.0)
+            for j in range(NC):
+                at = slice(128 * dt, 128 * dt + 128)
+                wc[q, 64 * j : 64 * j + 48, at] = tb[48 * j : 48 * j + 48, :].astype(BF16)
+                v = vn[pl.ds(tap * 48 + 12 * j, 16), :]
+                wc[q, 64 * j + 48 : 64 * j + 64, at] = jnp.where(row16 < 12, v, 0.0).astype(BF16)
+        wct[q] = jnp.transpose(wc[q])
+        return carry
+
+    lax.fori_loop(0, 9, one, 0)
+
+
+def prepare_readout(flat, rn, rp):
+    lane = lanes_of((32, 128))
+    tiles = [flat["readout"][pl.ds(i, 32, stride=25), :] for i in range(25)]
+    for t in range(4):
+        width = min(128, CLASSES - 128 * t)
+        for j in range(8):
+            v = piece(tiles, CLASSES * j + 128 * t, width, 0, lane)
+            rn[t, pl.ds(j, 32, stride=8), :] = v if width == 128 else jnp.where(lane < width, v, 0.0)
+        at = slice(128 * t, 128 * t + 128)
+        for dst, src, count in ((0, 0, 96), (96, 224, 32), (128, 96, 96), (224, 192, 32)):
+            rp[dst : dst + count, at] = rn[t, src : src + count, :].astype(BF16)
+
+
+def prepare_affine(aff, out):
+    a = [aff[:, 0:128], aff[:, 128:256]]
+    a.append(jnp.concatenate([aff[:, 256:316], jnp.zeros((2, 68), F32)], axis=1))
+    lane = lanes_of((2, 128))
+    t0 = jnp.where(lane < 96, a[0], piece(a, 156, 32, 96, lane))
+    t1 = jnp.where(lane < 60, piece(a, 96, 60, 0, lane), 0.0)
+    t2 = piece(a, 188, 128, 0, lane)
+    for i, t in enumerate((t0, t1, t2)):
+        out[0:2, 128 * i : 128 * i + 128] = t
+
+
+def flatten_96(src, rows, put):
+    lane = lanes_of((rows, 128))
+    for i, v in enumerate(joined([(src(j), 0, 96 * j, 96) for j in range(4)], lane, 3)):
+        put(i, v)
+
+
+def flatten_32(src, rows):
+    lane = lanes_of((rows, 128))
+    return joined([(src(j), 96, 32 * j, 32) for j in range(4)], lane, 1)[0]
+
+
 def total_of(buf, count):
     acc = buf[0]
     for slot in range(1, count):
@@ -123,18 +263,45 @@
 
 
 def core_kernel(
-    x_ref, len_ref, lab_ref, w1_ref, wc_ref, wct_ref, r_ref, aff_ref,
-    gwc_ref, gw1_ref, gr_ref, st_ref, sc_ref,
+    x_hbm, len_ref, lab_ref, direct_hbm, squeeze_hbm, spatial_hbm, shrink_hbm, volume_hbm,
+    pooled_hbm, readout_hbm, affine_ref,
+    gb_ref, late_ref, st_ref, sc_ref,
+    x_ref, f_direct, f_squeeze, f_spatial, f_shrink, f_volume, f_pooled, f_readout,
+    wn, wk, tb, vn, rn, wc_ref, wct_ref, r_ref, aff_ref,
     xf, xg, w1s, ynat, ypos, box, ob, msg, got, apad, acol, at, y2, dpre, dypad, dm, dgot, dnat,
+    gw1_ref, gq, gr, g, gcore, r1, r2, lsend, lgot,
     lbuf, sbuf_a, sbuf_b, sbuf_c, sbuf_d,
-    xs, xr, ms, mr, ls, lr, ds_, dr,
-    as_, ar, bs, br, cs, cr, es, er,
+    xin, win, xs, xr, ms, mr, ls, lr, ds_, dr,
+    as_, ar, bs, br, cs, cr, es, er, fs, fr, hs, hr,
+    co_s, co_r, s1s, s1r, s2s, s2r, g1s, g1r, g2s, g2r, g3s, g3r,
 ):
     me_b = lax.axis_index("batch")
     me = lax.axis_index("chan")
 
     barrier = pltpu.get_barrier_semaphore()
 
+    cuts = [0, 79 * 1024, 158 * 1024, 237 * 1024, 326144]
+    x_in = []
+    for i in range(4):
+        at_ = pl.ds(cuts[i], cuts[i + 1] - cuts[i])
+        c = pltpu.make_async_copy(x_hbm.at[:, at_], x_ref.at[:, at_], xin.at[i])
+        c.start()
+        x_in.append(c)
+    flat = dict(
+        direct=f_direct, squeeze=f_squeeze, spatial=f_spatial, shrink=f_shrink, volume=f_volume,
+        pooled=f_pooled, readout=f_readout,
+    )
+    w_in = []
+    for i, (src, name) in enumerate(
+        zip(
+            (direct_hbm, squeeze_hbm, spatial_hbm, shrink_hbm, volume_hbm, pooled_hbm, readout_hbm),
+            NAMES,
+        )
+    ):
+        c = pltpu.make_async_copy(src, flat[name], win.at[i])
+        c.start()
+        w_in.append(c)
+
     def greet(d, carry):
         pl.semaphore_signal(barrier, inc=1, device_id=batch_peer(me_b, d), device_id_type=MESH)
         return carry
@@ -148,7 +315,10 @@
         xf[pl.ds(pl.multiple_of(i * 8, 8), 8), :] = v.reshape(8, 128)
         return carry
 
-    lax.fori_loop(0, 318, flat_rows, 0, unroll=6)
+    for i in range(4):
+        x_in[i].wait()
+        first = 79 * i
+        lax.fori_loop(first, first + 79 if i < 3 else 318, flat_rows, 0, unroll=4)
     xf[pl.ds(2544, 4), :] = x_ref[:, 318 * 1024 : 318 * 1024 + 512].astype(F32).reshape(4, 128)
     xf[pl.ds(2548, 2704 - 2548), :] = jnp.zeros((2704 - 2548, 128), F32)
     for i in range(13):
@@ -195,10 +365,11 @@
         return carry
 
     lax.fori_loop(0, 8, zero_w, 0)
-    for r in range(8):
-        _, off, _ = window_of(r)
-        for k in range(NC):
-            w1s[r, k, off : off + CB, :] = w1_ref[k * CB : (k + 1) * CB, :]
+    for c in w_in:
+        c.wait()
+    prepare_w1(flat, wn, wk, w1s)
+    prepare_affine(affine_ref, aff_ref)
+    prepare_readout(flat, rn, r_ref)
 
     def zero_pad(i, carry):
         apad[i] = jnp.zeros((ROWS, 256), BF16)
@@ -208,6 +379,7 @@
 
     lax.fori_loop(0, 81, zero_pad, 0)
     dnat[...] = jnp.zeros_like(dnat)
+    prepare_conv(flat, tb, vn, wc_ref, wct_ref)
 
     hops[0].wait_recv()
     f0 = send_to(part(left_i, True), part(left_i, True), xs.at[4], xr.at[4], right)
@@ -426,7 +598,20 @@
     loss_row = jnp.broadcast_to(jnp.sum(loss_rows, axis=0, keepdims=True), (1, 128))
     sbuf_c[me_b] = pack_rows([col(g0), col(b0), col(g2), col(b2), loss_row])
     share_start(sbuf_c, me_b, cs, cr)
-    gr_ref[...] = dot_t(feature, dlog, 0, 0)
+    grr = dot_t(feature, dlog, 0, 0)
+    for t in range(4):
+        for dst, src, count in ((0, 0, 96), (96, 224, 32), (128, 96, 96), (224, 192, 32)):
+            gr[t, src : src + count, :] = grr[dst : dst + count, 128 * t : 128 * t + 128]
+    lane32 = lanes_of((32, 128))
+    parts = []
+    for j in range(8):
+        for t in range(4):
+            parts.append(
+                (gr[t, pl.ds(j, 32, stride=8), :], 0, CLASSES * j + 128 * t,
+                 min(128, CLASSES - 128 * t))
+            )
+    for i, v in enumerate(joined(parts, lane32, 25)):
+        g[pl.ds(BULK["readout"] + i, 32, stride=25), :] = v
     for c in ls_c:
         c.wait_send()
     for c in ms_c:
@@ -491,10 +676,25 @@
             ],
             axis=0,
         )
-        gwc_ref[q] = dot(at[...], rhs)
+        res = dot(at[...], rhs)
+        for dt in range(3):
+            tap = dt * 9 + q
+            for j in range(NC):
+                gq[48 * j : 48 * j + 48, :] = res[64 * j : 64 * j + 48, 128 * dt : 128 * dt + 128]
+                vn[pl.ds(tap * 48 + 12 * j, 12), :] = res[
+                    64 * j + 48 : 64 * j + 60, 128 * dt : 128 * dt + 128
+                ]
+
+            def put(i, v, tap=tap):
+                g[pl.ds(BULK["spatial"] + tap * 144 + i, 48, stride=3), :] = v
+
+            flatten_96(lambda j: gq[pl.ds(j, 48, stride=4), :], 48, put)
         return carry
 
     lax.fori_loop(0, 9, grad_conv, 0)
+    g[BULK["volume"] : BULK["volume"] + 324, :] = flatten_32(
+        lambda j: vn[pl.ds(j, 324, stride=4), :], 324
+    )
 
     def dy0_at(p, carry):
         v = finish(ypos[p][:, 0:128], n0, dpre[p][:, 0:128], totc[0:1], totc[1:2])
@@ -520,7 +720,7 @@
     lax.fori_loop(0, POS, dy0_nat, 0)
 
     for tile in range(2):
-        gw1_ref[:, 128 * tile : 128 * tile + 128] = jnp.zeros((CIN, 128), F32)
+        gw1_ref[tile] = jnp.zeros((CIN, 128), F32)
 
     def grad_one(r, width, fold):
         first, off, lanes = window_of(r)
@@ -530,12 +730,27 @@
         for k in range(NC):
             res = dot_t(xg[k, :, first : first + lanes], rhs, 0, 0)[off : off + CB]
             if fold:
-                gw1_ref[k * CB : (k + 1) * CB, 0:128] += res[:, 0:128] + res[:, 128:256]
+                gw1_ref[0, k * CB : (k + 1) * CB, :] += res[:, 0:128] + res[:, 128:256]
             else:
-                gw1_ref[k * CB : (k + 1) * CB, 128:256] += res
+                gw1_ref[1, k * CB : (k + 1) * CB, :] += res
 
     for r in range(8):
         grad_one(r, 256, True)
+
+    def put_direct(i, v):
+        g[pl.ds(BULK["direct"] + i, 208, stride=3), :] = v
+
+    flatten_96(lambda j: gw1_ref[0, pl.ds(j, 208, stride=4), :], 208, put_direct)
+    g[BULK["pooled"] : BULK["pooled"] + 208, :] = flatten_32(
+        lambda j: gw1_ref[0, pl.ds(j, 208, stride=4), :], 208
+    )
+
+    core_i = lax.rem(me_b, 2)
+    mate = digit_peer(me_b, 1, 2, 1)
+    half_at = pl.multiple_of(core_i * CORE_ROWS, CORE_ROWS)
+    mate_at = pl.multiple_of((1 - core_i) * CORE_ROWS, CORE_ROWS)
+    core_c = send_to(g.at[pl.ds(mate_at, CORE_ROWS)], gcore, co_s, co_r, mate)
+    core_c.start()
 
     for c in ds_c:
         c.wait_recv()
@@ -561,6 +776,34 @@
     share_start(sbuf_d, me_b, es, er)
     for c in ds_c:
         c.wait_send()
+
+    along = ((2, 8), (8, 2))
+    firsts = [digit_of(me_b, along[i][0], 4) for i in range(2)]
+    seconds = [digit_of(me_b, along[i][1], 4) for i in range(2)]
+    core_c.wait()
+
+    def add_core(i, carry):
+        at_ = pl.multiple_of(i * 96, 96)
+        gcore[pl.ds(at_, 96), :] = gcore[pl.ds(at_, 96), :] + g[
+            pl.ds(pl.multiple_of(half_at + at_, 96), 96), :
+        ]
+        return carry
+
+    lax.fori_loop(0, CORE_ROWS // 96, add_core, 0)
+
+    def first_at(i, digit):
+        return pl.ds(pl.multiple_of(i * GROUP_ROWS + digit * FIRST_ROWS, FIRST_ROWS), FIRST_ROWS)
+
+    one_c = []
+    for i in range(2):
+        for d in range(1, 4):
+            c = send_to(
+                gcore.at[first_at(i, lax.rem(firsts[i] + d, 4))], r1.at[i, firsts[i]],
+                s1s.at[i, d], s1r.at[i, d], digit_peer(me_b, along[i][0], 4, d),
+            )
+            c.start()
+            one_c.append(c)
+        r1[i, firsts[i]] = gcore[first_at(i, firsts[i]), :]
     share_wait(sbuf_d, me_b, es, er)
     totd = total_of(sbuf_d, NB)
 
@@ -572,6 +815,93 @@
     lax.fori_loop(0, POS, dy1_nat, 0)
     for r in range(8):
         grad_one(r, 128, False)
+
+    lane104, lane26 = lanes_of((104, 128)), lanes_of((26, 128))
+    lsend[pl.ds(384, 128), :] = jnp.zeros((128, 128), F32)
+    parts = [(gw1_ref[1, pl.ds(j, 104, stride=8), :], 0, 48 * j, 48) for j in range(8)]
+    for i, v in enumerate(joined(parts, lane104, 3)):
+        lsend[pl.ds(LATE["squeeze"] + i, 104, stride=3), :] = v
+    parts = [(gw1_ref[1, pl.ds(j, 26, stride=32), :], 48, 12 * j, 12) for j in range(32)]
+    for i, v in enumerate(joined(parts, lane26, 3)):
+        lsend[pl.ds(LATE["shrink"] + i, 26, stride=3), :] = v
+
+    def late_at(i):
+        return pl.ds(pl.multiple_of(i * LATE_ROWS, LATE_ROWS), LATE_ROWS)
+
+    def late_copy(d):
+        to = lax.rem(me_b + d, NB)
+        return send_to(
+            lsend.at[late_at(to)], lgot.at[me_b], fs.at[d], fr.at[d], batch_peer(me_b, d)
+        )
+
+    def late_start(d, carry):
+        late_copy(d).start()
+        return carry
+
+    def late_wait(d, carry):
+        late_copy(d).wait()
+        return carry
+
+    lax.fori_loop(1, NB, late_start, 0)
+    lgot[me_b] = lsend[late_at(me_b), :]
+
+    for c in one_c:
+        c.wait()
+    two_c = []
+    for i in range(2):
+        r1[i, 0] = total_of(r1.at[i], 4)
+        for d in range(1, 4):
+            to = lax.rem(seconds[i] + d, 4)
+            c = send_to(
+                r1.at[i, 0, pl.ds(pl.multiple_of(to * LAST_ROWS, LAST_ROWS), LAST_ROWS)],
+                r2.at[i, seconds[i]], s2s.at[i, d], s2r.at[i, d],
+                digit_peer(me_b, along[i][1], 4, d),
+            )
+            c.start()
+            two_c.append(c)
+        r2[i, seconds[i]] = r1[
+            i, 0, pl.ds(pl.multiple_of(seconds[i] * LAST_ROWS, LAST_ROWS), LAST_ROWS), :
+        ]
+    for c in two_c:
+        c.wait()
+
+    all_c = []
+    for i in range(2):
+        at_ = pl.ds(
+            pl.multiple_of(
+                half_at + i * GROUP_ROWS + firsts[i] * FIRST_ROWS + seconds[i] * LAST_ROWS,
+                LAST_ROWS,
+            ),
+            LAST_ROWS,
+        )
+        gb_ref[at_, :] = total_of(r2.at[i], 4)
+        for d in range(1, 4):
+            c = send_to(
+                gb_ref.at[at_], gb_ref.at[at_], g1s.at[i, d], g1r.at[i, d],
+                digit_peer(me_b, along[i][1], 4, d),
+            )
+            c.start()
+            all_c.append(c)
+
+    lax.fori_loop(1, NB, late_wait, 0)
+    late_ref[me_b] = total_of(lgot, NB)
+    share_start(late_ref, me_b, hs, hr)
+
+    for c in all_c:
+        c.wait()
+    more_c = []
+    for i in range(2):
+        at_ = pl.ds(
+            pl.multiple_of(half_at + i * GROUP_ROWS + firsts[i] * FIRST_ROWS, FIRST_ROWS),
+            FIRST_ROWS,
+        )
+        for d in range(1, 4):
+            c = send_to(
+                gb_ref.at[at_], gb_ref.at[at_], g2s.at[i, d], g2r.at[i, d],
+                digit_peer(me_b, along[i][0], 4, d),
+            )
+            c.start()
+            more_c.append(c)
 
     fix = voxels / (voxels - 1.0)
     for tile, n, gg, gb in (
@@ -582,81 +912,196 @@
         st_ref[:, 128 * tile : 128 * tile + 128] = pack_rows([gg, gb, n[0], n[1] * fix])
     sc_ref[...] = pack_rows([totc[4:5], counted])
 
-
-def core(x, lengths, labels, w1, wc, wct, r, aff):
+    for c in more_c:
+        c.wait()
+    last_c = send_to(
+        gb_ref.at[pl.ds(half_at, CORE_ROWS)], gb_ref.at[pl.ds(half_at, CORE_ROWS)], g3s, g3r, mate
+    )
+    last_c.start()
+    share_wait(late_ref, me_b, hs, hr)
+    last_c.wait()
+
+
+def core(x, lengths, labels, weights, affine):
     vm = pl.BlockSpec(memory_space=pltpu.VMEM)
     sm = pl.BlockSpec(memory_space=pltpu.SMEM)
+    hbm = pl.BlockSpec(memory_space=pl.ANY)
     dma = pltpu.SemaphoreType.DMA
+    vmem = pltpu.VMEM
     return pl.pallas_call(
         core_kernel,
         out_shape=(
-            jax.ShapeDtypeStruct((9, 256, 384), F32),
-            jax.ShapeDtypeStruct((CIN, 256), F32),
-            jax.ShapeDtypeStruct((256, 512), F32),
+            jax.ShapeDtypeStruct((2 * CORE_ROWS, 128), F32),
+            jax.ShapeDtypeStruct((NB, LATE_ROWS, 128), F32),
             jax.ShapeDtypeStruct((8, 384), F32),
             jax.ShapeDtypeStruct((8, 128), F32),
         ),
-        in_specs=[vm, sm, sm, vm, vm, vm, vm, vm],
-        out_specs=(vm,) * 5,
+        in_specs=[hbm, sm, sm] + [hbm] * 7 + [vm],
+        out_specs=(vm,) * 4,
         scratch_shapes=[
-            pltpu.VMEM((13 * GPAD, 128), F32),
-            pltpu.VMEM((NC, GPAD, GW), BF16),
-            pltpu.VMEM((8, NC, 384, 256), BF16),
-            pltpu.VMEM((2, 8 * GPAD, 128), F32),
-            pltpu.VMEM((POS, ROWS, 256), F32),
-            pltpu.VMEM((81, ROWS, 128), F32),
-            pltpu.VMEM((POS + 1, ROWS, 128), F32),
-            pltpu.VMEM((HALF, ROWS, 128), BF16),
-            pltpu.VMEM((NC, HALF, ROWS, 128), BF16),
-            pltpu.VMEM((81, ROWS, 256), BF16),
-            pltpu.VMEM((POS, ROWS, 256), BF16),
-            pltpu.VMEM((256, VOX), BF16),
-            pltpu.VMEM((POS, ROWS, 128), F32),
-            pltpu.VMEM((POS, ROWS, 256), F32),
-            pltpu.VMEM((81, ROWS, 384), BF16),
-            pltpu.VMEM((NC, HALF, ROWS, 128), F32),
-            pltpu.VMEM((NC, HALF, ROWS, 128), F32),
-            pltpu.VMEM((2, 8 * GPAD, 128), F32),
-            pltpu.VMEM((NC, ROWS, 512), F32),
-            pltpu.VMEM((NB, 8, 128), F32),
-            pltpu.VMEM((NB, 8, 128), F32),
-            pltpu.VMEM((NB, 8, 128), F32),
-            pltpu.VMEM((NB, 8, 128), F32),
-            dma((6,)), dma((6,)), dma((NC,)), dma((NC,)), dma((NC,)), dma((NC,)), dma((NC,)),
-            dma((NC,)),
-            dma((NB,)), dma((NB,)), dma((NB,)), dma((NB,)), dma((NB,)), dma((NB,)), dma((NB,)),
-            dma((NB,)),
+            vmem((1, 326144), BF16),
+            *[vmem((FLAT[n], 128), F32) for n in NAMES],
+            vmem((2, CIN, 128), F32),
+            vmem((CIN, 128), F32),
+            vmem((R1, 128), F32),
+            vmem((1304, 128), F32),
+            vmem((4, 256, 128), F32),
+            vmem((9, 256, 384), BF16),
+            vmem((9, 384, 256), BF16),
+            vmem((256, 512), BF16),
+            vmem((8, 384), F32),
+            vmem((13 * GPAD, 128), F32),
+            vmem((NC, GPAD, GW), BF16),
+            vmem((8, NC, 384, 256), BF16),
+            vmem((2, 8 * GPAD, 128), F32),
+            vmem((POS, ROWS, 256), F32),
+            vmem((81, ROWS, 128), F32),
+            vmem((POS + 1, ROWS, 128), F32),
+            vmem((HALF, ROWS, 128), BF16),
+            vmem((NC, HALF, ROWS, 128), BF16),
+            vmem((81, ROWS, 256), BF16),
+            vmem((POS, ROWS, 256), BF16),
+            vmem((256, VOX), BF16),
+            vmem((POS, ROWS, 128), F32),
+            vmem((POS, ROWS, 256), F32),
+            vmem((81, ROWS, 384), BF16),
+            vmem((NC, HALF, ROWS, 128), F32),
+            vmem((NC, HALF, ROWS, 128), F32),
+            vmem((2, 8 * GPAD, 128), F32),
+            vmem((2, CIN, 128), F32),
+            vmem((R1, 128), F32),
+            vmem((4, 256, 128), F32),
+            vmem((2 * CORE_ROWS, 128), F32),
+            vmem((CORE_ROWS, 128), F32),
+            vmem((2, 4, FIRST_ROWS, 128), F32),
+            vmem((2, 4, LAST_ROWS, 128), F32),
+            vmem((NB * LATE_ROWS, 128), F32),
+            vmem((NB, LATE_ROWS, 128), F32),
+            vmem((NC, ROWS, 512), F32),
+            *[vmem((NB, 8, 128), F32)] * 4,
+            dma((4,)), dma((7,)), dma((6,)), dma((6,)),
+            *[dma((NC,))] * 6,
+            *[dma((NB,))] * 12,
+            dma, dma,
+            *[dma((2, 4))] * 8,
+            dma, dma,
         ],
         compiler_params=pltpu.CompilerParams(
             collective_id=0, has_side_effects=True, vmem_limit_bytes=58 << 20
         ),
         name="block",
-    )(x, lengths, labels, w1, wc, wct, r, aff)
-
-
-def split_columns(packed, widths):
-    pieces = []
-    offset = 0
-    for channels in widths:
-        pieces.append(packed[..., offset : offset + channels])
-        offset = offset + channels
-    return pieces
-
-
-def conv_weights(spatial, volume):
-    sp = spatial.reshape(3, 9, NC, 48, 96)
-    vo = volume.reshape(3, 9, NC, 12, 32)
-    sp = jnp.pad(sp, ((0, 0), (0, 0), (0, 0), (0, 16), (0, 32)))
-    vo = jnp.pad(vo, ((0, 0), (0, 0), (0, 0), (48, 4), (96, 0)))
-    both = (sp + vo).astype(BF16)
-    return jnp.transpose(both, (1, 2, 3, 0, 4)).reshape(9, 256, 384)
-
-
-def conv_grads(g):
-    g = g.reshape(9, NC, 64, 3, 128)
-    sp = jnp.transpose(g[:, :, 0:48, :, 0:96], (3, 0, 1, 2, 4)).reshape(1, -1)
-    vo = jnp.transpose(g[:, :, 48:60, :, 96:128], (3, 0, 1, 2, 4)).reshape(1, -1)
-    return sp, vo
+    )(x, lengths, labels, *weights, affine)
+
+
+def unlanes(tiles):
+    t0, t1, t2 = tiles
+    lane = lanes_of(t0.shape)
+    parts = [(t0, 0, 0, 96), (t1, 0, 96, 60), (t0, 96, 156, 32), (t2, 0, 188, 128)]
+    return joined(parts, lane, 3)
+
+
+def adam_kernel(*refs):
+    gb, late, st, sc, running = refs[0:5]
+    w_in, m_in, v_in = refs[5:13], refs[13:21], refs[21:29]
+    m_out, v_out, w_out = refs[29:37], refs[37:45], refs[45:53]
+    run_out, loss_out, count_out, copies_out = refs[53:57]
+    wb, mb, vb = refs[57:64], refs[64:71], refs[71:78]
+    cb, insem, outsem, csem = refs[78:82]
+    rates = step_rates()
+    order = (2, 6, 0, 1, 4, 5, 3)
+    ins = {}
+    for i in order:
+        for kind, (src, dst) in enumerate(((w_in[i], wb[i]), (m_in[i], mb[i]), (v_in[i], vb[i]))):
+            c = pltpu.make_async_copy(src, dst, insem.at[i, kind])
+            c.start()
+            ins[i, kind] = c
+
+    starts = []
+    total = 0
+    for name in NAMES:
+        starts.append(total * 128)
+        total += FLAT[name]
+    outs = []
+    for i in order:
+        name = NAMES[i]
+        rows = FLAT[name]
+        for kind in range(3):
+            ins[i, kind].wait()
+        bulk = name in BULK
+
+        def step(at, count, i=i, name=name, bulk=bulk):
+            if bulk:
+                grad = gb[pl.ds(BULK[name] + at, count), :]
+            else:
+                grad = late[pl.ds(LATE[name] + at, count), :]
+            rows_ = pl.ds(at, count)
+            m, v, w = adamw(wb[i][rows_, :], mb[i][rows_, :], vb[i][rows_, :], grad, rates[i])
+            mb[i][rows_, :] = m
+            vb[i][rows_, :] = v
+            wb[i][rows_, :] = w
+            cb[:, pl.ds(pl.multiple_of(starts[i] + at * 128, 128), count * 128)] = w.reshape(
+                1, count * 128
+            ).astype(BF16)
+
+        block = 48 if bulk else 24
+        loops = rows // block
+
+        def body(j, carry, step=step, block=block):
+            step(pl.multiple_of(j * block, block), block)
+            return carry
+
+        lax.fori_loop(0, loops, body, 0)
+        at, rest = loops * block, rows - loops * block
+        if rest // 8:
+            step(at, rest // 8 * 8)
+        if rest % 8:
+            step(at + rest // 8 * 8, rest % 8)
+        for kind, (src, dst) in enumerate(((wb[i], w_out[i]), (mb[i], m_out[i]), (vb[i], v_out[i]))):
+            c = pltpu.make_async_copy(src, dst, outsem.at[i, kind])
+            c.start()
+            outs.append(c)
+        at = pl.ds(starts[i], rows * 128)
+        c = pltpu.make_async_copy(cb.at[:, at], copies_out.at[:, at], csem.at[i])
+        c.start()
+        outs.append(c)
+
+    tiles = [st[:, 128 * t : 128 * t + 128] for t in range(3)]
+    for t, v in enumerate(unlanes(tiles)):
+        width = min(128, 316 - 128 * t)
+        at = slice(128 * t, 128 * t + width)
+        v = v[:, 0:width]
+        m, s, w = adamw(w_in[7][:, at], m_in[7][:, at], v_in[7][:, at], v[0:2], rates[7])
+        m_out[7][:, at] = m
+        v_out[7][:, at] = s
+        w_out[7][:, at] = w
+        run_out[:, at] = MOMENTUM * running[:, at] + (1.0 - MOMENTUM) * v[2:4]
+    loss_out[...] = sc[0:1, 0:1]
+    count_out[...] = sc[1:2, 0:1]
+    for c in outs:
+        c.wait()
+
+
+def adam(gb, late, st, sc, running, masters, firsts, seconds):
+    vm = pl.BlockSpec(memory_space=pltpu.VMEM)
+    hbm = pl.BlockSpec(memory_space=pl.ANY)
+    dma = pltpu.SemaphoreType.DMA
+    flats = [jax.ShapeDtypeStruct((FLAT[n], 128), F32) for n in NAMES]
+    small = jax.ShapeDtypeStruct((2, 316), F32)
+    total = sum(FLAT[n] for n in NAMES) * 128
+    one = jax.ShapeDtypeStruct((1, 1), F32)
+    specs = [hbm] * 7 + [vm]
+    buffers = [pltpu.VMEM((FLAT[n], 128), F32) for n in NAMES]
+    return pl.pallas_call(
+        adam_kernel,
+        out_shape=[*(flats + [small]) * 3, small, one, one, jax.ShapeDtypeStruct((1, total), BF16)],
+        in_specs=[vm] * 5 + specs * 3,
+        out_specs=[*specs * 3, vm, vm, vm, hbm],
+        scratch_shapes=[
+            *buffers * 3, pltpu.VMEM((1, total), BF16), dma((7, 3)), dma((7, 3)), dma((7,)),
+        ],
+        compiler_params=pltpu.CompilerParams(vmem_limit_bytes=40 << 20),
+        name="adamw",
+    )(gb, late, st, sc, running, *masters, *firsts, *seconds)
 
 
 def per_device(
@@ -674,58 +1119,16 @@
         second_direct, second_squeeze, second_spatial, second_shrink, second_volume,
         second_pooled, second_readout, second_affine,
     ]
-    w1 = jnp.concatenate(
-        [
-            direct.reshape(CIN, 96), pooled.reshape(CIN, 32), squeeze.reshape(CIN, 48),
-            shrink.reshape(CIN, 12), jnp.zeros((CIN, 68), F32),
-        ],
-        axis=1,
-    ).astype(BF16)
-    wc = conv_weights(spatial, volume)
-    wct = jnp.transpose(wc, (0, 2, 1))
-    rd = readout.reshape(256, CLASSES)
-    rp = jnp.concatenate([rd[0:96], rd[224:256], rd[96:192], rd[192:224]], axis=0)
-    rp = jnp.pad(rp, ((0, 0), (0, 112))).astype(BF16)
-    a_d, a_s, a_k, a_p, a_sp, a_v = split_columns(affine, [96, 48, 12, 32, 96, 32])
-    aff = jnp.concatenate([a_d, a_p, a_s, a_k, jnp.zeros((2, 68), F32), a_sp, a_v], axis=1)
-    aff = jnp.pad(aff, ((0, 6), (0, 0)))
-
-    gwc, gw1, gr, stats, scal = core(features, lengths, labels, w1, wc, wct, rp, aff)
-
-    g_sp, g_vo = conv_grads(gwc)
-    g_rd = jnp.concatenate([gr[0:96], gr[128:224], gr[224:256], gr[96:128]], axis=0)[:, :CLASSES]
-    local = [
-        gw1[:, 0:96].reshape(1, -1),
-        gw1[:, 128:176].reshape(1, -1),
-        g_sp,
-        gw1[:, 176:188].reshape(1, -1),
-        g_vo,
-        gw1[:, 96:128].reshape(1, -1),
-        g_rd.reshape(1, -1),
-    ]
-    grads = list(lax.psum(tuple(local), "batch"))
-
-    def unlanes(rows):
-        return jnp.concatenate(
-            [rows[:, 0:96], rows[:, 128:188], rows[:, 96:128], rows[:, 256:384]], axis=1
-        )
-
-    grads.append(unlanes(stats[0:2]))
-    rates = step_rates()
-    updated = [
-        adamw(masters[i], firsts[i], seconds[i], grads[i], rates[i]) for i in range(8)
-    ]
-    running_next = MOMENTUM * running + (1.0 - MOMENTUM) * unlanes(stats[2:4])
-    copies = jnp.concatenate([updated[i][2] for i in range(7)], axis=1).astype(BF16)
-    return (
-        *[updated[i][0] for i in range(8)],
-        *[updated[i][1] for i in range(8)],
-        *[updated[i][2] for i in range(8)],
-        running_next,
-        scal[0, 0],
-        scal[1, 0],
-        copies,
+    def rows(flat):
+        return flat.reshape(-1, 128)
+
+    masters, firsts, seconds = (
+        [rows(a) for a in group[:7]] + [group[7]] for group in (masters, firsts, seconds)
     )
+    gb, late, st, sc = core(features, lengths, labels, masters[:7], affine)
+    out = adam(gb, late.reshape(NB * LATE_ROWS, 128), st, sc, running, masters, firsts, seconds)
+    flat_out = [a if i % 8 == 7 else a.reshape(1, -1) for i, a in enumerate(out[:24])]
+    return (*flat_out, out[24], out[25].reshape(()), out[26].reshape(()), out[27])
 
 
 def solution(mesh):

time: 398 us -> 197 us (0.49)
  blocking collectives: 126 us -> 0 us
  local copies, waits for them, and re-layouts: 68.5 us -> 16.1 us
  other arithmetic: 57.4 us -> 8.02 us
  Pallas kernels: 126 us -> 170 us
  between operations: 15 us -> 0.92 us
    psum x1 -> x0, blocking collectives: 126 us -> none  [per_device(): grads = list(lax.psum(tuple(local), 'batch'))]
    pallas_call x1 -> x2, Pallas kernels: 126 us -> 170 us  [the longest x1 156 us: core(): pl.pallas_call(core_kernel, out_shape=(jax.ShapeDtypeStruct((2 * CORE_ROW...]
    unnamed x8 -> x6, other arithmetic: 45.3 us -> 8.02 us
    reshape x16 -> x2, local copies, waits for them, and re-layouts: 33.2 us -> 1.77 us  [per_device(): a.reshape(1, -1)]
    slice x22 -> x0, local copies, waits for them, and re-layouts: 19.3 us -> none  [the longest x4 2.97 us: split_columns(): pieces.append(packed[..., offset:offset + channels])]
    unnamed x96 -> x53, local copies, waits for them, and re-layouts: 3.81 us -> 14.3 us
    transpose x5 -> x0, local copies, waits for them, and re-layouts: 10.3 us -> none  [the longest x2 4.51 us: conv_grads(): sp = jnp.transpose(g[:, :, 0:48, :, 0:96], (3, 0, 1, 2, 4)).reshape(1, -1)]
    another operation x5 -> x0, other arithmetic: 5.54 us -> none
  transfers between devices with their start and end apart: 1 -> 0, of which waited for: 0 -> 0; matrix products, arithmetic and copies ran while one was open for 1% -> 0% of each run, Pallas kernels for 0% -> 0%
where the time goes in v2:
time: 197 us; the launch traced here: 195 us
  Pallas kernels  170 us (86%)
  local copies, waits for them, and re-layouts  16.1 us (8%)
  other arithmetic  8.02 us (4%)
    pallas_call x1, Pallas kernels, core(): pl.pallas_call(core_kernel, out_shape=(jax.ShapeDtypeStruct((2 * CORE_ROW...  156 us
    unnamed x53, local copies, waits for them, and re-layouts  14.3 us
    pallas_call x1, Pallas kernels, adam(): pl.pallas_call(adam_kernel, out_shape=[*(flats + [small]) * 3, small, one...  13.3 us
    unnamed x6, other arithmetic  8.02 us

profile of v2, /device:TPU:0, one launch (start us, length us, event | category | flops | bytes accessed | tf_op | source)
XLA Modules:
  0.0 194.7 jit_solution(4234861393689300636)
XLA Ops:
  0.7 1.3 copy.56.lab_ref
  2.0 0.0 copy-start.15
  2.0 1.5 reduce
  3.5 0.9 reduce.2
  4.4 0.0 copy-start.9
  4.4 0.9 reduce.4
  5.4 0.0 copy-start.22
  5.4 0.0 copy-start.23
  5.4 0.0 copy-start.24
  5.4 2.0 %reduce.1 = f32[41472]{0:T(1024)} reduce(f32[1,41472]{1,0:T(1,128)} %param.35, f32[]{:T(128)} %constant.24), dimensions={0}, to_apply=%param.35.reduce_sub_computation | reduce | bytes 331780 | tf_op args[7]
  7.4 0.0 copy-start.6
  7.4 0.0 copy-start.11
  7.4 1.4 reduce.3
  8.7 0.0 copy-start.5
  8.8 0.0 copy-start.7
  8.8 1.4 reduce.5
  10.1 0.0 copy-start
  10.1 0.0 copy-start.2
  10.2 0.0 copy-start.4
  10.2 0.0 copy-start.8
  10.2 0.0 copy-start.20
  10.2 156.3 %block.1 = (f32[6144,128]{1,0:T(8,128)}, f32[32,16,128]{2,1,0:T(8,128)}, f32[8,384]{1,0:T(8,128)}, f32[8,128]{1,0:T(8,128)}) custom-call(bf16[1,326144]{1,0:T(2,128)(2,1)} %x_hbm.1, s32[8]{0:T(128)} %len_ref.1, s32[8,4]{1,0:T(8,128)} %copy.56.lab_ref, f32[624,128]{1,0:T(8,128)} %bitcast.73, f32[312,128]{1,0:T(8,128)} %bitcast.77, f32[3888,128]{1,0:T(8,128)} %bitcast.65, ...), custom_call_target="tpu_custom_call" | custom-call | tf_op jit(solution)/shard_map/block/pallas_call | solution.py:931
  166.5 0.0 copy-done.15
  166.6 0.0 copy-done.9
  166.6 0.0 copy-done.22
  166.6 0.0 copy-done.23
  166.6 0.0 copy-done.24
  166.6 0.0 copy-done.6
  166.6 0.0 copy-done.11
  166.6 0.0 copy-done.5
  166.6 0.0 copy-done.7
  166.6 0.0 copy-done
  166.6 0.0 copy-done.2
  166.7 0.0 copy-done.4
  166.7 0.0 copy-done.8
  166.7 0.0 copy-done.20
  166.7 0.0 copy-start.1
  166.7 1.9 copy-done.1
  168.6 0.0 copy-start.3
  168.6 1.6 copy-done.3
  170.1 0.0 copy-start.10
  170.1 1.0 copy-done.10
  171.1 0.0 copy-start.12
  171.1 1.0 copy-done.12
  172.1 0.0 copy-start.13
  172.1 1.0 copy-done.13
  173.1 0.0 copy-start.14
  173.1 0.9 copy-done.14
  174.0 0.0 copy-start.16
  174.0 0.9 copy-done.16
  174.9 0.0 copy-start.17
  174.9 0.9 copy-done.17
  175.8 0.0 copy-start.18
  175.8 0.9 copy-done.18
  176.7 0.0 copy-start.19
  176.7 0.7 copy-done.19
  177.4 0.0 copy-start.21
  177.4 0.7 copy-done.21
  178.1 13.3 %adamw.1 = (f32[624,128]{1,0:T(8,128)}, f32[312,128]{1,0:T(8,128)}, f32[3888,128]{1,0:T(8,128)}, f32[78,128]{1,0:T(8,128)S(1)}, f32[324,128]{1,0:T(8,128)S(1)}, ...) custom-call(f32[6144,128]{1,0:T(8,128)S(1)} %copy-done.1, ...), custom_call_target="tpu_custom_call" | custom-call | tf_op jit(solution)/shard_map/adamw/pallas_call | solution.py:1094
  191.4 0.7 copy.70
  192.1 0.7 copy_bitcast_fusion.3
  192.8 0.8 copy.69
  193.6 1.1 copy_bitcast_fusion
Async XLA Ops:
  2.0 164.5 %copy-start.15 = (f32[1,39936]{1,0:T(1,128)S(1)}, f32[1,39936]{1,0:T(1,128)}, u32[]{:S(2)}) copy-start(f32[1,39936]{1,0:T(1,128)} %param.40) | copy-start | bytes 479236
  4.4 162.1 %copy-start.9 = (f32[1,102400]{1,0:T(1,128)S(1)}, f32[1,102400]{1,0:T(1,128)}, u32[]{:S(2)}) copy-start(f32[1,102400]{1,0:T(1,128)} %param.45) | copy-start | bytes 1228804
  5.4 161.2 %copy-start.22 = (f32[2,316]{1,0:T(2,128)S(1)}, f32[2,316]{1,0:T(2,128)}, u32[]{:S(2)}) copy-start(f32[2,316]{1,0:T(2,128)} %refs_4_.1) | copy-start | bytes 7588
  5.4 161.2 %copy-start.23 = (f32[2,316]{1,0:T(2,128)S(1)}, f32[2,316]{1,0:T(2,128)}, u32[]{:S(2)}) copy-start(f32[2,316]{1,0:T(2,128)} %refs_20_.1) | copy-start | bytes 7588
  5.4 161.2 %copy-start.24 = (f32[2,316]{1,0:T(2,128)S(1)}, f32[2,316]{1,0:T(2,128)}, u32[]{:S(2)}) copy-start(f32[2,316]{1,0:T(2,128)} %refs_28_.1) | copy-start | bytes 7588
  7.4 159.2 %copy-start.6 = (f32[1,79872]{1,0:T(1,128)S(1)}, f32[1,79872]{1,0:T(1,128)}, u32[]{:S(2)}) copy-start(f32[1,79872]{1,0:T(1,128)} %param.31) | copy-start | bytes 958468
  7.4 159.2 %copy-start.11 = (f32[9984]{0:T(1024)S(1)}, f32[9984]{0:T(1024)}, u32[]{:S(2)}) copy-start(f32[9984]{0:T(1024)} %reduce) | copy-start | bytes 119812
  8.7 157.9 %copy-start.5 = (f32[41472]{0:T(1024)S(1)}, f32[41472]{0:T(1024)}, u32[]{:S(2)}) copy-start(f32[41472]{0:T(1024)} %reduce.1) | copy-start | bytes 497668
  8.8 157.9 %copy-start.7 = (f32[1,39936]{1,0:T(1,128)S(1)}, f32[1,39936]{1,0:T(1,128)}, u32[]{:S(2)}) copy-start(f32[1,39936]{1,0:T(1,128)} %param.32) | copy-start | bytes 479236
  10.1 156.5 %copy-start = (f32[1,497664]{1,0:T(1,128)S(1)}, f32[1,497664]{1,0:T(1,128)}, u32[]{:S(2)}) copy-start(f32[1,497664]{1,0:T(1,128)} %param.33) | copy-start | bytes 5971972
  10.1 156.5 %copy-start.2 = (f32[1,497664]{1,0:T(1,128)S(1)}, f32[1,497664]{1,0:T(1,128)}, u32[]{:S(2)}) copy-start(f32[1,497664]{1,0:T(1,128)} %param.41) | copy-start | bytes 5971972
  10.2 156.5 %copy-start.4 = (f32[1,102400]{1,0:T(1,128)S(1)}, f32[1,102400]{1,0:T(1,128)}, u32[]{:S(2)}) copy-start(f32[1,102400]{1,0:T(1,128)} %param.37) | copy-start | bytes 1228804
  10.2 156.5 %copy-start.8 = (f32[1,26624]{1,0:T(1,128)S(1)}, f32[1,26624]{1,0:T(1,128)}, u32[]{:S(2)}) copy-start(f32[1,26624]{1,0:T(1,128)} %param.36) | copy-start | bytes 319492
  10.2 156.5 %copy-start.20 = (f32[2,316]{1,0:T(2,128)S(1)}, f32[2,316]{1,0:T(2,128)}, u32[]{:S(2)}) copy-start(f32[2,316]{1,0:T(2,128)} %refs_12_.1) | copy-start | bytes 7588
  166.7 1.9 copy-start.1
  168.6 1.6 copy-start.3
  170.1 1.0 copy-start.10
  171.1 1.0 copy-start.12
  172.1 1.0 copy-start.13
  173.1 0.9 copy-start.14
  174.0 0.9 copy-start.16
  174.9 0.9 copy-start.17
  175.8 0.9 copy-start.18
  176.7 0.7 copy-start.19
  177.4 0.7 copy-start.21

commit v3 on v2

--- a/solution.py
+++ b/solution.py
@@ -28,17 +28,19 @@
 CB = CIN // NC
 GW = 8 * CB
 HALF = 25
+SHIFT = 112
+W1_ROWS = 448
 TAPS = 27
 FLAT = {"direct": 624, "squeeze": 312, "spatial": 3888, "shrink": 78, "volume": 324, "pooled": 208,
         "readout": 800}
 NAMES = ("direct", "squeeze", "spatial", "shrink", "volume", "pooled", "readout")
-BULK = {"spatial": 0, "volume": 3888, "direct": 4224, "pooled": 4848, "readout": 5056}
+BULK = {"spatial": 0, "volume": 3888, "direct": 4216, "pooled": 4840, "readout": 5048}
+NARROW = ("shrink", "volume")
 LATE = {"squeeze": 0, "shrink": 312}
-CORE_ROWS = 3072
-GROUP_ROWS = 1536
-FIRST_ROWS = 384
-LAST_ROWS = 96
+CHUNKS = ((0, 64), (4096, 32))
+BULK_ROWS = 6144
 LATE_ROWS = 16
+ADAM_ROWS = 648
 
 EPS = 1e-05
 BETA_ONE = 0.5
@@ -66,10 +68,12 @@
 
 def adamw(weight, moment_one, moment_two, gradient, step_rate):
     first_new = BETA_ONE * moment_one + (1.0 - BETA_ONE) * gradient
-    second_new = BETA_TWO * moment_two + (1.0 - BETA_TWO) * gradient * gradient
-    first_hat = first_new / (1.0 - BETA_ONE**STEP)
-    second_hat = second_new / (1.0 - BETA_TWO**STEP)
-    weight_new = weight - step_rate * (first_hat / (jnp.sqrt(second_hat) + 1e-08) + DECAY * weight)
+    second_new = BETA_TWO * moment_two + (1.0 - BETA_TWO) * (gradient * gradient)
+    scale_one = step_rate / (1.0 - BETA_ONE**STEP)
+    scale_two = 1.0 / (1.0 - BETA_TWO**STEP)
+    weight_new = weight * (1.0 - step_rate * DECAY) - scale_one * first_new / (
+        jnp.sqrt(second_new * scale_two) + 1e-08
+    )
     return (first_new, second_new, weight_new)
 
 
@@ -105,25 +109,23 @@
 
 def share_start(buf, me, send, recv):
     def one(d, carry):
-        send_to(buf.at[me], buf.at[me], send.at[d], recv.at[d], batch_peer(me, d)).start()
+        send_to(buf.at[me], buf.at[me], send, recv, batch_peer(me, d)).start()
         return carry
 
     lax.fori_loop(1, NB, one, 0)
 
 
+def share_copy(buf, me, send, recv):
+    others = buf.at[pl.ds(0, NB - 1)]
+    return send_to(others, others, send, recv, batch_peer(me, 1))
+
+
 def share_wait(buf, me, send, recv):
-    def one(d, carry):
-        src = lax.rem(me - d + NB, NB)
-        send_to(buf.at[src], buf.at[src], send.at[d], recv.at[d], batch_peer(me, d)).wait_recv()
-        return carry
-
-    lax.fori_loop(1, NB, one, 0)
-
-    def two(d, carry):
-        send_to(buf.at[me], buf.at[me], send.at[d], recv.at[d], batch_peer(me, d)).wait_send()
-        return carry
-
-    lax.fori_loop(1, NB, two, 0)
+    share_copy(buf, me, send, recv).wait_recv()
+
+
+def share_sent(buf, me, send, recv):
+    share_copy(buf, me, send, recv).wait_send()
 
 
 def digit_of(me, stride, size):
@@ -164,7 +166,7 @@
     return lax.broadcasted_iota(jnp.int32, v, 1)
 
 
-def prepare_w1(flat, wn, wk, w1s):
+def prepare_w1(flat, wn, wk, w1p):
     lane = lanes_of((208, 128))
     tiles = [flat["direct"][pl.ds(i, 208, stride=3), :] for i in range(3)]
     pool = flat["pooled"][...]
@@ -186,9 +188,9 @@
         rows = slice(k * CB, (k + 1) * CB)
         second = jnp.where(lane < 48, wn[1, rows, :], jnp.where(lane < 60, wk[rows, :], 0.0))
         both = jnp.concatenate([wn[0, rows, :], second], axis=1).astype(BF16)
-        for r in range(8):
-            _, off, _ = window_of(r)
-            w1s[r, k, off : off + CB, :] = both
+        w1p[k, 0:SHIFT, :] = jnp.zeros((SHIFT, 256), BF16)
+        w1p[k, SHIFT : SHIFT + CB, :] = both
+        w1p[k, SHIFT + CB : W1_ROWS, :] = jnp.zeros((W1_ROWS - SHIFT - CB, 256), BF16)
 
 
 def prepare_conv(flat, tb, vn, wc, wct):
@@ -266,10 +268,10 @@
     x_hbm, len_ref, lab_ref, direct_hbm, squeeze_hbm, spatial_hbm, shrink_hbm, volume_hbm,
     pooled_hbm, readout_hbm, affine_ref,
     gb_ref, late_ref, st_ref, sc_ref,
-    x_ref, f_direct, f_squeeze, f_spatial, f_shrink, f_volume, f_pooled, f_readout,
+    x_ref, n_shrink, n_volume,
     wn, wk, tb, vn, rn, wc_ref, wct_ref, r_ref, aff_ref,
-    xf, xg, w1s, ynat, ypos, box, ob, msg, got, apad, acol, at, y2, dpre, dypad, dm, dgot, dnat,
-    gw1_ref, gq, gr, g, gcore, r1, r2, lsend, lgot,
+    xf, xg, w1p, ynat, ypos, box, ob, got, apad, acol, at, y2, dpre, dypad, dm, dgot, dnat,
+    gw1_ref, gq, gr, g, gca, gcb, r1a, r1b, r2a, r2b, lsend, lgot,
     lbuf, sbuf_a, sbuf_b, sbuf_c, sbuf_d,
     xin, win, xs, xr, ms, mr, ls, lr, ds_, dr,
     as_, ar, bs, br, cs, cr, es, er, fs, fr, hs, hr,
@@ -280,17 +282,15 @@
 
     barrier = pltpu.get_barrier_semaphore()
 
-    cuts = [0, 79 * 1024, 158 * 1024, 237 * 1024, 326144]
+    cuts = [0, 91 * 1024, 182 * 1024, 250 * 1024, 326144]
     x_in = []
     for i in range(4):
         at_ = pl.ds(cuts[i], cuts[i + 1] - cuts[i])
         c = pltpu.make_async_copy(x_hbm.at[:, at_], x_ref.at[:, at_], xin.at[i])
         c.start()
         x_in.append(c)
-    flat = dict(
-        direct=f_direct, squeeze=f_squeeze, spatial=f_spatial, shrink=f_shrink, volume=f_volume,
-        pooled=f_pooled, readout=f_readout,
-    )
+    flat = {n: g.at[at_ : at_ + FLAT[n]] for n, at_ in BULK.items()}
+    flat.update({n: lsend.at[at_ : at_ + FLAT[n]] for n, at_ in LATE.items()})
     w_in = []
     for i, (src, name) in enumerate(
         zip(
@@ -298,7 +298,8 @@
             NAMES,
         )
     ):
-        c = pltpu.make_async_copy(src, flat[name], win.at[i])
+        dst = {"shrink": n_shrink, "volume": n_volume}.get(name, flat[name])
+        c = pltpu.make_async_copy(src, dst, win.at[i])
         c.start()
         w_in.append(c)
 
@@ -315,29 +316,37 @@
         xf[pl.ds(pl.multiple_of(i * 8, 8), 8), :] = v.reshape(8, 128)
         return carry
 
-    for i in range(4):
-        x_in[i].wait()
-        first = 79 * i
-        lax.fori_loop(first, first + 79 if i < 3 else 318, flat_rows, 0, unroll=4)
-    xf[pl.ds(2544, 4), :] = x_ref[:, 318 * 1024 : 318 * 1024 + 512].astype(F32).reshape(4, 128)
-    xf[pl.ds(2548, 2704 - 2548), :] = jnp.zeros((2704 - 2548, 128), F32)
-    for i in range(13):
-        xg[me, :, 128 * i : 128 * i + 128] = xf[pl.ds(i, GPAD, stride=13), :].astype(BF16)
-
-    pl.semaphore_wait(barrier, NB - 1 + NC - 1)
-
     right, left = chan_peer(me, 1), chan_peer(me, NC - 1)
     left_i, right_i = lax.rem(me + NC - 1, NC), lax.rem(me + 1, NC)
-    cut = 112
+    split = 112
 
     def part(who, low):
-        return xg.at[who, 0:cut] if low else xg.at[who, cut:GPAD]
-
-    hops = []
-    for i, (low, to) in enumerate([(True, right), (False, left), (False, right), (True, left)]):
-        c = send_to(part(me, low), part(me, low), xs.at[i], xr.at[i], to)
-        c.start()
-        hops.append(c)
+        return xg.at[who, 0:split] if low else xg.at[who, split:GPAD]
+
+    hops = [
+        send_to(part(me, low), part(me, low), xs.at[i], xr.at[i], to)
+        for i, (low, to) in enumerate([(True, right), (True, left), (False, right), (False, left)])
+    ]
+    xf[pl.ds(2548, 2704 - 2548), :] = jnp.zeros((2704 - 2548, 128), F32)
+    for i in range(2):
+        x_in[i].wait()
+        lax.fori_loop(91 * i, 91 * i + 91, flat_rows, 0, unroll=7)
+    for i in range(13):
+        xg[me, 0:split, 128 * i : 128 * i + 128] = xf[pl.ds(i, split, stride=13), :].astype(BF16)
+    pl.semaphore_wait(barrier, NB - 1 + NC - 1)
+    hops[0].start()
+    hops[1].start()
+    x_in[2].wait()
+    lax.fori_loop(182, 250, flat_rows, 0, unroll=4)
+    x_in[3].wait()
+    lax.fori_loop(250, 318, flat_rows, 0, unroll=4)
+    xf[pl.ds(2544, 4), :] = x_ref[:, 318 * 1024 : 318 * 1024 + 512].astype(F32).reshape(4, 128)
+    for i in range(13):
+        xg[me, split:GPAD, 128 * i : 128 * i + 128] = xf[
+            pl.ds(13 * split + i, GPAD - split, stride=13), :
+        ].astype(BF16)
+    hops[2].start()
+    hops[3].start()
 
     rowi = lax.broadcasted_iota(jnp.int32, (ROWS, 128), 0)
     lane = lax.broadcasted_iota(jnp.int32, (ROWS, 128), 1)
@@ -360,14 +369,14 @@
     is_pool = lane >= 96
     low_half = lane < 64
 
-    def zero_w(i, carry):
-        w1s[i] = jnp.zeros((NC, 384, 256), BF16)
-        return carry
-
-    lax.fori_loop(0, 8, zero_w, 0)
     for c in w_in:
         c.wait()
-    prepare_w1(flat, wn, wk, w1s)
+    for src, dst in ((n_shrink, flat["shrink"]), (n_volume, flat["volume"])):
+        count = dst.shape[0]
+        whole = count // 8 * 8
+        dst[0:whole, :] = src[:, 0 : whole * 128].reshape(whole, 128)
+        dst[whole:count, :] = src[:, whole * 128 : count * 128].reshape(count - whole, 128)
+    prepare_w1(flat, wn, wk, w1p)
     prepare_affine(affine_ref, aff_ref)
     prepare_readout(flat, rn, r_ref)
 
@@ -384,21 +393,21 @@
     hops[0].wait_recv()
     f0 = send_to(part(left_i, True), part(left_i, True), xs.at[4], xr.at[4], right)
     f0.start()
-    hops[1].wait_recv()
+    hops[3].wait_recv()
     f1 = send_to(part(right_i, False), part(right_i, False), xs.at[5], xr.at[5], left)
     f1.start()
+    hops[1].wait_recv()
     hops[2].wait_recv()
-    hops[3].wait_recv()
     f0.wait()
     f1.wait()
     for c in hops:
         c.wait_send()
 
     for r in range(8):
-        first, _, lanes = window_of(r)
+        first, off, lanes = window_of(r)
         acc = jnp.zeros((GPAD, 256), F32)
         for k in range(NC):
-            acc = acc + dot(xg[k, :, first : first + lanes], w1s[r, k, 0:lanes, :])
+            acc = acc + dot(xg[k, :, first : first + lanes], w1p[k, SHIFT - off : SHIFT - off + lanes, :])
         ynat[0, pl.ds(r, GPAD, stride=8), :] = acc[:, 0:128]
         ynat[1, pl.ds(r, GPAD, stride=8), :] = acc[:, 128:256]
 
@@ -445,8 +454,8 @@
     def col(v):
         return jnp.sum(v, axis=0, keepdims=True)
 
-    def pack_rows(rows):
-        fill = [jnp.zeros((1, 128), F32)] * (8 - len(rows))
+    def pack_rows(rows, count=8):
+        fill = [jnp.zeros((1, 128), F32)] * (count - len(rows))
         return jnp.concatenate(list(rows) + fill, axis=0)
 
     sbuf_a[me_b] = pack_rows(
@@ -484,16 +493,20 @@
     ob[POS] = zero128
 
     def to_msg(p, carry):
-        msg[p] = jnp.where(low_half, ob[p], pltpu.roll(ob[p + HALF], 64, 1)).astype(BF16)
+        got[me, p] = jnp.where(low_half, ob[p], pltpu.roll(ob[p + HALF], 64, 1)).astype(BF16)
         return carry
 
     lax.fori_loop(0, HALF, to_msg, 0)
+    near = 12
+
+    def half(who, low):
+        return got.at[who, 0:near] if low else got.at[who, near:HALF]
+
     ms_c = []
-    for d in range(1, NC):
-        c = send_to(msg, got.at[me], ms.at[d], mr.at[d], chan_peer(me, d))
+    for i, (low, to) in enumerate([(True, right), (False, left), (False, right), (True, left)]):
+        c = send_to(half(me, low), half(me, low), ms.at[i], mr.at[i], to)
         c.start()
         ms_c.append(c)
-    got[me] = msg[...]
 
     def act0(p, carry):
         _, pre, sig = forward(ypos[p][:, 0:128], n0)
@@ -501,7 +514,12 @@
 
     feat0 = lax.fori_loop(0, POS, act0, zero128)
 
-    for c in ms_c:
+    for i, (who, low, to) in enumerate([(left_i, True, right), (right_i, False, left)]):
+        ms_c[i].wait_recv()
+        c = send_to(half(who, low), half(who, low), ms.at[4 + i], mr.at[4 + i], to)
+        c.start()
+        ms_c.append(c)
+    for c in ms_c[2:]:
         c.wait_recv()
 
     def unpack(p, carry):
@@ -542,7 +560,7 @@
         return s1, s2
 
     s1, s2 = lax.fori_loop(0, SIDE, conv, (zero128, zero128))
-    sbuf_b[me_b] = pack_rows([col(s1), col(s2)])
+    sbuf_b[me_b] = pack_rows([col(s1), col(s2)], 2)
     share_start(sbuf_b, me_b, bs, br)
     at[...] = jnp.transpose(acol[...].reshape(VOX, 256))
     share_wait(sbuf_b, me_b, bs, br)
@@ -568,7 +586,7 @@
     row512 = lax.broadcasted_iota(jnp.int32, (ROWS, 512), 0)
     labs = jnp.zeros((ROWS, 512), jnp.int32)
     for i in range(ROWS):
-        labs = jnp.where(row512 == i, lab_ref[i // 4, i % 4], labs)
+        labs = jnp.where(row512 == i, lab_ref[i % 4, i // 4], labs)
     real = cls < CLASSES
     logits = jnp.where(real, logits, -1e30)
     peak = jnp.max(logits, axis=1, keepdims=True)
@@ -650,21 +668,34 @@
             a = ynat[j // 2, pl.ds(pl.multiple_of(p * ROWS, ROWS), ROWS), :]
             b = ynat[j // 2, pl.ds(pl.multiple_of((p + HALF) * ROWS, ROWS), ROWS), :]
             if j % 2 == 0:
-                dm[j, p] = jnp.where(low_half, a, pltpu.roll(b, 64, 1))
+                dm[j, p] = jnp.where(low_half, a, pltpu.roll(b, 64, 1)).astype(BF16)
             else:
-                dm[j, p] = jnp.where(low_half, pltpu.roll(a, 64, 1), b)
+                dm[j, p] = jnp.where(low_half, pltpu.roll(a, 64, 1), b).astype(BF16)
         return carry
 
     for t in range(2):
         ynat[t, pl.ds(VOX, ROWS), :] = zero128
     lax.fori_loop(0, HALF, to_dm, 0)
-    ds_c = []
-    for d in range(1, NC):
-        to = lax.rem(me + d, NC)
-        c = send_to(dm.at[to], dgot.at[me], ds_.at[d], dr.at[d], chan_peer(me, d))
+    far_i = lax.rem(me + 2, NC)
+    lo_, hi_ = pl.ds(0, near), pl.ds(near, HALF - near)
+
+    def far_copy(i):
+        rows_, to = ((lo_, right), (hi_, left))[i]
+        return send_to(dm.at[far_i, rows_], dgot.at[2, rows_], ds_.at[i], dr.at[i], to)
+
+    def near_copy(i):
+        who, rows_, to, slot = (
+            (right_i, hi_, right, 0), (left_i, lo_, left, 1), (right_i, lo_, right, 0),
+            (left_i, hi_, left, 1),
+        )[i]
+        return send_to(
+            dm.at[who, rows_], dgot.at[slot, rows_], ds_.at[2 + i], dr.at[2 + i], to
+        )
+
+    far_c = [far_copy(i) for i in range(2)]
+    near_c = [near_copy(i) for i in range(4)]
+    for c in far_c + near_c[0:2]:
         c.start()
-        ds_c.append(c)
-    dgot[me] = dm[me]
 
     def grad_conv(q, carry):
         dh = q // 3
@@ -691,10 +722,176 @@
             flatten_96(lambda j: gq[pl.ds(j, 48, stride=4), :], 48, put)
         return carry
 
-    lax.fori_loop(0, 9, grad_conv, 0)
+    lax.fori_loop(0, 4, grad_conv, 0)
+    for c in far_c:
+        c.wait_recv()
+
+    def add_far(p, carry):
+        who = jnp.where(p < near, right_i, left_i)
+        dm[who, p] = (dm[who, p].astype(F32) + dgot[2, p].astype(F32)).astype(dm.dtype)
+        return carry
+
+    lax.fori_loop(0, HALF, add_far, 0)
+    for c in near_c[2:4]:
+        c.start()
+    lax.fori_loop(4, 9, grad_conv, 0)
     g[BULK["volume"] : BULK["volume"] + 324, :] = flatten_32(
         lambda j: vn[pl.ds(j, 324, stride=4), :], 324
     )
+
+    core_i = lax.rem(me_b, 2)
+    mate = digit_peer(me_b, 1, 2, 1)
+    along = ((2, 8), (8, 2))
+    digits = [[digit_of(me_b, along[i][s], 4) for i in range(2)] for s in range(2)]
+
+    class Chunk:
+        def __init__(self, index):
+            self.base, self.last = CHUNKS[index]
+            self.k = index
+            self.first = 4 * self.last
+            self.group = 4 * self.first
+            self.half = 2 * self.group
+            self.own = pl.multiple_of(self.base + core_i * self.half, self.last)
+            self.r1 = (r1a, r1b)[index]
+            self.r2 = (r2a, r2b)[index]
+            self.gc = (gca, gcb)[index]
+
+        def rows(self, at, count):
+            return pl.ds(pl.multiple_of(at, self.last), count)
+
+        def core_start(self):
+            theirs = self.rows(self.base + (1 - core_i) * self.half, self.half)
+            self.c0 = send_to(g.at[theirs], self.gc, co_s.at[self.k], co_r.at[self.k], mate)
+            self.c0.start()
+
+        def one_start(self):
+            self.c0.wait()
+            n = self.last
+
+            def add(i, carry):
+                at_ = self.rows(i * n, n)
+                self.gc[at_, :] = self.gc[at_, :] + g[self.rows(self.own + i * n, n), :]
+                return carry
+
+            lax.fori_loop(0, self.half // n, add, 0)
+            self.c1 = []
+            for i in range(2):
+                mine = digits[0][i]
+                for d in range(1, 4):
+                    to = lax.rem(mine + d, 4)
+                    c = send_to(
+                        self.gc.at[self.rows(i * self.group + to * self.first, self.first)],
+                        self.r1.at[i, mine], s1s.at[self.k, i, d], s1r.at[self.k, i, d],
+                        digit_peer(me_b, along[i][0], 4, d),
+                    )
+                    c.start()
+                    self.c1.append(c)
+                self.r1[i, mine] = self.gc[
+                    self.rows(i * self.group + mine * self.first, self.first), :
+                ]
+
+        def two_start(self):
+            for c in self.c1:
+                c.wait()
+            self.c2 = []
+            for i in range(2):
+                mine = digits[1][i]
+                self.r1[i, 0] = total_of(self.r1.at[i], 4)
+                for d in range(1, 4):
+                    to = lax.rem(mine + d, 4)
+                    c = send_to(
+                        self.r1.at[i, 0, self.rows(to * self.last, self.last)],
+                        self.r2.at[i, mine], s2s.at[self.k, i, d], s2r.at[self.k, i, d],
+                        digit_peer(me_b, along[i][1], 4, d),
+                    )
+                    c.start()
+                    self.c2.append(c)
+                self.r2[i, mine] = self.r1[i, 0, self.rows(mine * self.last, self.last), :]
+
+        def gather_start(self):
+            for c in self.c2:
+                c.wait()
+            self.c3 = []
+            for i in range(2):
+                at_ = self.rows(
+                    self.own + i * self.group + digits[0][i] * self.first
+                    + digits[1][i] * self.last,
+                    self.last,
+                )
+                gb_ref[at_, :] = total_of(self.r2.at[i], 4)
+                for d in range(1, 4):
+                    c = send_to(
+                        gb_ref.at[at_], gb_ref.at[at_], g1s.at[self.k, i, d],
+                        g1r.at[self.k, i, d], digit_peer(me_b, along[i][1], 4, d),
+                    )
+                    c.start()
+                    self.c3.append(c)
+
+        def spread_start(self):
+            for c in self.c3:
+                c.wait()
+            self.c4 = []
+            self.c5 = []
+            for i in range(2):
+                mine = digits[0][i]
+                at_ = self.rows(self.own + i * self.group + mine * self.first, self.first)
+                for d in range(1, 4):
+                    c = send_to(
+                        gb_ref.at[at_], gb_ref.at[at_], g2s.at[self.k, i, d],
+                        g2r.at[self.k, i, d], digit_peer(me_b, along[i][0], 4, d),
+                    )
+                    c.start()
+                    self.c4.append((c, i, d))
+                self.mate_start(i, 0)
+
+        def mate_start(self, i, d):
+            digit = lax.rem(digits[0][i] - d + 4, 4)
+            at_ = self.rows(self.own + i * self.group + digit * self.first, self.first)
+            c = send_to(
+                gb_ref.at[at_], gb_ref.at[at_], g3s.at[self.k, i, d], g3r.at[self.k, i, d], mate
+            )
+            c.start()
+            self.c5.append(c)
+
+        def mate_rest(self):
+            for c, i, d in self.c4:
+                c.wait_recv()
+                self.mate_start(i, d)
+
+        def finish(self):
+            for c, i, d in self.c4:
+                c.wait_send()
+            for c in self.c5:
+                c.wait()
+
+    first_chunk, second_chunk = Chunk(0), Chunk(1)
+    first_chunk.core_start()
+
+    for c in near_c:
+        c.wait_recv()
+
+    def back1(p, carry):
+        g1, b1 = carry
+        s = dm[me, p].astype(F32) + dgot[0, p].astype(F32) + dgot[1, p].astype(F32)
+        d, m = back(ypos[p][:, 128:256], n1, jnp.where(low_half, s, 0.0))
+        ob[p] = d
+        g1, b1 = g1 + d * m, b1 + d
+        q = jnp.minimum(p + HALF, POS - 1)
+        live = (p < POS - HALF).astype(F32)
+        d, m = back(ypos[q][:, 128:256], n1, jnp.where(low_half, pltpu.roll(s, 64, 1), 0.0) * live)
+
+        @pl.when(p < POS - HALF)
+        def _():
+            ob[p + HALF] = d
+
+        return g1 + d * m, b1 + d
+
+    g1, b1 = lax.fori_loop(0, HALF, back1, (zero128, zero128))
+    sbuf_d[me_b] = pack_rows([col(g1), col(b1)], 2)
+    share_start(sbuf_d, me_b, es, er)
+    for c in far_c + near_c:
+        c.wait_send()
+    first_chunk.one_start()
 
     def dy0_at(p, carry):
         v = finish(ypos[p][:, 0:128], n0, dpre[p][:, 0:128], totc[0:1], totc[1:2])
@@ -745,70 +942,12 @@
         lambda j: gw1_ref[0, pl.ds(j, 208, stride=4), :], 208
     )
 
-    core_i = lax.rem(me_b, 2)
-    mate = digit_peer(me_b, 1, 2, 1)
-    half_at = pl.multiple_of(core_i * CORE_ROWS, CORE_ROWS)
-    mate_at = pl.multiple_of((1 - core_i) * CORE_ROWS, CORE_ROWS)
-    core_c = send_to(g.at[pl.ds(mate_at, CORE_ROWS)], gcore, co_s, co_r, mate)
-    core_c.start()
-
-    for c in ds_c:
-        c.wait_recv()
-
-    def back1(p, carry):
-        g1, b1 = carry
-        s = dgot[0, p] + dgot[1, p] + dgot[2, p] + dgot[3, p]
-        d, m = back(ypos[p][:, 128:256], n1, jnp.where(low_half, s, 0.0))
-        dpre[p, :, 0:128] = d
-        g1, b1 = g1 + d * m, b1 + d
-        q = jnp.minimum(p + HALF, POS - 1)
-        live = (p < POS - HALF).astype(F32)
-        d, m = back(ypos[q][:, 128:256], n1, jnp.where(low_half, pltpu.roll(s, 64, 1), 0.0) * live)
-
-        @pl.when(p < POS - HALF)
-        def _():
-            dpre[p + HALF, :, 0:128] = d
-
-        return g1 + d * m, b1 + d
-
-    g1, b1 = lax.fori_loop(0, HALF, back1, (zero128, zero128))
-    sbuf_d[me_b] = pack_rows([col(g1), col(b1)])
-    share_start(sbuf_d, me_b, es, er)
-    for c in ds_c:
-        c.wait_send()
-
-    along = ((2, 8), (8, 2))
-    firsts = [digit_of(me_b, along[i][0], 4) for i in range(2)]
-    seconds = [digit_of(me_b, along[i][1], 4) for i in range(2)]
-    core_c.wait()
-
-    def add_core(i, carry):
-        at_ = pl.multiple_of(i * 96, 96)
-        gcore[pl.ds(at_, 96), :] = gcore[pl.ds(at_, 96), :] + g[
-            pl.ds(pl.multiple_of(half_at + at_, 96), 96), :
-        ]
-        return carry
-
-    lax.fori_loop(0, CORE_ROWS // 96, add_core, 0)
-
-    def first_at(i, digit):
-        return pl.ds(pl.multiple_of(i * GROUP_ROWS + digit * FIRST_ROWS, FIRST_ROWS), FIRST_ROWS)
-
-    one_c = []
-    for i in range(2):
-        for d in range(1, 4):
-            c = send_to(
-                gcore.at[first_at(i, lax.rem(firsts[i] + d, 4))], r1.at[i, firsts[i]],
-                s1s.at[i, d], s1r.at[i, d], digit_peer(me_b, along[i][0], 4, d),
-            )
-            c.start()
-            one_c.append(c)
-        r1[i, firsts[i]] = gcore[first_at(i, firsts[i]), :]
+    second_chunk.core_start()
     share_wait(sbuf_d, me_b, es, er)
     totd = total_of(sbuf_d, NB)
 
     def dy1_nat(p, carry):
-        v = finish(ypos[p][:, 128:256], n1, dpre[p][:, 0:128], totd[0:1], totd[1:2])
+        v = finish(ypos[p][:, 128:256], n1, ob[p], totd[0:1], totd[1:2])
         dnat[0, pl.ds(p, ROWS, stride=POS), :] = v
         return carry
 
@@ -831,77 +970,25 @@
     def late_copy(d):
         to = lax.rem(me_b + d, NB)
         return send_to(
-            lsend.at[late_at(to)], lgot.at[me_b], fs.at[d], fr.at[d], batch_peer(me_b, d)
+            lsend.at[late_at(to)], lgot.at[me_b], fs, fr, batch_peer(me_b, d)
         )
 
     def late_start(d, carry):
         late_copy(d).start()
         return carry
 
-    def late_wait(d, carry):
-        late_copy(d).wait()
-        return carry
-
     lax.fori_loop(1, NB, late_start, 0)
     lgot[me_b] = lsend[late_at(me_b), :]
 
-    for c in one_c:
-        c.wait()
-    two_c = []
-    for i in range(2):
-        r1[i, 0] = total_of(r1.at[i], 4)
-        for d in range(1, 4):
-            to = lax.rem(seconds[i] + d, 4)
-            c = send_to(
-                r1.at[i, 0, pl.ds(pl.multiple_of(to * LAST_ROWS, LAST_ROWS), LAST_ROWS)],
-                r2.at[i, seconds[i]], s2s.at[i, d], s2r.at[i, d],
-                digit_peer(me_b, along[i][1], 4, d),
-            )
-            c.start()
-            two_c.append(c)
-        r2[i, seconds[i]] = r1[
-            i, 0, pl.ds(pl.multiple_of(seconds[i] * LAST_ROWS, LAST_ROWS), LAST_ROWS), :
-        ]
-    for c in two_c:
-        c.wait()
-
-    all_c = []
-    for i in range(2):
-        at_ = pl.ds(
-            pl.multiple_of(
-                half_at + i * GROUP_ROWS + firsts[i] * FIRST_ROWS + seconds[i] * LAST_ROWS,
-                LAST_ROWS,
-            ),
-            LAST_ROWS,
-        )
-        gb_ref[at_, :] = total_of(r2.at[i], 4)
-        for d in range(1, 4):
-            c = send_to(
-                gb_ref.at[at_], gb_ref.at[at_], g1s.at[i, d], g1r.at[i, d],
-                digit_peer(me_b, along[i][1], 4, d),
-            )
-            c.start()
-            all_c.append(c)
-
-    lax.fori_loop(1, NB, late_wait, 0)
+    first_chunk.two_start()
+    second_chunk.one_start()
+    first_chunk.gather_start()
+    share_wait(lgot, me_b, fs, fr)
     late_ref[me_b] = total_of(lgot, NB)
     share_start(late_ref, me_b, hs, hr)
-
-    for c in all_c:
-        c.wait()
-    more_c = []
-    for i in range(2):
-        at_ = pl.ds(
-            pl.multiple_of(half_at + i * GROUP_ROWS + firsts[i] * FIRST_ROWS, FIRST_ROWS),
-            FIRST_ROWS,
-        )
-        for d in range(1, 4):
-            c = send_to(
-                gb_ref.at[at_], gb_ref.at[at_], g2s.at[i, d], g2r.at[i, d],
-                digit_peer(me_b, along[i][0], 4, d),
-            )
-            c.start()
-            more_c.append(c)
+    second_chunk.two_start()
+    first_chunk.spread_start()
+    second_chunk.gather_start()
 
     fix = voxels / (voxels - 1.0)
     for tile, n, gg, gb in (
@@ -912,26 +999,29 @@
         st_ref[:, 128 * tile : 128 * tile + 128] = pack_rows([gg, gb, n[0], n[1] * fix])
     sc_ref[...] = pack_rows([totc[4:5], counted])
 
-    for c in more_c:
-        c.wait()
-    last_c = send_to(
-        gb_ref.at[pl.ds(half_at, CORE_ROWS)], gb_ref.at[pl.ds(half_at, CORE_ROWS)], g3s, g3r, mate
-    )
-    last_c.start()
+    for buf, send, recv in (
+        (sbuf_a, as_, ar), (sbuf_b, bs, br), (sbuf_c, cs, cr), (sbuf_d, es, er), (lgot, fs, fr),
+    ):
+        share_sent(buf, me_b, send, recv)
+    second_chunk.spread_start()
+    first_chunk.mate_rest()
+    second_chunk.mate_rest()
     share_wait(late_ref, me_b, hs, hr)
-    last_c.wait()
+    share_sent(late_ref, me_b, hs, hr)
+    first_chunk.finish()
+    second_chunk.finish()
 
 
 def core(x, lengths, labels, weights, affine):
     vm = pl.BlockSpec(memory_space=pltpu.VMEM)
     sm = pl.BlockSpec(memory_space=pltpu.SMEM)
-    hbm = pl.BlockSpec(memory_space=pl.ANY)
+    hbm = pl.BlockSpec(memory_space=pltpu.HBM)
     dma = pltpu.SemaphoreType.DMA
     vmem = pltpu.VMEM
     return pl.pallas_call(
         core_kernel,
         out_shape=(
-            jax.ShapeDtypeStruct((2 * CORE_ROWS, 128), F32),
+            jax.ShapeDtypeStruct((BULK_ROWS, 128), F32),
             jax.ShapeDtypeStruct((NB, LATE_ROWS, 128), F32),
             jax.ShapeDtypeStruct((8, 384), F32),
             jax.ShapeDtypeStruct((8, 128), F32),
@@ -940,7 +1030,7 @@
         out_specs=(vm,) * 4,
         scratch_shapes=[
             vmem((1, 326144), BF16),
-            *[vmem((FLAT[n], 128), F32) for n in NAMES],
+            *[vmem((1, FLAT[n] * 128), F32) for n in NARROW],
             vmem((2, CIN, 128), F32),
             vmem((CIN, 128), F32),
             vmem((R1, 128), F32),
@@ -952,12 +1042,11 @@
             vmem((8, 384), F32),
             vmem((13 * GPAD, 128), F32),
             vmem((NC, GPAD, GW), BF16),
-            vmem((8, NC, 384, 256), BF16),
+            vmem((NC, W1_ROWS, 256), BF16),
             vmem((2, 8 * GPAD, 128), F32),
             vmem((POS, ROWS, 256), F32),
             vmem((81, ROWS, 128), F32),
             vmem((POS + 1, ROWS, 128), F32),
-            vmem((HALF, ROWS, 128), BF16),
             vmem((NC, HALF, ROWS, 128), BF16),
             vmem((81, ROWS, 256), BF16),
             vmem((POS, ROWS, 256), BF16),
@@ -965,29 +1054,28 @@
             vmem((POS, ROWS, 128), F32),
             vmem((POS, ROWS, 256), F32),
             vmem((81, ROWS, 384), BF16),
-            vmem((NC, HALF, ROWS, 128), F32),
-            vmem((NC, HALF, ROWS, 128), F32),
+            vmem((NC, HALF, ROWS, 128), BF16),
+            vmem((3, HALF, ROWS, 128), BF16),
             vmem((2, 8 * GPAD, 128), F32),
             vmem((2, CIN, 128), F32),
             vmem((R1, 128), F32),
             vmem((4, 256, 128), F32),
-            vmem((2 * CORE_ROWS, 128), F32),
-            vmem((CORE_ROWS, 128), F32),
-            vmem((2, 4, FIRST_ROWS, 128), F32),
-            vmem((2, 4, LAST_ROWS, 128), F32),
+            vmem((BULK_ROWS, 128), F32),
+            *[vmem((32 * n, 128), F32) for _, n in CHUNKS],
+            *[vmem((2, 4, 4 * n, 128), F32) for _, n in CHUNKS],
+            *[vmem((2, 4, n, 128), F32) for _, n in CHUNKS],
             vmem((NB * LATE_ROWS, 128), F32),
             vmem((NB, LATE_ROWS, 128), F32),
             vmem((NC, ROWS, 512), F32),
-            *[vmem((NB, 8, 128), F32)] * 4,
+            *[vmem((NB, n, 128), F32) for n in (8, 2, 8, 2)],
             dma((4,)), dma((7,)), dma((6,)), dma((6,)),
-            *[dma((NC,))] * 6,
-            *[dma((NB,))] * 12,
-            dma, dma,
-            *[dma((2, 4))] * 8,
-            dma, dma,
+            dma((6,)), dma((6,)), dma((NC,)), dma((NC,)), dma((6,)), dma((6,)),
+            *[dma] * 12,
+            dma((2,)), dma((2,)),
+            *[dma((2, 2, 4))] * 10,
         ],
         compiler_params=pltpu.CompilerParams(
-            collective_id=0, has_side_effects=True, vmem_limit_bytes=58 << 20
+            collective_id=0, has_side_effects=True, vmem_limit_bytes=63 << 20
         ),
         name="block",
     )(x, lengths, labels, *weights, affine)
@@ -1001,20 +1089,39 @@
 
 
 def adam_kernel(*refs):
-    gb, late, st, sc, running = refs[0:5]
+    gb_in, late, st, sc, running = refs[0:5]
     w_in, m_in, v_in = refs[5:13], refs[13:21], refs[21:29]
     m_out, v_out, w_out = refs[29:37], refs[37:45], refs[45:53]
     run_out, loss_out, count_out, copies_out = refs[53:57]
     wb, mb, vb = refs[57:64], refs[64:71], refs[71:78]
-    cb, insem, outsem, csem = refs[78:82]
+    cb, gb, insem, gsem, outsem, csem = refs[78:84]
     rates = step_rates()
-    order = (2, 6, 0, 1, 4, 5, 3)
-    ins = {}
-    for i in order:
+    parts = []
+    for i in (4, 3, 5, 1, 0, 6):
+        parts.append((i, 0, FLAT[NAMES[i]]))
+    for first in range(0, FLAT["spatial"], ADAM_ROWS):
+        parts.append((2, first, ADAM_ROWS))
+
+    def at_rows(ref, i, first, count):
+        if NAMES[i] in NARROW:
+            return ref.at[:, pl.ds(first * 128, count * 128)]
+        return ref.at[pl.ds(first, count)]
+
+    ins = []
+    for n, (i, first, count) in enumerate(parts):
+        mine = []
         for kind, (src, dst) in enumerate(((w_in[i], wb[i]), (m_in[i], mb[i]), (v_in[i], vb[i]))):
-            c = pltpu.make_async_copy(src, dst, insem.at[i, kind])
+            c = pltpu.make_async_copy(
+                at_rows(src, i, first, count), at_rows(dst, i, first, count), insem.at[n, kind]
+            )
             c.start()
-            ins[i, kind] = c
+            mine.append(c)
+        if NAMES[i] in BULK:
+            at = pl.ds(BULK[NAMES[i]] + first, count)
+            c = pltpu.make_async_copy(gb_in.at[at], gb.at[at], gsem.at[n])
+            c.start()
+            mine.append(c)
+        ins.append(mine)
 
     starts = []
     total = 0
@@ -1022,46 +1129,61 @@
         starts.append(total * 128)
         total += FLAT[name]
     outs = []
-    for i in order:
+    for n, (i, first, rows) in enumerate(parts):
         name = NAMES[i]
-        rows = FLAT[name]
-        for kind in range(3):
-            ins[i, kind].wait()
-        bulk = name in BULK
-
-        def step(at, count, i=i, name=name, bulk=bulk):
-            if bulk:
+        for c in ins[n]:
+            c.wait()
+
+        def step(at, count, i=i, name=name):
+            if name in BULK:
                 grad = gb[pl.ds(BULK[name] + at, count), :]
             else:
                 grad = late[pl.ds(LATE[name] + at, count), :]
-            rows_ = pl.ds(at, count)
-            m, v, w = adamw(wb[i][rows_, :], mb[i][rows_, :], vb[i][rows_, :], grad, rates[i])
-            mb[i][rows_, :] = m
-            vb[i][rows_, :] = v
-            wb[i][rows_, :] = w
+            wide = pl.ds(pl.multiple_of(at * 128, 128), count * 128)
+            narrow = name in NARROW
+
+            def load(ref):
+                if narrow:
+                    return ref[:, wide].reshape(count, 128)
+                return ref[pl.ds(at, count), :]
+
+            def store(ref, v):
+                if narrow:
+                    ref[:, wide] = v.reshape(1, count * 128)
+                else:
+                    ref[pl.ds(at, count), :] = v
+
+            m, v, w = adamw(load(wb[i]), load(mb[i]), load(vb[i]), grad, rates[i])
+            store(mb[i], m)
+            store(vb[i], v)
+            store(wb[i], w)
             cb[:, pl.ds(pl.multiple_of(starts[i] + at * 128, 128), count * 128)] = w.reshape(
                 1, count * 128
             ).astype(BF16)
 
-        block = 48 if bulk else 24
+        block = {"spatial": 72, "readout": 80, "direct": 48, "pooled": 104, "squeeze": 104}.get(
+            name, 24
+        )
         loops = rows // block
 
-        def body(j, carry, step=step, block=block):
-            step(pl.multiple_of(j * block, block), block)
+        def body(j, carry, step=step, block=block, first=first):
+            step(pl.multiple_of(first + j * block, 8), block)
             return carry
 
         lax.fori_loop(0, loops, body, 0)
-        at, rest = loops * block, rows - loops * block
+        at, rest = first + loops * block, rows - loops * block
         if rest // 8:
             step(at, rest // 8 * 8)
         if rest % 8:
             step(at + rest // 8 * 8, rest % 8)
         for kind, (src, dst) in enumerate(((wb[i], w_out[i]), (mb[i], m_out[i]), (vb[i], v_out[i]))):
-            c = pltpu.make_async_copy(src, dst, outsem.at[i, kind])
+            c = pltpu.make_async_copy(
+                at_rows(src, i, first, rows), at_rows(dst, i, first, rows), outsem.at[n, kind]
+            )
             c.start()
             outs.append(c)
-        at = pl.ds(starts[i], rows * 128)
-        c = pltpu.make_async_copy(cb.at[:, at], copies_out.at[:, at], csem.at[i])
+        at = pl.ds(starts[i] + first * 128, rows * 128)
+        c = pltpu.make_async_copy(cb.at[:, at], copies_out.at[:, at], csem.at[n])
         c.start()
         outs.append(c)
 
@@ -1083,23 +1205,26 @@
 
 def adam(gb, late, st, sc, running, masters, firsts, seconds):
     vm = pl.BlockSpec(memory_space=pltpu.VMEM)
-    hbm = pl.BlockSpec(memory_space=pl.ANY)
+    hbm = pl.BlockSpec(memory_space=pltpu.HBM)
     dma = pltpu.SemaphoreType.DMA
-    flats = [jax.ShapeDtypeStruct((FLAT[n], 128), F32) for n in NAMES]
+    shapes = [(1, FLAT[n] * 128) if n in NARROW else (FLAT[n], 128) for n in NAMES]
+    flats = [jax.ShapeDtypeStruct(shape, F32) for shape in shapes]
     small = jax.ShapeDtypeStruct((2, 316), F32)
     total = sum(FLAT[n] for n in NAMES) * 128
     one = jax.ShapeDtypeStruct((1, 1), F32)
     specs = [hbm] * 7 + [vm]
-    buffers = [pltpu.VMEM((FLAT[n], 128), F32) for n in NAMES]
+    buffers = [pltpu.VMEM(shape, F32) for shape in shapes]
+    count = 6 + FLAT["spatial"] // ADAM_ROWS
     return pl.pallas_call(
         adam_kernel,
         out_shape=[*(flats + [small]) * 3, small, one, one, jax.ShapeDtypeStruct((1, total), BF16)],
-        in_specs=[vm] * 5 + specs * 3,
+        in_specs=[hbm] + [vm] * 4 + specs * 3,
         out_specs=[*specs * 3, vm, vm, vm, hbm],
         scratch_shapes=[
-            *buffers * 3, pltpu.VMEM((1, total), BF16), dma((7, 3)), dma((7, 3)), dma((7,)),
+            *buffers * 3, pltpu.VMEM((1, total), BF16), pltpu.VMEM((BULK_ROWS, 128), F32),
+            dma((count, 3)), dma((count,)), dma((count, 3)), dma((count,)),
         ],
-        compiler_params=pltpu.CompilerParams(vmem_limit_bytes=40 << 20),
+        compiler_params=pltpu.CompilerParams(vmem_limit_bytes=63 << 20),
         name="adamw",
     )(gb, late, st, sc, running, *masters, *firsts, *seconds)
 
@@ -1119,13 +1244,14 @@
         second_direct, second_squeeze, second_spatial, second_shrink, second_volume,
         second_pooled, second_readout, second_affine,
     ]
-    def rows(flat):
-        return flat.reshape(-1, 128)
+    def rows(flat, name):
+        return flat if name in NARROW else flat.reshape(-1, 128)
 
     masters, firsts, seconds = (
-        [rows(a) for a in group[:7]] + [group[7]] for group in (masters, firsts, seconds)
+        [rows(a, n) for a, n in zip(group, NAMES)] + [group[7]]
+        for group in (masters, firsts, seconds)
     )
-    gb, late, st, sc = core(features, lengths, labels, masters[:7], affine)
+    gb, late, st, sc = core(features, lengths, labels.T, masters[:7], affine)
     out = adam(gb, late.reshape(NB * LATE_ROWS, 128), st, sc, running, masters, firsts, seconds)
     flat_out = [a if i % 8 == 7 else a.reshape(1, -1) for i, a in enumerate(out[:24])]
     return (*flat_out, out[24], out[25].reshape(()), out[26].reshape(()), out[27])

time: 197 us -> 153 us (0.78)
  Pallas kernels: 170 us -> 151 us
  local copies, waits for them, and re-layouts: 16.1 us -> 0 us
  other arithmetic: 8.02 us -> 0 us
    pallas_call x1, Pallas kernels: 156 us -> 139 us  [core(): pl.pallas_call(core_kernel, out_shape=(jax.ShapeDtypeStruct((BULK_ROWS, 1...]
    unnamed x53 -> x0, local copies, waits for them, and re-layouts: 14.3 us -> none
    unnamed x6 -> x0, other arithmetic: 8.02 us -> none
where the time goes in v3:
time: 153 us; the launch traced here: 151 us
  Pallas kernels  151 us (99%)
    pallas_call x1, Pallas kernels, core(): pl.pallas_call(core_kernel, out_shape=(jax.ShapeDtypeStruct((BULK_ROWS, 1...  139 us
    pallas_call x1, Pallas kernels, adam(): pl.pallas_call(adam_kernel, out_shape=[*(flats + [small]) * 3, small, one...  12.1 us

profile of v3, /device:TPU:0, one launch (start us, length us, event | category | flops | bytes accessed | tf_op | source)
XLA Modules:
  0.0 151.4 jit_solution(12778458878536215173)
XLA Ops:
  0.7 138.7 %block.1 = (f32[6144,128]{1,0:T(8,128)}, f32[32,16,128]{2,1,0:T(8,128)}, f32[8,384]{1,0:T(8,128)}, f32[8,128]{1,0:T(8,128)}) custom-call(bf16[1,326144]{1,0:T(2,128)(2,1)} %x_hbm.1, s32[8]{0:T(128)} %len_ref.1, s32[4,8]{1,0:T(4,128)} %bitcast.55, f32[624,128]{1,0:T(8,128)} %bitcast.40, f32[312,128]{1,0:T(8,128)} %bitcast.42, f32[3888,128]{1,0:T(8,128)} %bitcast.34, ...), custom_call_target="tpu_custom_call" | custom-call | tf_op jit(solution)/shard_map/block/pallas_call | solution.py:1021
  139.4 12.1 %adamw.1 = (f32[624,128]{1,0:T(8,128)}, f32[312,128]{1,0:T(8,128)}, f32[3888,128]{1,0:T(8,128)}, f32[1,9984]{1,0:T(1,128)}, f32[1,41472]{1,0:T(1,128)}, /*index=...) custom-call(f32[6144,128]{1,0:T(8,128)} %get-tuple-element.60.refs_0, ...), custom_call_target="tpu_custom_call" | custom-call | tf_op jit(solution)/shard_map/adamw/pallas_call | solution.py:1218

commit v4 on v3

--- a/solution.py
+++ b/solution.py
@@ -34,13 +34,18 @@
 FLAT = {"direct": 624, "squeeze": 312, "spatial": 3888, "shrink": 78, "volume": 324, "pooled": 208,
         "readout": 800}
 NAMES = ("direct", "squeeze", "spatial", "shrink", "volume", "pooled", "readout")
-BULK = {"spatial": 0, "volume": 3888, "direct": 4216, "pooled": 4840, "readout": 5048}
+HELD = {"spatial": 0, "volume": 3888, "direct": 4216, "pooled": 4840, "readout": 5048}
+BULK = {"volume": 4720, "direct": 5120, "pooled": 5744, "readout": 1728}
+EARLY_TAPS = 4
 NARROW = ("shrink", "volume")
 LATE = {"squeeze": 0, "shrink": 312}
-CHUNKS = ((0, 64), (4096, 32))
+CHUNKS = ((0, 40), (2560, 40))
+DIRECT_AT = 5120
+DIRECT_ROWS = 32
 BULK_ROWS = 6144
 LATE_ROWS = 16
 ADAM_ROWS = 648
+ADAM_ORDER = (3, 1, 5, 0, 6, 4)
 
 EPS = 1e-05
 BETA_ONE = 0.5
@@ -164,6 +169,10 @@
 
 def lanes_of(v):
     return lax.broadcasted_iota(jnp.int32, v, 1)
+
+
+def tap_rows(dt, q):
+    return q * 432 + jnp.where(q >= EARLY_TAPS, 832, 0) + dt * 144
 
 
 def prepare_w1(flat, wn, wk, w1p):
@@ -270,26 +279,27 @@
     gb_ref, late_ref, st_ref, sc_ref,
     x_ref, n_shrink, n_volume,
     wn, wk, tb, vn, rn, wc_ref, wct_ref, r_ref, aff_ref,
-    xf, xg, w1p, ynat, ypos, box, ob, got, apad, acol, at, y2, dpre, dypad, dm, dgot, dnat,
-    gw1_ref, gq, gr, g, gca, gcb, r1a, r1b, r2a, r2b, lsend, lgot,
+    xf, xg, xt, cols, w1p, ynat, ypos, box, ob, got, apad, acol, at, y2, dpre, dypad, dm, dgot, dnat,
+    gw1_ref, gq, gr, g, gca, gcb, gcc, r1a, r1b, r2a, r2b, rc, lsend, lgot, psend, pgot,
     lbuf, sbuf_a, sbuf_b, sbuf_c, sbuf_d,
     xin, win, xs, xr, ms, mr, ls, lr, ds_, dr,
     as_, ar, bs, br, cs, cr, es, er, fs, fr, hs, hr,
-    co_s, co_r, s1s, s1r, s2s, s2r, g1s, g1r, g2s, g2r, g3s, g3r,
+    co_s, co_r, s1s, s1r, s2s, s2r, g1s, g1r, g2s, g2r, g3s, g3r, ps, pr, d1s, d1r, d2s, d2r, d3s, d3r,
 ):
     me_b = lax.axis_index("batch")
     me = lax.axis_index("chan")
 
     barrier = pltpu.get_barrier_semaphore()
 
-    cuts = [0, 91 * 1024, 182 * 1024, 250 * 1024, 326144]
+    loops = (0, 104, 182, 260, 318)
+    cuts = [1024 * n for n in loops[:4]] + [326144]
     x_in = []
     for i in range(4):
         at_ = pl.ds(cuts[i], cuts[i + 1] - cuts[i])
         c = pltpu.make_async_copy(x_hbm.at[:, at_], x_ref.at[:, at_], xin.at[i])
         c.start()
         x_in.append(c)
-    flat = {n: g.at[at_ : at_ + FLAT[n]] for n, at_ in BULK.items()}
+    flat = {n: g.at[at_ : at_ + FLAT[n]] for n, at_ in HELD.items()}
     flat.update({n: lsend.at[at_ : at_ + FLAT[n]] for n, at_ in LATE.items()})
     w_in = []
     for i, (src, name) in enumerate(
@@ -318,35 +328,37 @@
 
     right, left = chan_peer(me, 1), chan_peer(me, NC - 1)
     left_i, right_i = lax.rem(me + NC - 1, NC), lax.rem(me + 1, NC)
-    split = 112
-
-    def part(who, low):
-        return xg.at[who, 0:split] if low else xg.at[who, split:GPAD]
-
-    hops = [
-        send_to(part(me, low), part(me, low), xs.at[i], xr.at[i], to)
-        for i, (low, to) in enumerate([(True, right), (True, left), (False, right), (False, left)])
-    ]
+    bounds = (0, 64, 112, 160, GPAD)
+
+    def part(who, i):
+        return xg.at[who, bounds[i] : bounds[i + 1]]
+
+    def hop(i, side):
+        return send_to(
+            part(me, i), part(me, i), xs.at[4 * side + i], xr.at[4 * side + i], (right, left)[side]
+        )
+
+    def pass_on(i):
+        who, to = ((left_i, right), (right_i, left))[i // 2]
+        return send_to(part(who, i), part(who, i), xs.at[8 + i], xr.at[8 + i], to)
+
     xf[pl.ds(2548, 2704 - 2548), :] = jnp.zeros((2704 - 2548, 128), F32)
-    for i in range(2):
+    for i in range(4):
         x_in[i].wait()
-        lax.fori_loop(91 * i, 91 * i + 91, flat_rows, 0, unroll=7)
-    for i in range(13):
-        xg[me, 0:split, 128 * i : 128 * i + 128] = xf[pl.ds(i, split, stride=13), :].astype(BF16)
-    pl.semaphore_wait(barrier, NB - 1 + NC - 1)
-    hops[0].start()
-    hops[1].start()
-    x_in[2].wait()
-    lax.fori_loop(182, 250, flat_rows, 0, unroll=4)
-    x_in[3].wait()
-    lax.fori_loop(250, 318, flat_rows, 0, unroll=4)
-    xf[pl.ds(2544, 4), :] = x_ref[:, 318 * 1024 : 318 * 1024 + 512].astype(F32).reshape(4, 128)
-    for i in range(13):
-        xg[me, split:GPAD, 128 * i : 128 * i + 128] = xf[
-            pl.ds(13 * split + i, GPAD - split, stride=13), :
-        ].astype(BF16)
-    hops[2].start()
-    hops[3].start()
+        lax.fori_loop(loops[i], loops[i + 1], flat_rows, 0, unroll=(8, 6, 6, 2)[i])
+        if i == 3:
+            xf[pl.ds(2544, 4), :] = x_ref[:, 318 * 1024 : 318 * 1024 + 512].astype(F32).reshape(
+                4, 128
+            )
+        low, count = bounds[i], bounds[i + 1] - bounds[i]
+        for t in range(13):
+            xg[me, low : low + count, 128 * t : 128 * t + 128] = xf[
+                pl.ds(13 * low + t, count, stride=13), :
+            ].astype(BF16)
+        if i == 0:
+            pl.semaphore_wait(barrier, NB - 1 + NC - 1)
+        for side in range(2):
+            hop(i, side).start()
 
     rowi = lax.broadcasted_iota(jnp.int32, (ROWS, 128), 0)
     lane = lax.broadcasted_iota(jnp.int32, (ROWS, 128), 1)
@@ -386,30 +398,43 @@
         box[i] = jnp.zeros((ROWS, 128), F32)
         return carry
 
-    lax.fori_loop(0, 81, zero_pad, 0)
+    lax.fori_loop(0, 81, zero_pad, 0, unroll=9)
     dnat[...] = jnp.zeros_like(dnat)
     prepare_conv(flat, tb, vn, wc_ref, wct_ref)
 
-    hops[0].wait_recv()
-    f0 = send_to(part(left_i, True), part(left_i, True), xs.at[4], xr.at[4], right)
-    f0.start()
-    hops[3].wait_recv()
-    f1 = send_to(part(right_i, False), part(right_i, False), xs.at[5], xr.at[5], left)
-    f1.start()
-    hops[1].wait_recv()
-    hops[2].wait_recv()
-    f0.wait()
-    f1.wait()
-    for c in hops:
-        c.wait_send()
+    for i in range(4):
+        hop(i, i // 2).wait_recv()
+        pass_on(i).start()
+    for i in range(4):
+        hop(i, 1 - i // 2).wait_recv()
+
+    far_i = lax.rem(me + 2, NC)
+
+    def one_by_one(r, blocks):
+        first, off, lanes = window_of(r)
+        acc = None
+        for k in blocks:
+            v = dot(
+                xg[k, :, first : first + lanes], w1p[k, SHIFT - off : SHIFT - off + lanes, :]
+            )
+            acc = v if acc is None else acc + v
+        return acc
 
     for r in range(8):
-        first, off, lanes = window_of(r)
-        acc = jnp.zeros((GPAD, 256), F32)
-        for k in range(NC):
-            acc = acc + dot(xg[k, :, first : first + lanes], w1p[k, SHIFT - off : SHIFT - off + lanes, :])
-        ynat[0, pl.ds(r, GPAD, stride=8), :] = acc[:, 0:128]
-        ynat[1, pl.ds(r, GPAD, stride=8), :] = acc[:, 128:256]
+        acc = one_by_one(r, (me, left_i, right_i))
+        for t in range(2):
+            ynat[t, pl.ds(r, GPAD, stride=8), :] = acc[:, 128 * t : 128 * t + 128]
+    for i in range(4):
+        pass_on(i).wait_recv()
+    for r in range(8):
+        acc = one_by_one(r, (far_i,))
+        for t in range(2):
+            at_ = pl.ds(r, GPAD, stride=8)
+            ynat[t, at_, :] = ynat[t, at_, :] + acc[:, 128 * t : 128 * t + 128]
+    for i in range(4):
+        pass_on(i).wait_send()
+        for side in range(2):
+            hop(i, side).wait_send()
 
     def padded(p):
         return (p // SIDE + 1) * 9 + lax.rem(p, SIDE) + 1
@@ -422,7 +447,7 @@
         box[padded(p)] = mz + prev_t(mz) + next_t(mz)
         return carry
 
-    lax.fori_loop(0, POS, to_pos, 0)
+    lax.fori_loop(0, POS, to_pos, 0, unroll=7)
 
     def spread(p):
         h, w = p // SIDE, lax.rem(p, SIDE)
@@ -449,7 +474,7 @@
 
     zero256 = jnp.zeros((ROWS, 256), F32)
     zero128 = jnp.zeros((ROWS, 128), F32)
-    s1, s2 = lax.fori_loop(0, POS, pool, (zero256, zero256))
+    s1, s2 = lax.fori_loop(0, POS, pool, (zero256, zero256), unroll=7)
 
     def col(v):
         return jnp.sum(v, axis=0, keepdims=True)
@@ -462,6 +487,10 @@
         [col(s1[:, 0:128]), col(s1[:, 128:256]), col(s2[:, 0:128]), col(s2[:, 128:256]), col(mask)]
     )
     share_start(sbuf_a, me_b, as_, ar)
+    cols[...] = jnp.zeros_like(cols)
+    for k in range(NC):
+        xt[k, :, GPAD:256] = jnp.zeros((GW, 256 - GPAD), BF16)
+        xt[k, :, 0:GPAD] = jnp.transpose(xg[k])
     share_wait(sbuf_a, me_b, as_, ar)
     tot = total_of(sbuf_a, NB)
     counted = tot[4:5, :]
@@ -489,14 +518,14 @@
         ob[p] = (mask * (pre * sig))
         return carry
 
-    lax.fori_loop(0, POS, act1, 0)
+    lax.fori_loop(0, POS, act1, 0, unroll=7)
     ob[POS] = zero128
 
     def to_msg(p, carry):
         got[me, p] = jnp.where(low_half, ob[p], pltpu.roll(ob[p + HALF], 64, 1)).astype(BF16)
         return carry
 
-    lax.fori_loop(0, HALF, to_msg, 0)
+    lax.fori_loop(0, HALF, to_msg, 0, unroll=5)
     near = 12
 
     def half(who, low):
@@ -512,8 +541,61 @@
         _, pre, sig = forward(ypos[p][:, 0:128], n0)
         return carry + mask * (pre * sig)
 
-    feat0 = lax.fori_loop(0, POS, act0, zero128)
-
+    feat0 = lax.fori_loop(0, POS, act0, zero128, unroll=7)
+
+    def products(width):
+        for r in range(8):
+            for t in range(width // 128):
+                cols[r, 0:GPAD, 128 * t : 128 * t + 128] = dnat[
+                    t, pl.ds(r, GPAD, stride=8), :
+                ].astype(BF16)
+        rhs = cols[:, :, 0:width].reshape(8 * 256, width)
+        for k in range(NC):
+            lhs = jnp.concatenate([xt[k, CB * r : CB * r + CB, :] for r in range(8)], axis=1)
+            yield slice(k * CB, (k + 1) * CB), dot(lhs, rhs)
+
+    def put_late(dst):
+        lane104, lane26 = lanes_of((104, 128)), lanes_of((26, 128))
+        parts = [(gw1_ref[1, pl.ds(j, 104, stride=8), :], 0, 48 * j, 48) for j in range(8)]
+        for i, v in enumerate(joined(parts, lane104, 3)):
+            dst[pl.ds(LATE["squeeze"] + i, 104, stride=3), :] = v
+        parts = [(gw1_ref[1, pl.ds(j, 26, stride=32), :], 48, 12 * j, 12) for j in range(32)]
+        for i, v in enumerate(joined(parts, lane26, 3)):
+            dst[pl.ds(LATE["shrink"] + i, 26, stride=3), :] = v
+
+    def late_at(i):
+        return pl.ds(pl.multiple_of(i * LATE_ROWS, LATE_ROWS), LATE_ROWS)
+
+    def normed_nat(p, carry):
+        normed, _, _ = forward(ypos[p][:, 128:256], n1)
+        v = jnp.where(lane < 60, normed * mask, jnp.where(lane == 64, mask, 0.0))
+        dnat[0, pl.ds(p, ROWS, stride=POS), :] = v
+        return carry
+
+    def early_products():
+        lax.fori_loop(0, POS, normed_nat, 0, unroll=7)
+        for at_, v in products(128):
+            gw1_ref[1, at_, :] = v
+        psend[...] = jnp.zeros_like(psend)
+        put_late(psend.at[0])
+        for k in range(NC):
+            at_ = slice(k * CB, (k + 1) * CB)
+            gw1_ref[1, at_, :] = jnp.broadcast_to(gw1_ref[1, at_, 64:65], (CB, 128))
+        put_late(psend.at[1])
+
+    def early_copy(d):
+        to = lax.rem(me_b + d, NB)
+        return send_to(psend.at[:, late_at(to)], pgot.at[me_b], ps, pr, batch_peer(me_b, d))
+
+    def early_start():
+        def one(d, carry):
+            early_copy(d).start()
+            return carry
+
+        lax.fori_loop(1, NB, one, 0)
+        pgot[me_b] = psend[:, late_at(me_b), :]
+
+    early_products()
     for i, (who, low, to) in enumerate([(left_i, True, right), (right_i, False, left)]):
         ms_c[i].wait_recv()
         c = send_to(half(who, low), half(who, low), ms.at[4 + i], mr.at[4 + i], to)
@@ -541,7 +623,9 @@
 
         return carry
 
-    lax.fori_loop(0, HALF, unpack, 0)
+    lax.fori_loop(0, HALF, unpack, 0, unroll=5)
+
+    early_start()
 
     def conv(h, carry):
         s1, s2 = carry
@@ -571,7 +655,7 @@
         _, pre, sig = forward(y2[p], n2)
         return carry + mask * (pre * sig)
 
-    feat2 = lax.fori_loop(0, POS, act2, zero128)
+    feat2 = lax.fori_loop(0, POS, act2, zero128, unroll=7)
     feature = (jnp.concatenate([feat0, feat2], axis=1) / float(POS)).astype(BF16)
     lbuf[me] = dot(feature, r_ref[...])
     ls_c = []
@@ -612,7 +696,7 @@
         dpre[p] = jnp.concatenate([d0, d2], axis=1)
         return g0 + d0 * m0, b0 + d0, g2 + d2 * m2, b2 + d2
 
-    g0, b0, g2, b2 = lax.fori_loop(0, POS, back02, (zero128,) * 4)
+    g0, b0, g2, b2 = lax.fori_loop(0, POS, back02, (zero128,) * 4, unroll=7)
     loss_row = jnp.broadcast_to(jnp.sum(loss_rows, axis=0, keepdims=True), (1, 128))
     sbuf_c[me_b] = pack_rows([col(g0), col(b0), col(g2), col(b2), loss_row])
     share_start(sbuf_c, me_b, cs, cr)
@@ -647,55 +731,191 @@
         dypad[padded(p)] = jnp.concatenate([next_t(v), v, prev_t(v)], axis=1).astype(BF16)
         return carry
 
-    lax.fori_loop(0, POS, dy2_at, 0)
-
-    def conv_back(h, carry):
-        acc = jnp.zeros((SIDE * ROWS, 256), F32)
-        for q in range(9):
-            dh, dw = divmod(q, 3)
-            lhs = dypad[pl.ds((h + 2 - dh) * 9 + 2 - dw, SIDE)].reshape(SIDE * ROWS, 384)
-            acc = acc + dot(lhs, wct_ref[q])
-        for t in range(2):
-            ynat[t, pl.ds(pl.multiple_of(h * SIDE * ROWS, SIDE * ROWS), SIDE * ROWS), :] = acc[
-                :, 128 * t : 128 * t + 128
-            ]
-        return carry
-
-    lax.fori_loop(0, SIDE, conv_back, 0)
-
-    def to_dm(p, carry):
-        for j in range(NC):
-            a = ynat[j // 2, pl.ds(pl.multiple_of(p * ROWS, ROWS), ROWS), :]
-            b = ynat[j // 2, pl.ds(pl.multiple_of((p + HALF) * ROWS, ROWS), ROWS), :]
-            if j % 2 == 0:
-                dm[j, p] = jnp.where(low_half, a, pltpu.roll(b, 64, 1)).astype(BF16)
-            else:
-                dm[j, p] = jnp.where(low_half, pltpu.roll(a, 64, 1), b).astype(BF16)
-        return carry
-
-    for t in range(2):
-        ynat[t, pl.ds(VOX, ROWS), :] = zero128
-    lax.fori_loop(0, HALF, to_dm, 0)
-    far_i = lax.rem(me + 2, NC)
-    lo_, hi_ = pl.ds(0, near), pl.ds(near, HALF - near)
-
-    def far_copy(i):
-        rows_, to = ((lo_, right), (hi_, left))[i]
-        return send_to(dm.at[far_i, rows_], dgot.at[2, rows_], ds_.at[i], dr.at[i], to)
-
-    def near_copy(i):
-        who, rows_, to, slot = (
-            (right_i, hi_, right, 0), (left_i, lo_, left, 1), (right_i, lo_, right, 0),
-            (left_i, hi_, left, 1),
-        )[i]
-        return send_to(
-            dm.at[who, rows_], dgot.at[slot, rows_], ds_.at[2 + i], dr.at[2 + i], to
-        )
-
-    far_c = [far_copy(i) for i in range(2)]
-    near_c = [near_copy(i) for i in range(4)]
-    for c in far_c + near_c[0:2]:
-        c.start()
+    lax.fori_loop(0, POS, dy2_at, 0, unroll=7)
+
+    core_i = lax.rem(me_b, 2)
+    mate = digit_peer(me_b, 1, 2, 1)
+    along = ((2, 8), (8, 2))
+    digits = [[digit_of(me_b, along[i][s], 4) for i in range(2)] for s in range(2)]
+
+    class Chunk:
+        def __init__(self, index):
+            self.base, self.last = CHUNKS[index]
+            self.k = index
+            self.first = 4 * self.last
+            self.group = 4 * self.first
+            self.half = 2 * self.group
+            self.own = pl.multiple_of(self.base + core_i * self.half, self.last)
+            self.r1 = (r1a, r1b)[index]
+            self.r2 = (r2a, r2b)[index]
+            self.gc = (gca, gcb)[index]
+
+        def rows(self, at, count):
+            return pl.ds(pl.multiple_of(at, self.last), count)
+
+        def core_start(self):
+            theirs = self.rows(self.base + (1 - core_i) * self.half, self.half)
+            self.c0 = send_to(g.at[theirs], self.gc, co_s.at[self.k], co_r.at[self.k], mate)
+            self.c0.start()
+
+        def one_start(self):
+            self.c0.wait()
+            n = self.first
+
+            def add(i, carry):
+                at_ = self.rows(i * n, n)
+                self.gc[at_, :] = self.gc[at_, :] + g[self.rows(self.own + i * n, n), :]
+                return carry
+
+            lax.fori_loop(0, self.half // n, add, 0)
+            self.c1 = []
+            for i in range(2):
+                mine = digits[0][i]
+                for d in range(1, 4):
+                    to = lax.rem(mine + d, 4)
+                    c = send_to(
+                        self.gc.at[self.rows(i * self.group + to * self.first, self.first)],
+                        self.r1.at[i, mine], s1s.at[self.k, i, d], s1r.at[self.k, i, d],
+                        digit_peer(me_b, along[i][0], 4, d),
+                    )
+                    c.start()
+                    self.c1.append(c)
+                self.r1[i, mine] = self.gc[
+                    self.rows(i * self.group + mine * self.first, self.first), :
+                ]
+
+        def two_start(self):
+            for c in self.c1:
+                c.wait()
+            self.c2 = []
+            for i in range(2):
+                mine = digits[1][i]
+                self.r1[i, 0] = total_of(self.r1.at[i], 4)
+                for d in range(1, 4):
+                    to = lax.rem(mine + d, 4)
+                    c = send_to(
+                        self.r1.at[i, 0, self.rows(to * self.last, self.last)],
+                        self.r2.at[i, mine], s2s.at[self.k, i, d], s2r.at[self.k, i, d],
+                        digit_peer(me_b, along[i][1], 4, d),
+                    )
+                    c.start()
+                    self.c2.append(c)
+                self.r2[i, mine] = self.r1[i, 0, self.rows(mine * self.last, self.last), :]
+
+        def gather_start(self):
+            for c in self.c2:
+                c.wait()
+            self.c3 = []
+            for i in range(2):
+                at_ = self.rows(
+                    self.own + i * self.group + digits[0][i] * self.first
+                    + digits[1][i] * self.last,
+                    self.last,
+                )
+                gb_ref[at_, :] = total_of(self.r2.at[i], 4)
+                for d in range(1, 4):
+                    c = send_to(
+                        gb_ref.at[at_], gb_ref.at[at_], g1s.at[self.k, i, d],
+                        g1r.at[self.k, i, d], digit_peer(me_b, along[i][1], 4, d),
+                    )
+                    c.start()
+                    self.c3.append(c)
+
+        def spread_start(self):
+            for c in self.c3:
+                c.wait()
+            self.c4 = []
+            self.c5 = []
+            for i in range(2):
+                mine = digits[0][i]
+                at_ = self.rows(self.own + i * self.group + mine * self.first, self.first)
+                for d in range(1, 4):
+                    c = send_to(
+                        gb_ref.at[at_], gb_ref.at[at_], g2s.at[self.k, i, d],
+                        g2r.at[self.k, i, d], digit_peer(me_b, along[i][0], 4, d),
+                    )
+                    c.start()
+                    self.c4.append((c, i, d))
+                self.mate_start(i, 0)
+
+        def mate_start(self, i, d):
+            digit = lax.rem(digits[0][i] - d + 4, 4)
+            at_ = self.rows(self.own + i * self.group + digit * self.first, self.first)
+            c = send_to(
+                gb_ref.at[at_], gb_ref.at[at_], g3s.at[self.k, i, d], g3r.at[self.k, i, d], mate
+            )
+            c.start()
+            self.c5.append(c)
+
+        def mate_rest(self):
+            for c, i, d in self.c4:
+                c.wait_recv()
+                self.mate_start(i, d)
+
+        def finish(self):
+            for c, i, d in self.c4:
+                c.wait_send()
+            for c in self.c5:
+                c.wait()
+
+    chip = me_b // 2
+
+    def chip_peer(d):
+        return {"batch": lax.rem(chip + d, 16) * 2 + core_i}
+
+    class Direct:
+        half = 16 * DIRECT_ROWS
+
+        def rows(self, at_, count=DIRECT_ROWS):
+            return pl.ds(pl.multiple_of(at_, DIRECT_ROWS), count)
+
+        def core_start(self):
+            theirs = self.rows(DIRECT_AT + (1 - core_i) * self.half, self.half)
+            self.c0 = send_to(g.at[theirs], gcc, co_s.at[2], co_r.at[2], mate)
+            self.c0.start()
+
+        def one_start(self):
+            self.c0.wait()
+            own = DIRECT_AT + core_i * self.half
+            gcc[...] = gcc[...] + g[self.rows(own, self.half), :]
+
+            def one(d, carry):
+                to = lax.rem(chip + d, 16)
+                send_to(
+                    gcc.at[self.rows(to * DIRECT_ROWS)], rc.at[chip], d1s, d1r, chip_peer(d)
+                ).start()
+                return carry
+
+            lax.fori_loop(1, 16, one, 0)
+            rc[chip] = gcc[self.rows(chip * DIRECT_ROWS), :]
+
+        def all_of(self, send, recv):
+            some = rc.at[pl.ds(0, 15)]
+            return send_to(some, some, send, recv, chip_peer(1))
+
+        def two_start(self):
+            self.all_of(d1s, d1r).wait_recv()
+            mine = self.rows(DIRECT_AT + core_i * self.half + chip * DIRECT_ROWS)
+            gb_ref[mine, :] = total_of(rc, 16)
+
+            def one(d, carry):
+                send_to(gb_ref.at[mine], gb_ref.at[mine], d2s, d2r, chip_peer(d)).start()
+                return carry
+
+            lax.fori_loop(1, 16, one, 0)
+
+        def mate_rest(self):
+            self.all_of(d2s, d2r).wait_recv()
+            mine = self.rows(DIRECT_AT + core_i * self.half, self.half)
+            self.c3 = send_to(gb_ref.at[mine], gb_ref.at[mine], d3s, d3r, mate)
+            self.c3.start()
+
+        def finish(self):
+            self.all_of(d1s, d1r).wait_send()
+            self.all_of(d2s, d2r).wait_send()
+            self.c3.wait()
+
+    a_, b_, c_ = Chunk(0), Chunk(1), Direct()
 
     def grad_conv(q, carry):
         dh = q // 3
@@ -716,13 +936,96 @@
                     64 * j + 48 : 64 * j + 60, 128 * dt : 128 * dt + 128
                 ]
 
-            def put(i, v, tap=tap):
-                g[pl.ds(BULK["spatial"] + tap * 144 + i, 48, stride=3), :] = v
+            def put(i, v, base=tap_rows(dt, q)):
+                g[pl.ds(base + i, 48, stride=3), :] = v
 
             flatten_96(lambda j: gq[pl.ds(j, 48, stride=4), :], 48, put)
         return carry
 
-    lax.fori_loop(0, 4, grad_conv, 0)
+    lax.fori_loop(0, EARLY_TAPS, grad_conv, 0)
+    a_.core_start()
+    lax.fori_loop(EARLY_TAPS, 9, grad_conv, 0)
+    g[BULK["volume"] : BULK["volume"] + 324, :] = flatten_32(
+        lambda j: vn[pl.ds(j, 324, stride=4), :], 324
+    )
+
+    b_.core_start()
+    a_.one_start()
+
+    def conv_back(h, carry):
+        acc = jnp.zeros((SIDE * ROWS, 256), F32)
+        for q in range(9):
+            dh, dw = divmod(q, 3)
+            lhs = dypad[pl.ds((h + 2 - dh) * 9 + 2 - dw, SIDE)].reshape(SIDE * ROWS, 384)
+            acc = acc + dot(lhs, wct_ref[q])
+        for t in range(2):
+            ynat[t, pl.ds(pl.multiple_of(h * SIDE * ROWS, SIDE * ROWS), SIDE * ROWS), :] = acc[
+                :, 128 * t : 128 * t + 128
+            ]
+        return carry
+
+    lax.fori_loop(0, 5, conv_back, 0)
+    b_.one_start()
+    lax.fori_loop(5, SIDE, conv_back, 0)
+
+    def to_dm(p, carry):
+        for j in range(NC):
+            a = ynat[j // 2, pl.ds(pl.multiple_of(p * ROWS, ROWS), ROWS), :]
+            b = ynat[j // 2, pl.ds(pl.multiple_of((p + HALF) * ROWS, ROWS), ROWS), :]
+            if j % 2 == 0:
+                dm[j, p] = jnp.where(low_half, a, pltpu.roll(b, 64, 1)).astype(BF16)
+            else:
+                dm[j, p] = jnp.where(low_half, pltpu.roll(a, 64, 1), b).astype(BF16)
+        return carry
+
+    for t in range(2):
+        ynat[t, pl.ds(VOX, ROWS), :] = zero128
+    lax.fori_loop(0, HALF, to_dm, 0, unroll=5)
+    lo_, hi_ = pl.ds(0, near), pl.ds(near, HALF - near)
+
+    def far_copy(i):
+        rows_, to = ((lo_, right), (hi_, left))[i]
+        return send_to(dm.at[far_i, rows_], dgot.at[2, rows_], ds_.at[i], dr.at[i], to)
+
+    def near_copy(i):
+        who, rows_, to, slot = (
+            (right_i, hi_, right, 0), (left_i, lo_, left, 1), (right_i, lo_, right, 0),
+            (left_i, hi_, left, 1),
+        )[i]
+        return send_to(
+            dm.at[who, rows_], dgot.at[slot, rows_], ds_.at[2 + i], dr.at[2 + i], to
+        )
+
+    far_c = [far_copy(i) for i in range(2)]
+    near_c = [near_copy(i) for i in range(4)]
+    for c in far_c + near_c[0:2]:
+        c.start()
+
+    a_.two_start()
+
+    def dy0_at(p, carry):
+        v = finish(ypos[p][:, 0:128], n0, dpre[p][:, 0:128], totc[0:1], totc[1:2])
+        v = v.astype(BF16).astype(F32)
+        h, w = p // SIDE, lax.rem(p, SIDE)
+        n_h = 3 - (h == 0).astype(jnp.int32) - (h == SIDE - 1).astype(jnp.int32)
+        n_w = 3 - (w == 0).astype(jnp.int32) - (w == SIDE - 1).astype(jnp.int32)
+        share = v / jnp.maximum(n_t * (n_h * n_w).astype(F32), 1.0)
+        box[padded(p)] = share + prev_t(share) + next_t(share)
+        ypos[p, :, 0:128] = v
+        return carry
+
+    lax.fori_loop(0, POS, dy0_at, 0, unroll=7)
+
+    def dy0_nat(p, carry):
+        acc, _ = spread(p)
+        v = jnp.where(is_pool, acc * mask, ypos[p][:, 0:128])
+        lowv = v - v.astype(BF16).astype(F32)
+        dnat[0, pl.ds(p, ROWS, stride=POS), :] = v
+        dnat[1, pl.ds(p, ROWS, stride=POS), :] = lowv
+        return carry
+
+    lax.fori_loop(0, POS, dy0_nat, 0, unroll=7)
+
     for c in far_c:
         c.wait_recv()
 
@@ -731,144 +1034,27 @@
         dm[who, p] = (dm[who, p].astype(F32) + dgot[2, p].astype(F32)).astype(dm.dtype)
         return carry
 
-    lax.fori_loop(0, HALF, add_far, 0)
+    lax.fori_loop(0, HALF, add_far, 0, unroll=5)
     for c in near_c[2:4]:
         c.start()
-    lax.fori_loop(4, 9, grad_conv, 0)
-    g[BULK["volume"] : BULK["volume"] + 324, :] = flatten_32(
-        lambda j: vn[pl.ds(j, 324, stride=4), :], 324
+    for at_, v in products(256):
+        gw1_ref[0, at_, :] = v[:, 0:128] + v[:, 128:256]
+
+    def put_direct(i, v):
+        g[pl.ds(BULK["direct"] + i, 208, stride=3), :] = v
+
+    flatten_96(lambda j: gw1_ref[0, pl.ds(j, 208, stride=4), :], 208, put_direct)
+    g[BULK["pooled"] : BULK["pooled"] + 208, :] = flatten_32(
+        lambda j: gw1_ref[0, pl.ds(j, 208, stride=4), :], 208
     )
 
-    core_i = lax.rem(me_b, 2)
-    mate = digit_peer(me_b, 1, 2, 1)
-    along = ((2, 8), (8, 2))
-    digits = [[digit_of(me_b, along[i][s], 4) for i in range(2)] for s in range(2)]
-
-    class Chunk:
-        def __init__(self, index):
-            self.base, self.last = CHUNKS[index]
-            self.k = index
-            self.first = 4 * self.last
-            self.group = 4 * self.first
-            self.half = 2 * self.group
-            self.own = pl.multiple_of(self.base + core_i * self.half, self.last)
-            self.r1 = (r1a, r1b)[index]
-            self.r2 = (r2a, r2b)[index]
-            self.gc = (gca, gcb)[index]
-
-        def rows(self, at, count):
-            return pl.ds(pl.multiple_of(at, self.last), count)
-
-        def core_start(self):
-            theirs = self.rows(self.base + (1 - core_i) * self.half, self.half)
-            self.c0 = send_to(g.at[theirs], self.gc, co_s.at[self.k], co_r.at[self.k], mate)
-            self.c0.start()
-
-        def one_start(self):
-            self.c0.wait()
-            n = self.last
-
-            def add(i, carry):
-                at_ = self.rows(i * n, n)
-                self.gc[at_, :] = self.gc[at_, :] + g[self.rows(self.own + i * n, n), :]
-                return carry
-
-            lax.fori_loop(0, self.half // n, add, 0)
-            self.c1 = []
-            for i in range(2):
-                mine = digits[0][i]
-                for d in range(1, 4):
-                    to = lax.rem(mine + d, 4)
-                    c = send_to(
-                        self.gc.at[self.rows(i * self.group + to * self.first, self.first)],
-                        self.r1.at[i, mine], s1s.at[self.k, i, d], s1r.at[self.k, i, d],
-                        digit_peer(me_b, along[i][0], 4, d),
-                    )
-                    c.start()
-                    self.c1.append(c)
-                self.r1[i, mine] = self.gc[
-                    self.rows(i * self.group + mine * self.first, self.first), :
-                ]
-
-        def two_start(self):
-            for c in self.c1:
-                c.wait()
-            self.c2 = []
-            for i in range(2):
-                mine = digits[1][i]
-                self.r1[i, 0] = total_of(self.r1.at[i], 4)
-                for d in range(1, 4):
-                    to = lax.rem(mine + d, 4)
-                    c = send_to(
-                        self.r1.at[i, 0, self.rows(to * self.last, self.last)],
-                        self.r2.at[i, mine], s2s.at[self.k, i, d], s2r.at[self.k, i, d],
-                        digit_peer(me_b, along[i][1], 4, d),
-                    )
-                    c.start()
-                    self.c2.append(c)
-                self.r2[i, mine] = self.r1[i, 0, self.rows(mine * self.last, self.last), :]
-
-        def gather_start(self):
-            for c in self.c2:
-                c.wait()
-            self.c3 = []
-            for i in range(2):
-                at_ = self.rows(
-                    self.own + i * self.group + digits[0][i] * self.first
-                    + digits[1][i] * self.last,
-                    self.last,
-                )
-                gb_ref[at_, :] = total_of(self.r2.at[i], 4)
-                for d in range(1, 4):
-                    c = send_to(
-                        gb_ref.at[at_], gb_ref.at[at_], g1s.at[self.k, i, d],
-                        g1r.at[self.k, i, d], digit_peer(me_b, along[i][1], 4, d),
-                    )
-                    c.start()
-                    self.c3.append(c)
-
-        def spread_start(self):
-            for c in self.c3:
-                c.wait()
-            self.c4 = []
-            self.c5 = []
-            for i in range(2):
-                mine = digits[0][i]
-                at_ = self.rows(self.own + i * self.group + mine * self.first, self.first)
-                for d in range(1, 4):
-                    c = send_to(
-                        gb_ref.at[at_], gb_ref.at[at_], g2s.at[self.k, i, d],
-                        g2r.at[self.k, i, d], digit_peer(me_b, along[i][0], 4, d),
-                    )
-                    c.start()
-                    self.c4.append((c, i, d))
-                self.mate_start(i, 0)
-
-        def mate_start(self, i, d):
-            digit = lax.rem(digits[0][i] - d + 4, 4)
-            at_ = self.rows(self.own + i * self.group + digit * self.first, self.first)
-            c = send_to(
-                gb_ref.at[at_], gb_ref.at[at_], g3s.at[self.k, i, d], g3r.at[self.k, i, d], mate
-            )
-            c.start()
-            self.c5.append(c)
-
-        def mate_rest(self):
-            for c, i, d in self.c4:
-                c.wait_recv()
-                self.mate_start(i, d)
-
-        def finish(self):
-            for c, i, d in self.c4:
-                c.wait_send()
-            for c in self.c5:
-                c.wait()
-
-    first_chunk, second_chunk = Chunk(0), Chunk(1)
-    first_chunk.core_start()
+    c_.core_start()
+    a_.gather_start()
+    b_.two_start()
 
     for c in near_c:
         c.wait_recv()
+
 
     def back1(p, carry):
         g1, b1 = carry
@@ -886,109 +1072,62 @@
 
         return g1 + d * m, b1 + d
 
-    g1, b1 = lax.fori_loop(0, HALF, back1, (zero128, zero128))
+    g1, b1 = lax.fori_loop(0, HALF, back1, (zero128, zero128), unroll=5)
     sbuf_d[me_b] = pack_rows([col(g1), col(b1)], 2)
     share_start(sbuf_d, me_b, es, er)
+
+    def dy1_nat(p, carry):
+        d = ob[p]
+        top = d.astype(BF16).astype(F32)
+        dnat[0, pl.ds(p, ROWS, stride=POS), :] = top + pltpu.roll(d - top, 64, 1)
+        return carry
+
+    lax.fori_loop(0, POS, dy1_nat, 0, unroll=7)
+    for at_, v in products(128):
+        gw1_ref[1, at_, :] = v + pltpu.roll(v, 64, 1)
+    lsend[pl.ds(384, 128), :] = jnp.zeros((128, 128), F32)
+    put_late(lsend)
+
+    def late_copy(d):
+        to = lax.rem(me_b + d, NB)
+        return send_to(lsend.at[late_at(to)], lgot.at[me_b], fs, fr, batch_peer(me_b, d))
+
+    def late_start(d, carry):
+        late_copy(d).start()
+        return carry
+
+    lax.fori_loop(1, NB, late_start, 0)
+    lgot[me_b] = lsend[late_at(me_b), :]
     for c in far_c + near_c:
         c.wait_send()
-    first_chunk.one_start()
-
-    def dy0_at(p, carry):
-        v = finish(ypos[p][:, 0:128], n0, dpre[p][:, 0:128], totc[0:1], totc[1:2])
-        v = v.astype(BF16).astype(F32)
-        h, w = p // SIDE, lax.rem(p, SIDE)
-        n_h = 3 - (h == 0).astype(jnp.int32) - (h == SIDE - 1).astype(jnp.int32)
-        n_w = 3 - (w == 0).astype(jnp.int32) - (w == SIDE - 1).astype(jnp.int32)
-        share = v / jnp.maximum(n_t * (n_h * n_w).astype(F32), 1.0)
-        box[padded(p)] = share + prev_t(share) + next_t(share)
-        ypos[p, :, 0:128] = v
-        return carry
-
-    lax.fori_loop(0, POS, dy0_at, 0)
-
-    def dy0_nat(p, carry):
-        acc, _ = spread(p)
-        v = jnp.where(is_pool, acc * mask, ypos[p][:, 0:128])
-        lowv = v - v.astype(BF16).astype(F32)
-        dnat[0, pl.ds(p, ROWS, stride=POS), :] = v
-        dnat[1, pl.ds(p, ROWS, stride=POS), :] = lowv
-        return carry
-
-    lax.fori_loop(0, POS, dy0_nat, 0)
-
-    for tile in range(2):
-        gw1_ref[tile] = jnp.zeros((CIN, 128), F32)
-
-    def grad_one(r, width, fold):
-        first, off, lanes = window_of(r)
-        rhs = jnp.concatenate(
-            [dnat[t, pl.ds(r, GPAD, stride=8), :] for t in range(width // 128)], axis=1
-        ).astype(BF16)
-        for k in range(NC):
-            res = dot_t(xg[k, :, first : first + lanes], rhs, 0, 0)[off : off + CB]
-            if fold:
-                gw1_ref[0, k * CB : (k + 1) * CB, :] += res[:, 0:128] + res[:, 128:256]
-            else:
-                gw1_ref[1, k * CB : (k + 1) * CB, :] += res
-
-    for r in range(8):
-        grad_one(r, 256, True)
-
-    def put_direct(i, v):
-        g[pl.ds(BULK["direct"] + i, 208, stride=3), :] = v
-
-    flatten_96(lambda j: gw1_ref[0, pl.ds(j, 208, stride=4), :], 208, put_direct)
-    g[BULK["pooled"] : BULK["pooled"] + 208, :] = flatten_32(
-        lambda j: gw1_ref[0, pl.ds(j, 208, stride=4), :], 208
-    )
-
-    second_chunk.core_start()
+    c_.one_start()
+    a_.spread_start()
+    b_.gather_start()
     share_wait(sbuf_d, me_b, es, er)
     totd = total_of(sbuf_d, NB)
 
-    def dy1_nat(p, carry):
-        v = finish(ypos[p][:, 128:256], n1, ob[p], totd[0:1], totd[1:2])
-        dnat[0, pl.ds(p, ROWS, stride=POS), :] = v
-        return carry
-
-    lax.fori_loop(0, POS, dy1_nat, 0)
-    for r in range(8):
-        grad_one(r, 128, False)
-
-    lane104, lane26 = lanes_of((104, 128)), lanes_of((26, 128))
-    lsend[pl.ds(384, 128), :] = jnp.zeros((128, 128), F32)
-    parts = [(gw1_ref[1, pl.ds(j, 104, stride=8), :], 0, 48 * j, 48) for j in range(8)]
-    for i, v in enumerate(joined(parts, lane104, 3)):
-        lsend[pl.ds(LATE["squeeze"] + i, 104, stride=3), :] = v
-    parts = [(gw1_ref[1, pl.ds(j, 26, stride=32), :], 48, 12 * j, 12) for j in range(32)]
-    for i, v in enumerate(joined(parts, lane26, 3)):
-        lsend[pl.ds(LATE["shrink"] + i, 26, stride=3), :] = v
-
-    def late_at(i):
-        return pl.ds(pl.multiple_of(i * LATE_ROWS, LATE_ROWS), LATE_ROWS)
-
-    def late_copy(d):
-        to = lax.rem(me_b + d, NB)
-        return send_to(
-            lsend.at[late_at(to)], lgot.at[me_b], fs, fr, batch_peer(me_b, d)
-        )
-
-    def late_start(d, carry):
-        late_copy(d).start()
-        return carry
-
-    lax.fori_loop(1, NB, late_start, 0)
-    lgot[me_b] = lsend[late_at(me_b), :]
-
-    first_chunk.two_start()
-    second_chunk.one_start()
-    first_chunk.gather_start()
+    rowl = lax.broadcasted_iota(jnp.int32, (LATE_ROWS, 128), 0) + me_b * LATE_ROWS
+    third = lax.rem(rowl, 3)
+
+    def late_lanes(v):
+        lane1 = lanes_of((1, 128))
+        sq = joined([(v, 0, 48 * j, 48) for j in range(8)], lane1, 3)
+        sh = joined([(v, 48, 12 * j, 12) for j in range(32)], lane1, 3)
+        pick = [jnp.where(rowl < LATE["shrink"], a, b) for a, b in zip(sq, sh)]
+        return jnp.where(third == 0, pick[0], jnp.where(third == 1, pick[1], pick[2]))
+
+    scale_l = late_lanes(n1[3] * n1[2])
+    bias_l = late_lanes(totd[1:2] / voxels)
+    gain_l = late_lanes(totd[0:1] / voxels)
+    share_wait(pgot, me_b, ps, pr)
+    c_.two_start()
     share_wait(lgot, me_b, fs, fr)
-    late_ref[me_b] = total_of(lgot, NB)
+    both = total_of(pgot, NB)
+    late_ref[me_b] = scale_l * (total_of(lgot, NB) - bias_l * both[1] - gain_l * both[0])
     share_start(late_ref, me_b, hs, hr)
-    second_chunk.two_start()
-    first_chunk.spread_start()
-    second_chunk.gather_start()
+    b_.spread_start()
+    a_.mate_rest()
+    b_.mate_rest()
 
     fix = voxels / (voxels - 1.0)
     for tile, n, gg, gb in (
@@ -1001,15 +1140,14 @@
 
     for buf, send, recv in (
         (sbuf_a, as_, ar), (sbuf_b, bs, br), (sbuf_c, cs, cr), (sbuf_d, es, er), (lgot, fs, fr),
+        (pgot, ps, pr),
     ):
         share_sent(buf, me_b, send, recv)
-    second_chunk.spread_start()
-    first_chunk.mate_rest()
-    second_chunk.mate_rest()
+    c_.mate_rest()
     share_wait(late_ref, me_b, hs, hr)
     share_sent(late_ref, me_b, hs, hr)
-    first_chunk.finish()
-    second_chunk.finish()
+    for chunk in (a_, b_, c_):
+        chunk.finish()
 
 
 def core(x, lengths, labels, weights, affine):
@@ -1021,7 +1159,7 @@
     return pl.pallas_call(
         core_kernel,
         out_shape=(
-            jax.ShapeDtypeStruct((BULK_ROWS, 128), F32),
+            pltpu.VMEM((BULK_ROWS, 128), F32),
             jax.ShapeDtypeStruct((NB, LATE_ROWS, 128), F32),
             jax.ShapeDtypeStruct((8, 384), F32),
             jax.ShapeDtypeStruct((8, 128), F32),
@@ -1042,6 +1180,8 @@
             vmem((8, 384), F32),
             vmem((13 * GPAD, 128), F32),
             vmem((NC, GPAD, GW), BF16),
+            vmem((NC, GW, 256), BF16),
+            vmem((8, 256, 256), BF16),
             vmem((NC, W1_ROWS, 256), BF16),
             vmem((2, 8 * GPAD, 128), F32),
             vmem((POS, ROWS, 256), F32),
@@ -1062,20 +1202,25 @@
             vmem((4, 256, 128), F32),
             vmem((BULK_ROWS, 128), F32),
             *[vmem((32 * n, 128), F32) for _, n in CHUNKS],
+            vmem((16 * DIRECT_ROWS, 128), F32),
             *[vmem((2, 4, 4 * n, 128), F32) for _, n in CHUNKS],
             *[vmem((2, 4, n, 128), F32) for _, n in CHUNKS],
+            vmem((16, DIRECT_ROWS, 128), F32),
             vmem((NB * LATE_ROWS, 128), F32),
             vmem((NB, LATE_ROWS, 128), F32),
+            vmem((2, NB * LATE_ROWS, 128), F32),
+            vmem((NB, 2, LATE_ROWS, 128), F32),
             vmem((NC, ROWS, 512), F32),
             *[vmem((NB, n, 128), F32) for n in (8, 2, 8, 2)],
-            dma((4,)), dma((7,)), dma((6,)), dma((6,)),
+            dma((4,)), dma((7,)), dma((12,)), dma((12,)),
             dma((6,)), dma((6,)), dma((NC,)), dma((NC,)), dma((6,)), dma((6,)),
             *[dma] * 12,
-            dma((2,)), dma((2,)),
+            dma((3,)), dma((3,)),
             *[dma((2, 2, 4))] * 10,
+            *[dma] * 8,
         ],
         compiler_params=pltpu.CompilerParams(
-            collective_id=0, has_side_effects=True, vmem_limit_bytes=63 << 20
+            collective_id=0, has_side_effects=True, vmem_limit_bytes=47 << 20
         ),
         name="block",
     )(x, lengths, labels, *weights, affine)
@@ -1089,15 +1234,15 @@
 
 
 def adam_kernel(*refs):
-    gb_in, late, st, sc, running = refs[0:5]
+    gb, late, st, sc, running = refs[0:5]
     w_in, m_in, v_in = refs[5:13], refs[13:21], refs[21:29]
     m_out, v_out, w_out = refs[29:37], refs[37:45], refs[45:53]
     run_out, loss_out, count_out, copies_out = refs[53:57]
     wb, mb, vb = refs[57:64], refs[64:71], refs[71:78]
-    cb, gb, insem, gsem, outsem, csem = refs[78:84]
+    cb, insem, outsem, csem = refs[78:82]
     rates = step_rates()
     parts = []
-    for i in (4, 3, 5, 1, 0, 6):
+    for i in ADAM_ORDER:
         parts.append((i, 0, FLAT[NAMES[i]]))
     for first in range(0, FLAT["spatial"], ADAM_ROWS):
         parts.append((2, first, ADAM_ROWS))
@@ -1111,14 +1256,11 @@
     for n, (i, first, count) in enumerate(parts):
         mine = []
         for kind, (src, dst) in enumerate(((w_in[i], wb[i]), (m_in[i], mb[i]), (v_in[i], vb[i]))):
+            if NAMES[i] == "spatial" and kind < 2:
+                continue
             c = pltpu.make_async_copy(
                 at_rows(src, i, first, count), at_rows(dst, i, first, count), insem.at[n, kind]
             )
-            c.start()
-            mine.append(c)
-        if NAMES[i] in BULK:
-            at = pl.ds(BULK[NAMES[i]] + first, count)
-            c = pltpu.make_async_copy(gb_in.at[at], gb.at[at], gsem.at[n])
             c.start()
             mine.append(c)
         ins.append(mine)
@@ -1134,8 +1276,12 @@
         for c in ins[n]:
             c.wait()
 
-        def step(at, count, i=i, name=name):
-            if name in BULK:
+        def step(at, count, i=i, name=name, first=first):
+            if name == "spatial":
+                tap = at // 144
+                row = tap_rows(tap // 9, lax.rem(tap, 9)) + lax.rem(at, 144)
+                grad = gb[pl.ds(pl.multiple_of(row, 8), count), :]
+            elif name in BULK:
                 grad = gb[pl.ds(BULK[name] + at, count), :]
             else:
                 grad = late[pl.ds(LATE[name] + at, count), :]
@@ -1153,13 +1299,14 @@
                 else:
                     ref[pl.ds(at, count), :] = v
 
-            m, v, w = adamw(load(wb[i]), load(mb[i]), load(vb[i]), grad, rates[i])
+            old = (w_in, m_in, vb) if name == "spatial" else (wb, mb, vb)
+            m, v, w = adamw(*(load(group[i]) for group in old), grad, rates[i])
             store(mb[i], m)
             store(vb[i], v)
             store(wb[i], w)
-            cb[:, pl.ds(pl.multiple_of(starts[i] + at * 128, 128), count * 128)] = w.reshape(
-                1, count * 128
-            ).astype(BF16)
+            cb[:, pl.ds(pl.multiple_of(starts[i] + at * 128, 128), count * 128)] = w.astype(
+                BF16
+            ).reshape(1, count * 128)
 
         block = {"spatial": 72, "readout": 80, "direct": 48, "pooled": 104, "squeeze": 104}.get(
             name, 24
@@ -1170,7 +1317,7 @@
             step(pl.multiple_of(first + j * block, 8), block)
             return carry
 
-        lax.fori_loop(0, loops, body, 0)
+        lax.fori_loop(0, loops, body, 0, unroll=3)
         at, rest = first + loops * block, rows - loops * block
         if rest // 8:
             step(at, rest // 8 * 8)
@@ -1218,13 +1365,12 @@
     return pl.pallas_call(
         adam_kernel,
         out_shape=[*(flats + [small]) * 3, small, one, one, jax.ShapeDtypeStruct((1, total), BF16)],
-        in_specs=[hbm] + [vm] * 4 + specs * 3,
+        in_specs=[vm] * 5 + ([hbm] * 2 + [vm] + [hbm] * 4 + [vm]) * 2 + specs,
         out_specs=[*specs * 3, vm, vm, vm, hbm],
         scratch_shapes=[
-            *buffers * 3, pltpu.VMEM((1, total), BF16), pltpu.VMEM((BULK_ROWS, 128), F32),
-            dma((count, 3)), dma((count,)), dma((count, 3)), dma((count,)),
+            *buffers * 3, pltpu.VMEM((1, total), BF16), dma((count, 3)), dma((count, 3)), dma((count,)),
         ],
-        compiler_params=pltpu.CompilerParams(vmem_limit_bytes=63 << 20),
+        compiler_params=pltpu.CompilerParams(vmem_limit_bytes=20 << 20),
         name="adamw",
     )(gb, late, st, sc, running, *masters, *firsts, *seconds)
 
@@ -1251,7 +1397,17 @@
         [rows(a, n) for a, n in zip(group, NAMES)] + [group[7]]
         for group in (masters, firsts, seconds)
     )
-    gb, late, st, sc = core(features, lengths, labels.T, masters[:7], affine)
+    def put(arrays, space):
+        return [pltpu.with_memory_space_constraint(a, space) for a in arrays]
+
+    x, lens, labs, aff = put([features, lengths, labels.T, affine], pltpu.HBM)
+    gb, late, st, sc = core(x, lens, labs, put(masters[:7], pltpu.HBM), aff)
+    (gb,) = put([gb], pltpu.VMEM)
+    masters, firsts, seconds = (
+        put(group[:2], pltpu.HBM) + put(group[2:3], space) + put(group[3:7], pltpu.HBM)
+        + [group[7]]
+        for group, space in ((masters, pltpu.VMEM), (firsts, pltpu.VMEM), (seconds, pltpu.HBM))
+    )
     out = adam(gb, late.reshape(NB * LATE_ROWS, 128), st, sc, running, masters, firsts, seconds)
     flat_out = [a if i % 8 == 7 else a.reshape(1, -1) for i, a in enumerate(out[:24])]
     return (*flat_out, out[24], out[25].reshape(()), out[26].reshape(()), out[27])

time: 153 us -> 138 us (0.902)
  Pallas kernels: 151 us -> 135 us
    pallas_call x1, Pallas kernels: 139 us -> 128 us  [core(): pl.pallas_call(core_kernel, out_shape=(pltpu.VMEM((BULK_ROWS, 128), F32),...]
    pallas_call x1, Pallas kernels: 12.1 us -> 7.63 us  [adam(): pl.pallas_call(adam_kernel, out_shape=[*(flats + [small]) * 3, small, one...]
where the time goes in v4:
time: 138 us; the launch traced here: 136 us
  Pallas kernels  135 us (98%)
    pallas_call x1, Pallas kernels, core(): pl.pallas_call(core_kernel, out_shape=(pltpu.VMEM((BULK_ROWS, 128), F32),...  128 us
    pallas_call x1, Pallas kernels, adam(): pl.pallas_call(adam_kernel, out_shape=[*(flats + [small]) * 3, small, one...  7.63 us

profile of v4, /device:TPU:0, one launch (start us, length us, event | category | flops | bytes accessed | tf_op | source)
XLA Modules:
  0.0 136.2 jit_solution(8088439261650857424)
XLA Ops:
  0.7 0.0 copy-start
  0.7 0.0 copy-start.1
  0.7 0.0 copy-start.2
  0.7 0.0 copy-start.3
  0.7 0.0 copy-start.4
  0.7 0.0 copy-start.5
  0.7 127.6 %block.1 = (f32[6144,128]{1,0:T(8,128)S(1)}, f32[32,16,128]{2,1,0:T(8,128)S(1)}, f32[8,384]{1,0:T(8,128)S(1)}, f32[8,128]{1,0:T(8,128)S(1)}) custom-call(bf16[1,326144]{1,0:T(2,128)(2,1)} %x_hbm.1, s32[8]{0:T(128)} %len_ref.1, s32[4,8]{1,0:T(4,128)} %bitcast.55, f32[624,128]{1,0:T(8,128)} %bitcast.41, f32[312,128]{1,0:T(8,128)} %bitcast.43, ...), custom_call_target="tpu_custom_call" | custom-call | tf_op jit(solution)/shard_map/block/pallas_call | solution.py:1159
  128.3 0.0 copy-done
  128.3 0.0 copy-done.1
  128.4 0.0 copy-done.2
  128.4 0.0 copy-done.3
  128.4 0.0 copy-done.4
  128.4 0.0 copy-done.5
  128.4 7.6 %adamw.1 = (f32[624,128]{1,0:T(8,128)}, f32[312,128]{1,0:T(8,128)}, f32[3888,128]{1,0:T(8,128)}, f32[1,9984]{1,0:T(1,128)}, f32[1,41472]{1,0:T(1,128)}, /*index=...) custom-call(f32[6144,128]{1,0:T(8,128)S(1)} %get-tuple-element.60.re, ...), custom_call_target="tpu_custom_call" | custom-call | tf_op jit(solution)/shard_map/adamw/pallas_call | solution.py:1365
Async XLA Ops:
  0.7 127.7 %copy-start = (f32[1,497664]{1,0:T(1,128)S(1)}, f32[1,497664]{1,0:T(1,128)}, u32[]{:S(2)}) copy-start(f32[1,497664]{1,0:T(1,128)} %param.33) | copy-start | bytes 5971972
  0.7 127.7 %copy-start.1 = (f32[1,497664]{1,0:T(1,128)S(1)}, f32[1,497664]{1,0:T(1,128)}, u32[]{:S(2)}) copy-start(f32[1,497664]{1,0:T(1,128)} %param.41) | copy-start | bytes 5971972
  0.7 127.7 %copy-start.2 = (f32[2,316]{1,0:T(2,128)S(1)}, f32[2,316]{1,0:T(2,128)}, u32[]{:S(2)}) copy-start(f32[2,316]{1,0:T(2,128)} %refs_12_.1) | copy-start | bytes 7588
  0.7 127.7 %copy-start.3 = (f32[2,316]{1,0:T(2,128)S(1)}, f32[2,316]{1,0:T(2,128)}, u32[]{:S(2)}) copy-start(f32[2,316]{1,0:T(2,128)} %refs_4_.1) | copy-start | bytes 7588
  0.7 127.7 %copy-start.4 = (f32[2,316]{1,0:T(2,128)S(1)}, f32[2,316]{1,0:T(2,128)}, u32[]{:S(2)}) copy-start(f32[2,316]{1,0:T(2,128)} %refs_20_.1) | copy-start | bytes 7588
  0.7 127.7 %copy-start.5 = (f32[2,316]{1,0:T(2,128)S(1)}, f32[2,316]{1,0:T(2,128)}, u32[]{:S(2)}) copy-start(f32[2,316]{1,0:T(2,128)} %refs_28_.1) | copy-start | bytes 7588

commit v5 on v4

--- a/solution.py
+++ b/solution.py
@@ -284,7 +284,7 @@
     lbuf, sbuf_a, sbuf_b, sbuf_c, sbuf_d,
     xin, win, xs, xr, ms, mr, ls, lr, ds_, dr,
     as_, ar, bs, br, cs, cr, es, er, fs, fr, hs, hr,
-    co_s, co_r, s1s, s1r, s2s, s2r, g1s, g1r, g2s, g2r, g3s, g3r, ps, pr, d1s, d1r, d2s, d2r, d3s, d3r,
+    co_s, co_r, s1s, s1r, s2s, s2r, g1sa, g1sb, g1ra, g1rb, g3s, g3r, ps, pr, d1s, d1r, d2s, d2r, d3s, d3r,
 ):
     me_b = lax.axis_index("batch")
     me = lax.axis_index("chan")
@@ -749,6 +749,7 @@
             self.r1 = (r1a, r1b)[index]
             self.r2 = (r2a, r2b)[index]
             self.gc = (gca, gcb)[index]
+            self.s1 = ((g1sa, g1ra), (g1sb, g1rb))[index]
 
         def rows(self, at, count):
             return pl.ds(pl.multiple_of(at, self.last), count)
@@ -805,58 +806,37 @@
         def gather_start(self):
             for c in self.c2:
                 c.wait()
-            self.c3 = []
             for i in range(2):
-                at_ = self.rows(
-                    self.own + i * self.group + digits[0][i] * self.first
-                    + digits[1][i] * self.last,
-                    self.last,
-                )
-                gb_ref[at_, :] = total_of(self.r2.at[i], 4)
-                for d in range(1, 4):
-                    c = send_to(
-                        gb_ref.at[at_], gb_ref.at[at_], g1s.at[self.k, i, d],
-                        g1r.at[self.k, i, d], digit_peer(me_b, along[i][1], 4, d),
-                    )
-                    c.start()
-                    self.c3.append(c)
-
-        def spread_start(self):
-            for c in self.c3:
-                c.wait()
-            self.c4 = []
-            self.c5 = []
-            for i in range(2):
-                mine = digits[0][i]
-                at_ = self.rows(self.own + i * self.group + mine * self.first, self.first)
-                for d in range(1, 4):
-                    c = send_to(
-                        gb_ref.at[at_], gb_ref.at[at_], g2s.at[self.k, i, d],
-                        g2r.at[self.k, i, d], digit_peer(me_b, along[i][0], 4, d),
-                    )
-                    c.start()
-                    self.c4.append((c, i, d))
-                self.mate_start(i, 0)
-
-        def mate_start(self, i, d):
-            digit = lax.rem(digits[0][i] - d + 4, 4)
-            at_ = self.rows(self.own + i * self.group + digit * self.first, self.first)
-            c = send_to(
-                gb_ref.at[at_], gb_ref.at[at_], g3s.at[self.k, i, d], g3r.at[self.k, i, d], mate
+                mine = self.piece_at(i)
+                gb_ref[mine, :] = total_of(self.r2.at[i], 4)
+
+                def one(d, carry, mine=mine):
+                    send_to(gb_ref.at[mine], gb_ref.at[mine], *self.s1, chip_peer(d)).start()
+                    return carry
+
+                lax.fori_loop(1, 16, one, 0)
+
+        def piece_at(self, i):
+            return self.rows(
+                self.own + i * self.group + digits[0][i] * self.first + digits[1][i] * self.last,
+                self.last,
             )
-            c.start()
-            self.c5.append(c)
+
+        def all_others(self):
+            some = gb_ref.at[pl.ds(self.base, 30 * self.last)]
+            return send_to(some, some, *self.s1, mate)
 
         def mate_rest(self):
-            for c, i, d in self.c4:
-                c.wait_recv()
-                self.mate_start(i, d)
+            self.all_others().wait_recv()
+            rows_ = self.rows(self.own, self.half)
+            self.c5 = send_to(
+                gb_ref.at[rows_], gb_ref.at[rows_], g3s.at[self.k], g3r.at[self.k], mate
+            )
+            self.c5.start()
 
         def finish(self):
-            for c, i, d in self.c4:
-                c.wait_send()
-            for c in self.c5:
-                c.wait()
+            self.all_others().wait_send()
+            self.c5.wait()
 
     chip = me_b // 2
 
@@ -1075,6 +1055,7 @@
     g1, b1 = lax.fori_loop(0, HALF, back1, (zero128, zero128), unroll=5)
     sbuf_d[me_b] = pack_rows([col(g1), col(b1)], 2)
     share_start(sbuf_d, me_b, es, er)
+    c_.one_start()
 
     def dy1_nat(p, carry):
         d = ob[p]
@@ -1100,8 +1081,6 @@
     lgot[me_b] = lsend[late_at(me_b), :]
     for c in far_c + near_c:
         c.wait_send()
-    c_.one_start()
-    a_.spread_start()
     b_.gather_start()
     share_wait(sbuf_d, me_b, es, er)
     totd = total_of(sbuf_d, NB)
@@ -1125,7 +1104,6 @@
     both = total_of(pgot, NB)
     late_ref[me_b] = scale_l * (total_of(lgot, NB) - bias_l * both[1] - gain_l * both[0])
     share_start(late_ref, me_b, hs, hr)
-    b_.spread_start()
     a_.mate_rest()
     b_.mate_rest()
 
@@ -1216,7 +1194,9 @@
             dma((6,)), dma((6,)), dma((NC,)), dma((NC,)), dma((6,)), dma((6,)),
             *[dma] * 12,
             dma((3,)), dma((3,)),
-            *[dma((2, 2, 4))] * 10,
+            *[dma((2, 2, 4))] * 4,
+            *[dma] * 4,
+            dma((2,)), dma((2,)),
             *[dma] * 8,
         ],
         compiler_params=pltpu.CompilerParams(

time: 138 us -> 135 us (0.978)
  Pallas kernels: 135 us -> 133 us
    pallas_call x1, Pallas kernels: 128 us -> 125 us  [core(): pl.pallas_call(core_kernel, out_shape=(pltpu.VMEM((BULK_ROWS, 128), F32),...]
where the time goes in v5:
time: 135 us; the launch traced here: 134 us
  Pallas kernels  133 us (99%)
    pallas_call x1, Pallas kernels, core(): pl.pallas_call(core_kernel, out_shape=(pltpu.VMEM((BULK_ROWS, 128), F32),...  125 us
    pallas_call x1, Pallas kernels, adam(): pl.pallas_call(adam_kernel, out_shape=[*(flats + [small]) * 3, small, one...  7.63 us

profile of v5, /device:TPU:0, one launch (start us, length us, event | category | flops | bytes accessed | tf_op | source)
XLA Modules:
  0.0 133.6 jit_solution(2610070494931213847)
XLA Ops:
  0.7 0.0 copy-start
  0.7 0.0 copy-start.1
  0.7 0.0 copy-start.2
  0.7 0.0 copy-start.3
  0.7 0.0 copy-start.4
  0.7 0.0 copy-start.5
  0.7 125.1 %block.1 = (f32[6144,128]{1,0:T(8,128)S(1)}, f32[32,16,128]{2,1,0:T(8,128)S(1)}, f32[8,384]{1,0:T(8,128)S(1)}, f32[8,128]{1,0:T(8,128)S(1)}) custom-call(bf16[1,326144]{1,0:T(2,128)(2,1)} %x_hbm.1, s32[8]{0:T(128)} %len_ref.1, s32[4,8]{1,0:T(4,128)} %bitcast.55, f32[624,128]{1,0:T(8,128)} %bitcast.41, f32[312,128]{1,0:T(8,128)} %bitcast.43, ...), custom_call_target="tpu_custom_call" | custom-call | tf_op jit(solution)/shard_map/block/pallas_call | solution.py:1137
  125.8 0.0 copy-done
  125.8 0.0 copy-done.1
  125.8 0.0 copy-done.2
  125.8 0.0 copy-done.3
  125.8 0.0 copy-done.4
  125.8 0.0 copy-done.5
  125.9 7.6 %adamw.1 = (f32[624,128]{1,0:T(8,128)}, f32[312,128]{1,0:T(8,128)}, f32[3888,128]{1,0:T(8,128)}, f32[1,9984]{1,0:T(1,128)}, f32[1,41472]{1,0:T(1,128)}, /*index=...) custom-call(f32[6144,128]{1,0:T(8,128)S(1)} %get-tuple-element.60.re, ...), custom_call_target="tpu_custom_call" | custom-call | tf_op jit(solution)/shard_map/adamw/pallas_call | solution.py:1345
Async XLA Ops:
  0.7 125.1 %copy-start = (f32[1,497664]{1,0:T(1,128)S(1)}, f32[1,497664]{1,0:T(1,128)}, u32[]{:S(2)}) copy-start(f32[1,497664]{1,0:T(1,128)} %param.33) | copy-start | bytes 5971972
  0.7 125.1 %copy-start.1 = (f32[1,497664]{1,0:T(1,128)S(1)}, f32[1,497664]{1,0:T(1,128)}, u32[]{:S(2)}) copy-start(f32[1,497664]{1,0:T(1,128)} %param.41) | copy-start | bytes 5971972
  0.7 125.1 %copy-start.2 = (f32[2,316]{1,0:T(2,128)S(1)}, f32[2,316]{1,0:T(2,128)}, u32[]{:S(2)}) copy-start(f32[2,316]{1,0:T(2,128)} %refs_12_.1) | copy-start | bytes 7588
  0.7 125.1 %copy-start.3 = (f32[2,316]{1,0:T(2,128)S(1)}, f32[2,316]{1,0:T(2,128)}, u32[]{:S(2)}) copy-start(f32[2,316]{1,0:T(2,128)} %refs_4_.1) | copy-start | bytes 7588
  0.7 125.1 %copy-start.4 = (f32[2,316]{1,0:T(2,128)S(1)}, f32[2,316]{1,0:T(2,128)}, u32[]{:S(2)}) copy-start(f32[2,316]{1,0:T(2,128)} %refs_20_.1) | copy-start | bytes 7588
  0.7 125.1 %copy-start.5 = (f32[2,316]{1,0:T(2,128)S(1)}, f32[2,316]{1,0:T(2,128)}, u32[]{:S(2)}) copy-start(f32[2,316]{1,0:T(2,128)} %refs_28_.1) | copy-start | bytes 7588

commit v6 on v5

--- a/solution.py
+++ b/solution.py
@@ -643,7 +643,7 @@
             s2 = s2 + m * y
         return s1, s2
 
-    s1, s2 = lax.fori_loop(0, SIDE, conv, (zero128, zero128))
+    s1, s2 = lax.fori_loop(0, SIDE, conv, (zero128, zero128), unroll=7)
     sbuf_b[me_b] = pack_rows([col(s1), col(s2)], 2)
     share_start(sbuf_b, me_b, bs, br)
     at[...] = jnp.transpose(acol[...].reshape(VOX, 256))
@@ -922,9 +922,9 @@
             flatten_96(lambda j: gq[pl.ds(j, 48, stride=4), :], 48, put)
         return carry
 
-    lax.fori_loop(0, EARLY_TAPS, grad_conv, 0)
+    lax.fori_loop(0, EARLY_TAPS, grad_conv, 0, unroll=2)
     a_.core_start()
-    lax.fori_loop(EARLY_TAPS, 9, grad_conv, 0)
+    lax.fori_loop(EARLY_TAPS, 9, grad_conv, 0, unroll=5)
     g[BULK["volume"] : BULK["volume"] + 324, :] = flatten_32(
         lambda j: vn[pl.ds(j, 324, stride=4), :], 324
     )

time: 135 us -> 132 us (0.978)
  Pallas kernels: 133 us -> 130 us
    pallas_call x1, Pallas kernels: 125 us -> 122 us  [core(): pl.pallas_call(core_kernel, out_shape=(pltpu.VMEM((BULK_ROWS, 128), F32),...]
where the time goes in v6:
time: 132 us; the launch traced here: 131 us
  Pallas kernels  130 us (98%)
    pallas_call x1, Pallas kernels, core(): pl.pallas_call(core_kernel, out_shape=(pltpu.VMEM((BULK_ROWS, 128), F32),...  122 us
    pallas_call x1, Pallas kernels, adam(): pl.pallas_call(adam_kernel, out_shape=[*(flats + [small]) * 3, small, one...  7.63 us

profile of v6, /device:TPU:0, one launch (start us, length us, event | category | flops | bytes accessed | tf_op | source)
XLA Modules:
  0.0 131.0 jit_solution(9062234480602804407)
XLA Ops:
  0.7 0.0 copy-start
  0.7 0.0 copy-start.1
  0.7 0.0 copy-start.2
  0.7 0.0 copy-start.3
  0.7 0.0 copy-start.4
  0.7 0.0 copy-start.5
  0.7 122.4 %block.1 = (f32[6144,128]{1,0:T(8,128)S(1)}, f32[32,16,128]{2,1,0:T(8,128)S(1)}, f32[8,384]{1,0:T(8,128)S(1)}, f32[8,128]{1,0:T(8,128)S(1)}) custom-call(bf16[1,326144]{1,0:T(2,128)(2,1)} %x_hbm.1, s32[8]{0:T(128)} %len_ref.1, s32[4,8]{1,0:T(4,128)} %bitcast.55, f32[624,128]{1,0:T(8,128)} %bitcast.41, f32[312,128]{1,0:T(8,128)} %bitcast.43, ...), custom_call_target="tpu_custom_call" | custom-call | tf_op jit(solution)/shard_map/block/pallas_call | solution.py:1137
  123.1 0.0 copy-done
  123.1 0.0 copy-done.1
  123.2 0.0 copy-done.2
  123.2 0.0 copy-done.3
  123.2 0.0 copy-done.4
  123.2 0.0 copy-done.5
  123.2 7.6 %adamw.1 = (f32[624,128]{1,0:T(8,128)}, f32[312,128]{1,0:T(8,128)}, f32[3888,128]{1,0:T(8,128)}, f32[1,9984]{1,0:T(1,128)}, f32[1,41472]{1,0:T(1,128)}, /*index=...) custom-call(f32[6144,128]{1,0:T(8,128)S(1)} %get-tuple-element.60.re, ...), custom_call_target="tpu_custom_call" | custom-call | tf_op jit(solution)/shard_map/adamw/pallas_call | solution.py:1345
Async XLA Ops:
  0.7 122.5 %copy-start = (f32[1,497664]{1,0:T(1,128)S(1)}, f32[1,497664]{1,0:T(1,128)}, u32[]{:S(2)}) copy-start(f32[1,497664]{1,0:T(1,128)} %param.33) | copy-start | bytes 5971972
  0.7 122.5 %copy-start.1 = (f32[1,497664]{1,0:T(1,128)S(1)}, f32[1,497664]{1,0:T(1,128)}, u32[]{:S(2)}) copy-start(f32[1,497664]{1,0:T(1,128)} %param.41) | copy-start | bytes 5971972
  0.7 122.5 %copy-start.2 = (f32[2,316]{1,0:T(2,128)S(1)}, f32[2,316]{1,0:T(2,128)}, u32[]{:S(2)}) copy-start(f32[2,316]{1,0:T(2,128)} %refs_12_.1) | copy-start | bytes 7588
  0.7 122.5 %copy-start.3 = (f32[2,316]{1,0:T(2,128)S(1)}, f32[2,316]{1,0:T(2,128)}, u32[]{:S(2)}) copy-start(f32[2,316]{1,0:T(2,128)} %refs_4_.1) | copy-start | bytes 7588
  0.7 122.5 %copy-start.4 = (f32[2,316]{1,0:T(2,128)S(1)}, f32[2,316]{1,0:T(2,128)}, u32[]{:S(2)}) copy-start(f32[2,316]{1,0:T(2,128)} %refs_20_.1) | copy-start | bytes 7588
  0.7 122.5 %copy-start.5 = (f32[2,316]{1,0:T(2,128)S(1)}, f32[2,316]{1,0:T(2,128)}, u32[]{:S(2)}) copy-start(f32[2,316]{1,0:T(2,128)} %refs_28_.1) | copy-start | bytes 7588
